TPU v7x, 256 devices: a whole 4x4x8 slice. The times are simulated.
256 devices in a mesh: rep: 16 (over x_lo, z), row: 8 (over y, core), col: 2 (over x_hi).
Axes of the slice: x: 4 (x_hi: 2, x_lo: 2; x = x_hi * 2 + x_lo), y: 4, z: 8, core: 2. Of those that a mesh axis runs over, the one named last changes fastest.
Arguments:
- design_rows: bfloat16 [16384, 49152], P('rep', ('row', 'col')), may hold values from -0.046875 to 0.046875
- design_panel: bfloat16 [16384, 2, 512], P('rep', 'col', 'row'), may hold values from -6 to 6
- observations: float32 [16384], P('rep'), may hold values from -6 to 6
- group_ids: int32 [16384], P('rep'), may hold values from 0 to 7
- group_sigma: float32 [8], replicated, may hold values from 0.5 to 2
Outputs:
- normal_panel: float32 [8, 2, 3072, 1024], P('row', None, 'rep', 'col')
- normal_rhs: float32 [8, 2, 3072], P('row', None, 'rep')
All inputs are finite; a program needn't handle non-finite values.
Results may differ from a plain program's by a relative error of at most 0.0029.
Values may be sent and summed in bfloat16 or wider, within the bound.
No kernel may reach another device: no remote copies, remote signals or barrier semaphores. Data moves between devices by JAX's collectives and lax.ppermute only.
A program may use at most 128 MiB of HBM per device.

v0:
```python
import jax
import jax.numpy as jnp
from jax import lax
from jax.sharding import PartitionSpec as P


def contract(left, right):
    return lax.dot_general(
        left, right, (((0,), (0,)), ((), ())), preferred_element_type=jnp.float32
    )


def per_device(design_rows, design_panel, observations, group_ids, group_sigma):
    levels = jnp.arange(group_sigma.shape[0], dtype=jnp.int32)
    inverse_var = 1.0 / (group_sigma * group_sigma)
    onehot = (group_ids[:, None] == levels[None, :]).astype(jnp.float32)
    weights = jnp.sum(onehot * inverse_var[None, :], axis=1)
    local_panel = (weights[:, None, None] * design_panel.astype(jnp.float32)).astype(jnp.bfloat16)
    weighted_obs = (weights * observations).astype(jnp.bfloat16)
    col_panel = lax.all_gather(local_panel, "row", axis=2, tiled=True)
    col_count = lax.axis_size("col")
    row_tile = lax.all_gather(design_rows, "col", axis=1, tiled=True)
    weighted = col_panel.reshape(col_panel.shape[0], col_panel.shape[2])
    partial_value = contract(row_tile, weighted)
    rhs_part = contract(row_tile, weighted_obs)
    shard_rows = design_rows.shape[1]
    summed, rhs_sum = (
        lax.psum_scatter(
            partial_value.reshape(col_count, shard_rows, weighted.shape[1]),
            "rep",
            scatter_dimension=1,
            tiled=True,
        ),
        lax.psum_scatter(
            rhs_part.reshape(col_count, shard_rows), "rep", scatter_dimension=1, tiled=True
        ),
    )
    return (summed[None], rhs_sum[None])


def solution(mesh):
    in_specs = (P("rep", ("row", "col")), P("rep", "col", "row"), P("rep"), P("rep"), P())
    out_specs = (P("row", None, "rep", "col"), P("row", None, "rep"))
    return jax.shard_map(
        per_device, mesh=mesh, in_specs=in_specs, out_specs=out_specs, check_vma=False
    )
```

profile of v0, /device:TPU:16, one launch (start us, length us, event | category | flops | bytes accessed | tf_op | source)
XLA Modules:
  0.0 424.0 jit_solution(11811272827904853425)
XLA Ops:
  7.2 0.0 all-gather.5.cloned.1.call-start
  7.2 0.7 all-gather.5.cloned.1.call-update
  7.9 0.0 all-gather.3.cloned.1.call-start
  7.9 0.7 multiply_divide_fusion
  8.6 0.8 select_reduce_fusion
  9.4 1.6 multiply_convert_fusion
  11.0 0.0 all-gather.3.cloned.1.call-update
  11.0 0.0 reduce-scatter.7.cloned.1.call-start
  11.0 0.7 multiply_convert_fusion.1
  11.7 160.0 %all-gather.5.cloned.1.call-done = bf16[1024,6144]{1,0:T(8,128)(2,1)} async-done(((bf16[1024,3072]{1,0:T(8,128)(2,1)}), bf16[1024,6144]{1,0:T(8,128)(2,1)}) %all-gather.5.cloned.1.call-update) | async-done | bytes 12582928 | tf_op jit(solution)/shard_map/all_gather | solution.py:22
  171.7 6.3 %fusion.1 = f32[1,6144]{1,0:T(1,128)S(1)} fusion(bf16[1024,1]{0,1:T(2,128)(2,1)S(1)} %reshape.21, bf16[1024,6144]{1,0:T(8,128)(2,1)} %all-gather.5.cloned.1.call-done), kind=kOutput, calls=%fused_computation.7 | convolution fusion | flops 12582912 | bytes 12609536 | tf_op jit(solution)/shard_map/dot_general | solution.py:8
  178.0 1.7 copy.11
  179.8 0.0 reduce-scatter.7.cloned.1.call-update
  179.8 0.0 reduce-scatter.5.cloned.1.call-start
  179.9 18.3 %all-gather.3.cloned.1.call-done = bf16[1024,1,512]{0,2,1:T(8,128)(2,1)} async-done(((bf16[1024,1,64]{0,2,1:T(8,128)(2,1)}), bf16[1024,1,512]{0,2,1:T(8,128)(2,1)}) %all-gather.3.cloned.1.call-update) | async-done | bytes 1048592 | tf_op jit(solution)/shard_map/all_gather | solution.py:20
  198.2 12.5 %convolution_bitcast_fusion = f32[6144,512]{0,1:T(8,128)} fusion(bf16[1024,6144]{1,0:T(8,128)(2,1)} %all-gather.5.cloned.1.call-done, bf16[1024,1,512]{0,2,1:T(8,128)(2,1)} %all-gather.3.cloned.1.call-done), kind=kOutput, calls=%fused_computation | convolution fusion | flops 6442450944 | bytes 26214400 | tf_op jit(solution)/shard_map/dot_general | solution.py:8
  210.7 12.6 %copy.10 = f32[6144,512]{1,0:T(8,128)} copy(f32[6144,512]{0,1:T(8,128)} %convolution_bitcast_fusion) | data formatting | bytes 25165824 | tf_op jit(solution)/shard_map/reshape | solution.py:29
  223.3 0.0 reduce-scatter.5.cloned.1.call-update
  223.4 51.5 %reduce-scatter.7.cloned.1.call-done = f32[192,2]{1,0:T(8,128)} async-done(((f32[3072,2]{1,0:T(8,128)}), f32[192,2]{1,0:T(8,128)}) %reduce-scatter.7.cloned.1.call-update) | async-done | bytes 1552
  274.9 1.5 copy.12
  276.4 141.1 %reduce-scatter.5.cloned.1.call-done = f32[2,192,512]{2,1,0:T(8,128)} async-done(((f32[2,3072,512]{2,1,0:T(8,128)}), f32[2,192,512]{2,1,0:T(8,128)}) %reduce-scatter.5.cloned.1.call-update) | async-done | bytes 786448 | tf_op jit(solution)/shard_map/reduce_scatter | solution.py:28
  (2 shorter events, 0.0 us)
Async XLA Ops:
  7.2 164.6 %all-gather.5.cloned.1.call-start = ((), (), s32[]{:S(2)}) async-start(), calls=%async_computation.3 | async-start | bytes 18874368 | tf_op jit(solution)/shard_map/all_gather | solution.py:22
  7.9 190.3 %all-gather.3.cloned.1.call-start = ((), (), s32[]{:S(2)}) async-start(), calls=%async_computation.2 | async-start | bytes 1179648 | tf_op jit(solution)/shard_map/all_gather | solution.py:20
  11.0 263.9 %reduce-scatter.7.cloned.1.call-start = ((), (), s32[]{:S(2)}) async-start(), calls=%async_computation.5 | async-start | bytes 1671168
  179.8 237.7 %reduce-scatter.5.cloned.1.call-start = ((), (), s32[]{:S(2)}) async-start(), calls=%async_computation.4 | async-start | bytes 13369344 | tf_op jit(solution)/shard_map/reduce_scatter | solution.py:28
Sparse Core Ops, SparseCore 0:
  9.8 161.8 all-gather.4
  174.1 23.9 all-gather.2
  200.7 74.1 reduce-scatter.6
  278.0 139.4 reduce-scatter.4
where the time goes:
time: 425 us; the launch traced here: 424 us
  waiting for transfers between devices  372 us (88%)
  matrix products  18.9 us (4%)
  local copies, waits for them, and re-layouts  15.9 us (4%)
  between operations  13.8 us (3%)
    all_gather x1, waiting for transfers between devices, per_device(): row_tile = lax.all_gather(design_rows, 'col', axis=1, tiled=True)  160 us
    reduce_scatter x1, waiting for transfers between devices, per_device(): lax.psum_scatter(partial_value.reshape(col_count, shard_rows, weighted.sh...  141 us
    unnamed x5, waiting for transfers between devices  52.3 us
    dot_general x2, matrix products, contract(): lax.dot_general(left, right, (((0,), (0,)), ((), ())), preferred_element_...  18.9 us
    all_gather x1, waiting for transfers between devices, per_device(): col_panel = lax.all_gather(local_panel, 'row', axis=2, tiled=True)  18.3 us
    reshape x1, local copies, waits for them, and re-layouts, per_device(): partial_value.reshape(col_count, shard_rows, weighted.shape[1])  12.6 us
  transfers between devices with their start and end apart: 4, of which 4 were waited for; matrix products, arithmetic and copies ran while one was open for 9% of the time, Pallas kernels for 0%

commit v1 on v0

v1 whole, which is shorter than its diff:
```python
import functools

import jax
import jax.numpy as jnp
from jax import lax
from jax.experimental import pallas as pl
from jax.experimental.pallas import tpu as pltpu
from jax.sharding import PartitionSpec as P

NZ = 8
ROWS = 192
PAIR = 2 * ROWS
HALF = 512
PART = 256
TAIL = 16
BF16, F32 = jnp.bfloat16, jnp.float32
IN_VMEM = pl.BlockSpec(memory_space=pltpu.VMEM)
IN_SMEM = pl.BlockSpec(memory_space=pltpu.SMEM)


def call(kernel, out_shape, n_in, scratch=(), flops=0, moved=0, limit=16, first=IN_SMEM):
    several = isinstance(out_shape, (list, tuple))
    return pl.pallas_call(
        kernel,
        out_shape=out_shape,
        in_specs=[first] + [IN_VMEM] * (n_in - 1),
        out_specs=[IN_VMEM] * len(out_shape) if several else IN_VMEM,
        scratch_shapes=list(scratch),
        compiler_params=pltpu.CompilerParams(vmem_limit_bytes=limit * 2**20),
        cost_estimate=pl.CostEstimate(
            flops=flops, bytes_accessed=moved, transcendentals=0
        ),
    )


def weigh_kernel(sigma_ref, panel_ref, obs_ref, ids_ref, panel_out, obs_out):
    ids = ids_ref[...]
    sigma = jnp.full(ids.shape, sigma_ref[0], F32)
    for g in range(1, sigma_ref.shape[0]):
        sigma = jnp.where(ids == g, sigma_ref[g], sigma)
    weights = 1.0 / (sigma * sigma)
    panel_out[...] = (weights * panel_ref[...].astype(F32)).astype(BF16)
    weighted = (weights * obs_ref[...]).astype(BF16)
    obs_out[...] = jnp.broadcast_to(weighted, obs_out.shape)


def weigh(panel_t, observations, group_ids, group_sigma):
    cols, points = panel_t.shape
    flat = pl.BlockSpec((1, points), lambda i: (0, 0))
    return pl.pallas_call(
        weigh_kernel,
        grid=(1,),
        out_shape=(
            jax.ShapeDtypeStruct((cols, points), BF16),
            jax.ShapeDtypeStruct((TAIL, points), BF16),
        ),
        in_specs=[IN_SMEM, pl.BlockSpec((cols, points), lambda i: (0, 0)), flat, flat],
        out_specs=[
            pl.BlockSpec((cols, points), lambda i: (0, 0)),
            pl.BlockSpec((TAIL, points), lambda i: (0, 0)),
        ],
    )(group_sigma, panel_t, observations.reshape(1, -1), group_ids.reshape(1, -1))


def pair_kernel(rows_ref, out_ref, held, sems):
    copies = []
    for e in range(NZ // 2):
        for a in range(2):
            n = a * (NZ // 2) + e
            copies.append(
                pltpu.make_async_copy(
                    rows_ref.at[:, n * PAIR : (n + 1) * PAIR], held.at[n], sems.at[n]
                )
            )
            copies[-1].start()
    for e in range(NZ // 2):
        copies[2 * e].wait()
        copies[2 * e + 1].wait()
        for half in range(2):
            lanes = slice(half * ROWS, (half + 1) * ROWS)
            out_ref[2 * e + half] = jnp.concatenate(
                [held[e, :, lanes], held[NZ // 2 + e, :, lanes]], axis=1
            )


def pair_up(design_rows):
    points = design_rows.shape[0]
    return call(
        pair_kernel,
        jax.ShapeDtypeStruct((NZ, points, PAIR), BF16),
        1,
        scratch=[pltpu.VMEM((NZ, points, PAIR), BF16), pltpu.SemaphoreType.DMA((NZ,))],
        moved=4 * design_rows.size,
        limit=12,
        first=pl.BlockSpec(memory_space=pl.ANY),
    )(design_rows)


def product(left, right):
    return jnp.dot(left, right, preferred_element_type=F32)


def plus(total, received):
    main = total[:-TAIL] + received[:-TAIL, :].astype(F32)
    tail = received[-TAIL:, :].astype(F32)
    more = tail[: TAIL // 2] + tail[TAIL // 2 :]
    return jnp.concatenate([main, total[-TAIL:] + jnp.concatenate([more, more], axis=0)], axis=0)


def packed(total):
    high = total[-TAIL : -TAIL // 2].astype(BF16).astype(F32)
    low = total[-TAIL // 2 :] - high
    main = [total[:-TAIL]] if total.shape[0] > TAIL else []
    return jnp.concatenate(main + [high, low], axis=0).astype(BF16)


def place(meta_ref, dz):
    return (meta_ref[0] + dz) & (NZ - 1)


def x_rows(panel_ref, which):
    at = pl.multiple_of(which * PART, PART)
    return jnp.concatenate([panel_ref[pl.ds(at, PART), :], panel_ref[HALF:, :]], axis=0)


def z_kernel(steps, meta_ref, rows_ref, panel_ref, *refs):
    received, outs = refs[: -len(steps)], refs[-len(steps) :]
    left = panel_ref[...]
    for i, dz in enumerate(steps):
        total = product(left, rows_ref[place(meta_ref, dz)])
        if i < len(received):
            total = plus(total, received[i])
        outs[i][...] = packed(total)


def z_step(meta, rows, panel, steps, received):
    shape = (panel.shape[0], PAIR)
    n = len(steps)
    return call(
        functools.partial(z_kernel, steps),
        [jax.ShapeDtypeStruct(shape, BF16)] * n,
        3 + len(received),
        flops=2 * n * shape[0] * PAIR * rows.shape[1],
        moved=2 * n * (rows.shape[1] * PAIR + 2 * shape[0] * PAIR),
    )(meta, rows, panel, *received)


def over_kernel(steps, meta_ref, rows_ref, panel_ref, out_ref):
    left = x_rows(panel_ref, 1 - meta_ref[1])
    for i, dz in enumerate(steps):
        out_ref[i] = packed(product(left, rows_ref[place(meta_ref, dz)]))


def over_x(meta, rows, panel, steps):
    shape = (len(steps), PART + TAIL, PAIR)
    return call(
        functools.partial(over_kernel, steps),
        jax.ShapeDtypeStruct(shape, BF16),
        3,
        flops=2 * len(steps) * shape[1] * PAIR * rows.shape[1],
        moved=2 * len(steps) * (rows.shape[1] * PAIR + shape[1] * PAIR),
    )(meta, rows, panel)


def x_kernel(steps, picks, n_over, meta_ref, rows_ref, panel_ref, *refs):
    over, refs = refs[:n_over], refs[n_over:]
    received, outs = refs[: -len(steps)], refs[-len(steps) :]
    left = x_rows(panel_ref, meta_ref[1])
    for i, dz in enumerate(steps):
        total = product(left, rows_ref[place(meta_ref, dz)])
        which, at = picks[i]
        total = plus(total, over[which].at[at])
        if i < len(received):
            total = plus(total, received[i])
        outs[i][...] = packed(total)


def x_step(meta, rows, panel, steps, over, received):
    arrays, picks = [], []
    for dz in steps:
        array, at = over[dz]
        known = [a is array for a in arrays]
        if not any(known):
            known.append(True)
            arrays.append(array)
        picks.append((known.index(True), at))
    shape = (PART + TAIL, PAIR)
    n = len(steps)
    return call(
        functools.partial(x_kernel, steps, tuple(picks), len(arrays)),
        [jax.ShapeDtypeStruct(shape, BF16)] * n,
        3 + len(arrays) + len(received),
        flops=2 * n * shape[0] * PAIR * rows.shape[1],
        moved=2 * n * (rows.shape[1] * PAIR + 3 * shape[0] * PAIR),
    )(meta, rows, panel, *arrays, *received)


def widened(tail, width):
    zeros = jnp.zeros((tail.shape[0], width - tail.shape[1]), tail.dtype)
    return jnp.concatenate([tail, zeros], axis=1)


def z_last_kernel(meta_ref, rows_ref, panel_ref, down, up, own_ref, rhs_ref, sent_ref, turned):
    side = meta_ref[1]
    total = product(panel_ref[...], rows_ref[meta_ref[0]])
    total = plus(plus(total, down), up)
    turned[...] = total[:HALF].T
    own_ref[...] = turned[pl.ds(pl.multiple_of(side * ROWS, ROWS), ROWS), :]
    sent_ref[:ROWS, :] = turned[
        pl.ds(pl.multiple_of((1 - side) * ROWS, ROWS), ROWS), :
    ].astype(BF16)
    tail = total[HALF:]
    lower, upper = tail[:, :ROWS], tail[:, ROWS:]
    rhs_ref[...] = jnp.where(side == 0, lower, upper)[: TAIL // 2]
    other = packed(jnp.where(side == 0, upper, lower))
    sent_ref[ROWS:, :] = widened(other.astype(F32), HALF).astype(BF16)


def z_last(meta, rows, panel, down, up):
    return call(
        z_last_kernel,
        [
            jax.ShapeDtypeStruct((ROWS, HALF), F32),
            jax.ShapeDtypeStruct((TAIL // 2, ROWS), F32),
            jax.ShapeDtypeStruct((ROWS + TAIL, HALF), BF16),
        ],
        5,
        scratch=[pltpu.VMEM((PAIR, HALF), F32)],
        flops=2 * panel.shape[0] * PAIR * rows.shape[1],
        moved=4 * rows.shape[1] * PAIR,
    )(meta, rows, panel, down, up)


def x_last_kernel(at, meta_ref, rows_ref, panel_ref, over, up, down, near_ref, cross_ref, turned):
    side = meta_ref[1]
    total = product(x_rows(panel_ref, side), rows_ref[meta_ref[0]])
    total = plus(plus(plus(total, over.at[at]), up), down)
    turned[...] = total[:PART].T
    near_ref[...] = turned[pl.ds(pl.multiple_of(side * ROWS, ROWS), ROWS), :]
    cross_ref[:ROWS, :] = turned[pl.ds(pl.multiple_of((1 - side) * ROWS, ROWS), ROWS), :]
    tail = total[PART:]
    other = jnp.where(side == 0, tail[:, ROWS:], tail[:, :ROWS])[: TAIL // 2]
    cross_ref[ROWS:, :] = widened(other, PART)


def x_last(meta, rows, panel, over, up, down):
    array, at = over
    return call(
        functools.partial(x_last_kernel, at),
        [
            jax.ShapeDtypeStruct((ROWS, PART), F32),
            jax.ShapeDtypeStruct((ROWS + TAIL // 2, PART), F32),
        ],
        6,
        scratch=[pltpu.VMEM((PAIR, PART), F32)],
        flops=2 * (PART + TAIL) * PAIR * rows.shape[1],
        moved=4 * rows.shape[1] * PAIR,
    )(meta, rows, panel, array, up, down)


def finish_kernel(meta_ref, own_ref, rhs_ref, part_ref, near_ref, cross_ref, out_ref, rhs_out):
    side, y, core, half = meta_ref[1], meta_ref[2], meta_ref[3], meta_ref[4]
    own = own_ref[...] + part_ref[:ROWS, :].astype(F32)
    near, cross = near_ref[...], cross_ref[:ROWS, :]
    first = jnp.where(side == 0, near, cross)
    second = jnp.where(side == 0, cross, near)
    for where_to, left, right in (
        (half, own[:, :PART], own[:, PART:]),
        (1 - half, first, second),
    ):
        mine = jnp.where(core == 0, left, right)
        other = jnp.where(core == 0, right, left)
        for dy in range(4):
            lanes = slice(dy * 64, dy * 64 + 64)
            at = pl.multiple_of(((y + dy) & 3) * 128, 128)
            out_ref[0, where_to, :, pl.ds(at, 128)] = jnp.concatenate(
                [mine[:, lanes], other[:, lanes]], axis=1
            )
    tail = part_ref[ROWS:, :].astype(F32)[:, :ROWS]
    mine = (rhs_ref[...] + (tail[: TAIL // 2] + tail[TAIL // 2 :]))[:1]
    other = cross_ref[ROWS:, :][:1, :ROWS]
    rhs_out[0] = jnp.concatenate(
        [jnp.where(half == 0, mine, other), jnp.where(half == 0, other, mine)], axis=0
    )


def finish(meta, own, rhs, part, near, cross):
    return call(
        finish_kernel,
        [
            jax.ShapeDtypeStruct((1, 2, ROWS, HALF), F32),
            jax.ShapeDtypeStruct((1, 2, ROWS), F32),
        ],
        6,
        moved=6 * 2**20,
    )(meta, own, rhs, part, near, cross)


def z_shift(x, d):
    return lax.ppermute(
        x, "rep", [(a * NZ + z, a * NZ + (z + d) % NZ) for a in range(2) for z in range(NZ)]
    )


def x_swap(x):
    return lax.ppermute(
        x, "rep", [(a * NZ + z, (1 - a) * NZ + z) for a in range(2) for z in range(NZ)]
    )


def y_shift(x, d):
    return lax.ppermute(
        x, "row", [(y * 2 + c, (y + d) % 4 * 2 + c) for y in range(4) for c in range(2)]
    )


def core_swap(x):
    return lax.ppermute(x, "row", [(i, i ^ 1) for i in range(8)])


def half_swap(x):
    return lax.ppermute(x, "col", [(0, 1), (1, 0)])


def cross_swap(x):
    pairs = []
    for a in range(2):
        for z in range(NZ):
            for h in range(2):
                pairs.append(((a * NZ + z) * 2 + h, ((1 - a) * NZ + z) * 2 + 1 - h))
    return lax.ppermute(x, ("rep", "col"), pairs)


def per_device(design_rows, design_panel, observations, group_ids, group_sigma):
    rep, row, half = (lax.axis_index(n) for n in ("rep", "row", "col"))
    meta = jnp.stack([rep & (NZ - 1), rep >> 3, row >> 1, row & 1, half]).astype(jnp.int32)
    points = design_rows.shape[0]
    panel_t = jnp.transpose(design_panel.reshape(points, -1))
    mine, weighted_obs = weigh(panel_t, observations, group_ids, group_sigma)
    rows = pair_up(design_rows)

    def along_y(block):
        near = jnp.concatenate([block] + [y_shift(block, -d) for d in (1, 2, 3)], axis=0)
        return jnp.concatenate([near, core_swap(near), weighted_obs], axis=0)

    foreign = half_swap(mine)
    panel_z = along_y(mine)
    panel_x = along_y(foreign)

    over = {}
    for piece in ((4,), (3, -3), (2, -2), (1, -1, 0)):
        got = x_swap(over_x(meta, rows, panel_x, piece))
        for i, dz in enumerate(piece):
            over[dz] = (got, i)

    z_got, x_got = (), ()
    for s in (4, 3, 2, 1):
        steps = (-s,) if s == 4 else (-s, s)
        sent = z_step(meta, rows, panel_z, steps, z_got)
        z_got = (z_shift(sent[0], -1),) + tuple(z_shift(v, 1) for v in sent[1:])
        steps = (s,) if s == 4 else (s, -s)
        sent = x_step(meta, rows, panel_x, steps, over, x_got)
        x_got = (z_shift(sent[0], 1),) + tuple(z_shift(v, -1) for v in sent[1:])

    own, rhs, sent = z_last(meta, rows, panel_z, *z_got)
    part = x_swap(sent)
    near, cross = x_last(meta, rows, panel_x, over[0], *x_got)
    near, cross = half_swap(near), cross_swap(cross)
    return finish(meta, own, rhs, part, near, cross)


def solution(mesh):
    in_specs = (P("rep", ("row", "col")), P("rep", "col", "row"), P("rep"), P("rep"), P())
    out_specs = (P("row", None, "rep", "col"), P("row", None, "rep"))
    return jax.shard_map(
        per_device, mesh=mesh, in_specs=in_specs, out_specs=out_specs, check_vma=False
    )
```

time: 425 us -> 124 us (0.29)
  waiting for transfers between devices: 372 us -> 42.5 us
  starting transfers between devices: 0.16 us -> 44.9 us
  Pallas kernels: 0 us -> 25.3 us
  matrix products: 18.9 us -> 0 us
  between operations: 13.8 us -> 0.97 us
  local copies, waits for them, and re-layouts: 15.9 us -> 9.42 us
    all_gather x2 -> x0, waiting for transfers between devices: 178 us -> none  [the longest x1 160 us: per_device(): row_tile = lax.all_gather(design_rows, 'col', axis=1, tiled=True)]
    reduce_scatter x1 -> x0, waiting for transfers between devices: 141 us -> none  [per_device(): lax.psum_scatter(partial_value.reshape(col_count, shard_rows, weighted.sh...]
    unnamed x5 -> x0, waiting for transfers between devices: 52.3 us -> none
    ppermute x0 -> x30, starting transfers between devices: none -> 44.9 us  [the longest x14 26.3 us: z_shift(): lax.ppermute(x, 'rep', [(a * NZ + z, a * NZ + (z + d) % NZ) for a in rang...]
    ppermute x0 -> x30, waiting for transfers between devices: none -> 42.5 us  [the longest x14 18.2 us: z_shift(): lax.ppermute(x, 'rep', [(a * NZ + z, a * NZ + (z + d) % NZ) for a in rang...]
    pallas_call x0 -> x17, Pallas kernels: none -> 25.3 us  [the longest x4 6.8 us: z_step(): call(functools.partial(z_kernel, steps), [jax.ShapeDtypeStruct(shape, BF1...]
    dot_general x2 -> x0, matrix products: 18.9 us -> none  [contract(): lax.dot_general(left, right, (((0,), (0,)), ((), ())), preferred_element_...]
    reshape x2 -> x0, local copies, waits for them, and re-layouts: 12.6 us -> none  [the longest x1 12.6 us: per_device(): partial_value.reshape(col_count, shard_rows, weighted.shape[1])]
  transfers between devices with their start and end apart: 4 -> 30, of which waited for: 4 -> 15; matrix products, arithmetic and copies ran while one was open for 9% -> 1% of each run, Pallas kernels for 0% -> 15%
where the time goes in v1:
time: 124 us; the launch traced here: 123 us
  starting transfers between devices  44.9 us (36%)
  waiting for transfers between devices  42.5 us (34%)
  Pallas kernels  25.3 us (20%)
  local copies, waits for them, and re-layouts  9.42 us (8%)
    ppermute x14, starting transfers between devices, z_shift(): lax.ppermute(x, 'rep', [(a * NZ + z, a * NZ + (z + d) % NZ) for a in rang...  26.3 us
    ppermute x14, waiting for transfers between devices, z_shift(): lax.ppermute(x, 'rep', [(a * NZ + z, a * NZ + (z + d) % NZ) for a in rang...  18.2 us
    unnamed x20, local copies, waits for them, and re-layouts  9.33 us
    ppermute x6, starting transfers between devices, y_shift(): lax.ppermute(x, 'row', [(y * 2 + c, (y + d) % 4 * 2 + c) for y in range(4...  9.1 us
    ppermute x5, waiting for transfers between devices, x_swap(): lax.ppermute(x, 'rep', [(a * NZ + z, (1 - a) * NZ + z) for a in range(2)...  8.93 us
    ppermute x6, waiting for transfers between devices, y_shift(): lax.ppermute(x, 'row', [(y * 2 + c, (y + d) % 4 * 2 + c) for y in range(4...  7.63 us
    pallas_call x4, Pallas kernels, z_step(): call(functools.partial(z_kernel, steps), [jax.ShapeDtypeStruct(shape, BF1...  6.8 us
    ppermute x2, waiting for transfers between devices, half_swap(): return lax.ppermute(x, 'col', [(0, 1), (1, 0)])  5.26 us
  transfers between devices with their start and end apart: 30, of which 15 were waited for; matrix products, arithmetic and copies ran while one was open for 1% of the time, Pallas kernels for 15%

profile of v1, /device:TPU:16, one launch (start us, length us, event | category | flops | bytes accessed | tf_op | source)
XLA Modules:
  0.0 123.1 jit_solution(8817692186072823855)
XLA Ops:
  0.6 1.6 %shard_map.69 = (bf16[64,1024]{1,0:T(8,128)(2,1)}, bf16[16,1024]{1,0:T(8,128)(2,1)}) custom-call(f32[8]{0:T(128)} %sigma_ref.1, bf16[64,1024]{1,0:T(8,128)(2,1)} %bitcast.10, f32[1,1024]{1,0:T(1,128)} %bitcast.11, s32[1,1024]{1,0:T(1,128)} %bitcast.12), custom_call_target="tpu_custom_call" | custom-call | tf_op jit(solution)/shard_map/pallas_call | solution.py:50
  2.7 2.9 %collective-permute-start.1 = (bf16[64,1024]{1,0:T(8,128)(2,1)}, bf16[64,1024]{1,0:T(8,128)(2,1)S(1)}, u32[]{:S(2)}, u32[]{:S(2)}) collective-permute-start(bf16[64,1024]{1,0:T(8,128)(2,1)} %get-tuple-element.21), channel_id=1, source_target_pairs={{0,8},{2,10},{4,12},{6,14},{8,0},{10,2},{12,4},{14,6},{1,9},{3,11}... | collective-permute-start | bytes 393224 | tf_op jit(solution)/shard_map/ppermute | solution.py:312
  5.6 1.4 %collective-permute-start.2 = (bf16[64,1024]{1,0:T(8,128)(2,1)}, bf16[64,1024]{1,0:T(8,128)(2,1)S(1)}, u32[]{:S(2)}, u32[]{:S(2)}) collective-permute-start(bf16[64,1024]{1,0:T(8,128)(2,1)} %get-tuple-element.21), channel_id=1, source_target_pairs={{0,4},{2,6},{4,8},{6,10},{8,12},{10,14},{12,0},{14,2},{1,5},{3,7},... | collective-permute-start | bytes 393224 | tf_op jit(solution)/shard_map/ppermute | solution.py:312
  7.0 1.7 %collective-permute-start.12 = (bf16[64,1024]{1,0:T(8,128)(2,1)}, bf16[64,1024]{1,0:T(8,128)(2,1)S(1)}, u32[]{:S(2)}, u32[]{:S(2)}) collective-permute-start(bf16[64,1024]{1,0:T(8,128)(2,1)} %get-tuple-element.21), channel_id=1, source_target_pairs={{0,1},{1,0},{2,3},{3,2},{4,5},{5,4},{6,7},{7,6},{8,9},{9,8},{10,11... | collective-permute-start | bytes 393224 | tf_op jit(solution)/shard_map/ppermute | solution.py:322
  8.6 0.9 constant_dynamic-update-slice_fusion.5
  9.6 2.8 %copy-done.2 = bf16[1024,3072]{1,0:T(8,128)(2,1)S(1)} copy-done((bf16[1024,3072]{1,0:T(8,128)(2,1)S(1)}, bf16[1024,3072]{1,0:T(8,128)(2,1)}, u32[]{:S(2)}) %copy-start.2) | copy-done | bytes 6291480
  12.4 2.3 %shard_map.68.rows_ref = bf16[8,1024,384]{2,1,0:T(8,128)(2,1)S(1)} custom-call(bf16[1024,3072]{1,0:T(8,128)(2,1)S(1)} %copy-done.2), custom_call_target="tpu_custom_call" | custom-call | bytes 12582912 | tf_op jit(solution)/shard_map/pallas_call | solution.py:88
  14.7 2.7 %copy-done = bf16[8,1024,384]{2,1,0:T(8,128)(2,1)} copy-done((bf16[8,1024,384]{2,1,0:T(8,128)(2,1)}, bf16[8,1024,384]{2,1,0:T(8,128)(2,1)S(1)}, u32[]{:S(2)}) %copy-start) | copy-done | bytes 6291480
  17.7 2.1 %collective-permute-start.13 = (bf16[64,1024]{1,0:T(8,128)(2,1)S(1)}, bf16[64,1024]{1,0:T(8,128)(2,1)S(1)}, u32[]{:S(2)}, u32[]{:S(2)}) collective-permute-start(bf16[64,1024]{1,0:T(8,128)(2,1)S(1)} %collective-permute-done.12), channel_id=1, source_target_pairs={{0,12},{2,14},{4,0},{6,2},{8,4},{10,6},{12,8},{14,10},{1,13},{3,15... | collective-permute-start | bytes 393224 | tf_op jit(solution)/shard_map/ppermute | solution.py:312
  19.8 1.9 %collective-permute-start.14 = (bf16[64,1024]{1,0:T(8,128)(2,1)S(1)}, bf16[64,1024]{1,0:T(8,128)(2,1)S(1)}, u32[]{:S(2)}, u32[]{:S(2)}) collective-permute-start(bf16[64,1024]{1,0:T(8,128)(2,1)S(1)} %collective-permute-done.12), channel_id=1, source_target_pairs={{0,8},{2,10},{4,12},{6,14},{8,0},{10,2},{12,4},{14,6},{1,9},{3,11}... | collective-permute-start | bytes 393224 | tf_op jit(solution)/shard_map/ppermute | solution.py:312
  22.1 3.9 %collective-permute-done.13 = bf16[64,1024]{1,0:T(8,128)(2,1)S(1)} collective-permute-done((bf16[64,1024]{1,0:T(8,128)(2,1)S(1)}, bf16[64,1024]{1,0:T(8,128)(2,1)S(1)}, u32[]{:S(2)}, u32[]{:S(2)}) %collective-permute-start.13) | collective-permute-done | bytes 131104 | tf_op jit(solution)/shard_map/ppermute | solution.py:312
  25.9 1.8 %collective-permute-done.14 = bf16[64,1024]{1,0:T(8,128)(2,1)S(1)} collective-permute-done((bf16[64,1024]{1,0:T(8,128)(2,1)S(1)}, bf16[64,1024]{1,0:T(8,128)(2,1)S(1)}, u32[]{:S(2)}, u32[]{:S(2)}) %collective-permute-start.14) | collective-permute-done | bytes 131104 | tf_op jit(solution)/shard_map/ppermute | solution.py:312
  27.7 2.0 %collective-permute-done.15 = bf16[64,1024]{1,0:T(8,128)(2,1)S(1)} collective-permute-done((bf16[64,1024]{1,0:T(8,128)(2,1)S(1)}, bf16[64,1024]{1,0:T(8,128)(2,1)S(1)}, u32[]{:S(2)}, u32[]{:S(2)}) %collective-permute-start.15) | collective-permute-done | bytes 131104 | tf_op jit(solution)/shard_map/ppermute | solution.py:312
  30.0 1.8 %collective-permute-done.16 = bf16[256,1024]{1,0:T(8,128)(2,1)S(1)} collective-permute-done((bf16[256,1024]{1,0:T(8,128)(2,1)S(1)}, bf16[256,1024]{1,0:T(8,128)(2,1)S(1)}, u32[]{:S(2)}, u32[]{:S(2)}) %collective-permute-start.16) | collective-permute-done | bytes 524320 | tf_op jit(solution)/shard_map/ppermute | solution.py:318
  31.8 2.8 %copy-done.1 = bf16[8,1024,384]{2,1,0:T(8,128)(2,1)S(1)} copy-done((bf16[8,1024,384]{2,1,0:T(8,128)(2,1)S(1)}, bf16[8,1024,384]{2,1,0:T(8,128)(2,1)}, u32[]{:S(2)}) %copy-start.1) | copy-done | bytes 6291480
  34.6 1.3 %shard_map.70 = bf16[528,384]{1,0:T(8,128)(2,1)S(1)} custom-call(s32[5]{0:T(128)S(1)} %stack.23.meta_ref, bf16[8,1024,384]{2,1,0:T(8,128)(2,1)S(1)} %copy-done.1, bf16[528,1024]{1,0:T(8,128)(2,1)S(1)} %get-tuple-element.41.panel_ref), custom_call_target="tpu_custom_call" | custom-call | flops 415236096 | bytes 1597440 | tf_op jit(solution)/shard_map/pallas_call | solution.py:139
  35.9 5.9 %collective-permute-start.4 = (bf16[528,384]{1,0:T(8,128)(2,1)S(1)}, bf16[528,384]{1,0:T(8,128)(2,1)S(1)}, u32[]{:S(2)}, u32[]{:S(2)}) collective-permute-start(bf16[528,384]{1,0:T(8,128)(2,1)S(1)} %shard_map.70), channel_id=1, source_target_pairs={{0,112},{16,0},{32,16},{48,32},{64,48},{80,64},{96,80},{112,96},{1... | collective-permute-start | bytes 1216520 | tf_op jit(solution)/shard_map/ppermute | solution.py:300
  41.8 8.9 %collective-permute-done.4.refs_0_ = bf16[528,384]{1,0:T(8,128)(2,1)S(1)} collective-permute-done((bf16[528,384]{1,0:T(8,128)(2,1)S(1)}, bf16[528,384]{1,0:T(8,128)(2,1)S(1)}, u32[]{:S(2)}, u32[]{:S(2)}) %collective-permute-start.4) | collective-permute-done | bytes 405536 | tf_op jit(solution)/shard_map/ppermute | solution.py:300
  50.8 1.8 %shard_map.71 = (bf16[528,384]{1,0:T(8,128)(2,1)S(1)}, bf16[528,384]{1,0:T(8,128)(2,1)S(1)}) custom-call(s32[5]{0:T(128)S(1)} %stack.23.meta_ref, bf16[8,1024,384]{2,1,0:T(8,128)(2,1)S(1)} %copy-done.1, bf16[528,1024]{1,0:T(8,128)(2,1)S(1)} %get-tuple-element.41.panel_ref, bf16[528,384]{1,0:T(8,128)(2,1)S(1)} %collective-permute-done.4.refs_0_), custom_call_target="tpu_custom_call" | custom-call | flops 830472192 | bytes 3194880 | tf_op jit(solution)/shard_map/pallas_call | solution.py:139
  52.6 3.8 %collective-permute-start.5 = (bf16[528,384]{1,0:T(8,128)(2,1)S(1)}, bf16[528,384]{1,0:T(8,128)(2,1)S(1)}, u32[]{:S(2)}, u32[]{:S(2)}) collective-permute-start(bf16[528,384]{1,0:T(8,128)(2,1)S(1)} %get-tuple-element.23), channel_id=1, source_target_pairs={{0,112},{16,0},{32,16},{48,32},{64,48},{80,64},{96,80},{112,96},{1... | collective-permute-start | bytes 1216520 | tf_op jit(solution)/shard_map/ppermute | solution.py:300
  56.4 1.0 shard_map.78
  58.1 1.3 %shard_map.77 = bf16[2,272,384]{2,1,0:T(8,128)(2,1)S(1)} custom-call(s32[5]{0:T(128)S(1)} %stack.23.meta_ref, bf16[8,1024,384]{2,1,0:T(8,128)(2,1)S(1)} %copy-done.1, bf16[528,1024]{1,0:T(8,128)(2,1)S(1)} %get-tuple-element.40.panel_ref), custom_call_target="tpu_custom_call" | custom-call | flops 427819008 | bytes 1990656 | tf_op jit(solution)/shard_map/pallas_call | solution.py:156
  59.4 1.5 %collective-permute-start.19 = (bf16[2,272,384]{2,1,0:T(8,128)(2,1)S(1)}, bf16[2,272,384]{2,1,0:T(8,128)(2,1)S(1)}, u32[]{:S(2)}, u32[]{:S(2)}) collective-permute-start(bf16[2,272,384]{2,1,0:T(8,128)(2,1)S(1)} %shard_map.77), channel_id=1, source_target_pairs={{0,128},{16,144},{32,160},{48,176},{64,192},{80,208},{96,224},{112... | collective-permute-start | bytes 1253384 | tf_op jit(solution)/shard_map/ppermute | solution.py:306
  60.9 1.3 %shard_map.76 = bf16[2,272,384]{2,1,0:T(8,128)(2,1)S(1)} custom-call(s32[5]{0:T(128)S(1)} %stack.23.meta_ref, bf16[8,1024,384]{2,1,0:T(8,128)(2,1)S(1)} %copy-done.1, bf16[528,1024]{1,0:T(8,128)(2,1)S(1)} %get-tuple-element.40.panel_ref), custom_call_target="tpu_custom_call" | custom-call | flops 427819008 | bytes 1990656 | tf_op jit(solution)/shard_map/pallas_call | solution.py:156
  62.9 2.7 %collective-permute-done.20.refs_0_ = bf16[1,272,384]{2,1,0:T(8,128)(2,1)S(1)} collective-permute-done((bf16[1,272,384]{2,1,0:T(8,128)(2,1)S(1)}, bf16[1,272,384]{2,1,0:T(8,128)(2,1)S(1)}, u32[]{:S(2)}, u32[]{:S(2)}) %collective-permute-start.20) | collective-permute-done | bytes 208928 | tf_op jit(solution)/shard_map/ppermute | solution.py:306
  65.6 1.0 shard_map.79
  66.7 2.4 %collective-permute-done.6.refs_1_ = bf16[528,384]{1,0:T(8,128)(2,1)S(1)} collective-permute-done((bf16[528,384]{1,0:T(8,128)(2,1)S(1)}, bf16[528,384]{1,0:T(8,128)(2,1)S(1)}, u32[]{:S(2)}, u32[]{:S(2)}) %collective-permute-start.6) | collective-permute-done | bytes 405536 | tf_op jit(solution)/shard_map/ppermute | solution.py:300
  69.1 1.8 %shard_map.72 = (bf16[528,384]{1,0:T(8,128)(2,1)S(1)}, bf16[528,384]{1,0:T(8,128)(2,1)S(1)}) custom-call(s32[5]{0:T(128)S(1)} %stack.23.meta_ref, bf16[8,1024,384]{2,1,0:T(8,128)(2,1)S(1)} %copy-done.1, bf16[528,1024]{1,0:T(8,128)(2,1)S(1)} %get-tuple-element.41.panel_ref, bf16[528,384]{1,0:T(8,128)(2,1)S(1)} %collective-permute-done.5.refs_0_, ...), custom_call_target="tpu_custom_call" | custom-call | flops 830472192 | bytes 3194880 | tf_op jit(solution)/shard_map/pallas_call | solution.py:139
  71.9 1.2 collective-permute-start.8
  73.1 1.6 %shard_map.75 = bf16[3,272,384]{2,1,0:T(8,128)(2,1)S(1)} custom-call(s32[5]{0:T(128)S(1)} %stack.23.meta_ref, bf16[8,1024,384]{2,1,0:T(8,128)(2,1)S(1)} %copy-done.1, bf16[528,1024]{1,0:T(8,128)(2,1)S(1)} %get-tuple-element.40.panel_ref), custom_call_target="tpu_custom_call" | custom-call | flops 641728512 | bytes 2985984 | tf_op jit(solution)/shard_map/pallas_call | solution.py:156
  75.8 1.3 %shard_map.80 = (bf16[272,384]{1,0:T(8,128)(2,1)S(1)}, bf16[272,384]{1,0:T(8,128)(2,1)S(1)}) custom-call(s32[5]{0:T(128)S(1)} %stack.23.meta_ref, bf16[8,1024,384]{2,1,0:T(8,128)(2,1)S(1)} %copy-done.1, bf16[528,1024]{1,0:T(8,128)(2,1)S(1)} %get-tuple-element.40.panel_ref, bf16[2,272,384]{2,1,0:T(8,128)(2,1)S(1)} %collective-permute-done.19.refs_0_, ...), custom_call_target="tpu_custom_call" | custom-call | flops 427819008 | bytes 2826240 | tf_op jit(solution)/shard_map/pallas_call | solution.py:189
  77.3 6.2 %collective-permute-done.18.refs_0_ = bf16[2,272,384]{2,1,0:T(8,128)(2,1)S(1)} collective-permute-done((bf16[2,272,384]{2,1,0:T(8,128)(2,1)S(1)}, bf16[2,272,384]{2,1,0:T(8,128)(2,1)S(1)}, u32[]{:S(2)}, u32[]{:S(2)}) %collective-permute-start.18) | collective-permute-done | bytes 417824 | tf_op jit(solution)/shard_map/ppermute | solution.py:306
  83.5 3.2 %collective-permute-start.23 = (bf16[272,384]{1,0:T(8,128)(2,1)S(1)}, bf16[272,384]{1,0:T(8,128)(2,1)S(1)}, u32[]{:S(2)}, u32[]{:S(2)}) collective-permute-start(bf16[272,384]{1,0:T(8,128)(2,1)S(1)} %get-tuple-element.33), channel_id=1, source_target_pairs={{0,112},{16,0},{32,16},{48,32},{64,48},{80,64},{96,80},{112,96},{1... | collective-permute-start | bytes 626696 | tf_op jit(solution)/shard_map/ppermute | solution.py:300
  86.9 3.2 %collective-permute-done.23.refs_2_ = bf16[272,384]{1,0:T(8,128)(2,1)S(1)} collective-permute-done((bf16[272,384]{1,0:T(8,128)(2,1)S(1)}, bf16[272,384]{1,0:T(8,128)(2,1)S(1)}, u32[]{:S(2)}, u32[]{:S(2)}) %collective-permute-start.23) | collective-permute-done | bytes 208928 | tf_op jit(solution)/shard_map/ppermute | solution.py:300
  90.0 1.3 %shard_map.81 = (bf16[272,384]{1,0:T(8,128)(2,1)S(1)}, bf16[272,384]{1,0:T(8,128)(2,1)S(1)}) custom-call(s32[5]{0:T(128)S(1)} %stack.23.meta_ref, bf16[8,1024,384]{2,1,0:T(8,128)(2,1)S(1)} %copy-done.1, bf16[528,1024]{1,0:T(8,128)(2,1)S(1)} %get-tuple-element.40.panel_ref, bf16[2,272,384]{2,1,0:T(8,128)(2,1)S(1)} %collective-permute-done.18.refs_0_, ...), custom_call_target="tpu_custom_call" | custom-call | flops 427819008 | bytes 2826240 | tf_op jit(solution)/shard_map/pallas_call | solution.py:189
  91.5 4.0 %collective-permute-start.25 = (bf16[272,384]{1,0:T(8,128)(2,1)S(1)}, bf16[272,384]{1,0:T(8,128)(2,1)S(1)}, u32[]{:S(2)}, u32[]{:S(2)}) collective-permute-start(bf16[272,384]{1,0:T(8,128)(2,1)S(1)} %get-tuple-element.35), channel_id=1, source_target_pairs={{0,112},{16,0},{32,16},{48,32},{64,48},{80,64},{96,80},{112,96},{1... | collective-permute-start | bytes 626696 | tf_op jit(solution)/shard_map/ppermute | solution.py:300
  95.5 1.8 %shard_map.73 = (bf16[528,384]{1,0:T(8,128)(2,1)S(1)}, bf16[528,384]{1,0:T(8,128)(2,1)S(1)}) custom-call(s32[5]{0:T(128)S(1)} %stack.23.meta_ref, bf16[8,1024,384]{2,1,0:T(8,128)(2,1)S(1)} %copy-done.1, bf16[528,1024]{1,0:T(8,128)(2,1)S(1)} %get-tuple-element.41.panel_ref, bf16[528,384]{1,0:T(8,128)(2,1)S(1)} %collective-permute-done.7.refs_0_, ...), custom_call_target="tpu_custom_call" | custom-call | flops 830472192 | bytes 3194880 | tf_op jit(solution)/shard_map/pallas_call | solution.py:139
  97.4 3.2 %collective-permute-start.9 = (bf16[528,384]{1,0:T(8,128)(2,1)S(1)}, bf16[528,384]{1,0:T(8,128)(2,1)S(1)}, u32[]{:S(2)}, u32[]{:S(2)}) collective-permute-start(bf16[528,384]{1,0:T(8,128)(2,1)S(1)} %get-tuple-element.27), channel_id=1, source_target_pairs={{0,112},{16,0},{32,16},{48,32},{64,48},{80,64},{96,80},{112,96},{1... | collective-permute-start | bytes 1216520 | tf_op jit(solution)/shard_map/ppermute | solution.py:300
  101.2 1.3 %shard_map.82 = (bf16[272,384]{1,0:T(8,128)(2,1)S(1)}, bf16[272,384]{1,0:T(8,128)(2,1)S(1)}) custom-call(s32[5]{0:T(128)S(1)} %stack.23.meta_ref, bf16[8,1024,384]{2,1,0:T(8,128)(2,1)S(1)} %copy-done.1, bf16[528,1024]{1,0:T(8,128)(2,1)S(1)} %get-tuple-element.40.panel_ref, bf16[3,272,384]{2,1,0:T(8,128)(2,1)S(1)} %collective-permute-done.17.refs_0_.over, ...), custom_call_target="tpu_custom_call" | custom-call | flops 427819008 | bytes 2826240 | tf_op jit(solution)/shard_map/pallas_call | solution.py:189
  102.7 3.6 %collective-permute-start.27 = (bf16[272,384]{1,0:T(8,128)(2,1)S(1)}, bf16[272,384]{1,0:T(8,128)(2,1)S(1)}, u32[]{:S(2)}, u32[]{:S(2)}) collective-permute-start(bf16[272,384]{1,0:T(8,128)(2,1)S(1)} %get-tuple-element.37), channel_id=1, source_target_pairs={{0,112},{16,0},{32,16},{48,32},{64,48},{80,64},{96,80},{112,96},{1... | collective-permute-start | bytes 626696 | tf_op jit(solution)/shard_map/ppermute | solution.py:300
  106.3 2.2 %collective-permute-done.10.up = bf16[528,384]{1,0:T(8,128)(2,1)S(1)} collective-permute-done((bf16[528,384]{1,0:T(8,128)(2,1)S(1)}, bf16[528,384]{1,0:T(8,128)(2,1)S(1)}, u32[]{:S(2)}, u32[]{:S(2)}) %collective-permute-start.10) | collective-permute-done | bytes 405536 | tf_op jit(solution)/shard_map/ppermute | solution.py:300
  108.5 1.5 %shard_map.74 = (f32[192,512]{1,0:T(8,128)S(1)}, f32[8,192]{1,0:T(8,128)S(1)}, bf16[208,512]{1,0:T(8,128)(2,1)S(1)}) custom-call(s32[5]{0:T(128)S(1)} %stack.23.meta_ref, bf16[8,1024,384]{2,1,0:T(8,128)(2,1)S(1)} %copy-done.1, bf16[528,1024]{1,0:T(8,128)(2,1)S(1)} %get-tuple-element.41.panel_ref, bf16[528,384]{1,0:T(8,128)(2,1)S(1)} %collective-permute-done.9.down, ...), custom_call_target="tpu_custom_call" | custom-call | flops 415236096 | bytes 1572864 | tf_op jit(solution)/shard_map/pallas_call | solution.py:220
  109.9 1.0 collective-permute-start.11
  111.0 1.2 shard_map.83
  112.2 1.2 collective-permute-start.29
  113.4 2.0 %collective-permute-start.28 = (f32[192,256]{1,0:T(8,128)S(1)}, f32[192,256]{1,0:T(8,128)S(1)}, u32[]{:S(2)}, u32[]{:S(2)}) collective-permute-start(f32[192,256]{1,0:T(8,128)S(1)} %get-tuple-element.38), channel_id=1, source_target_pairs={{0,1},{1,0},{2,3},{3,2},{4,5},{5,4},{6,7},{7,6},{8,9},{9,8},{10,11... | collective-permute-start | bytes 589832 | tf_op jit(solution)/shard_map/ppermute | solution.py:322
  115.4 5.3 %collective-permute-done.28.near_ref = f32[192,256]{1,0:T(8,128)S(1)} collective-permute-done((f32[192,256]{1,0:T(8,128)S(1)}, f32[192,256]{1,0:T(8,128)S(1)}, u32[]{:S(2)}, u32[]{:S(2)}) %collective-permute-start.28) | collective-permute-done | bytes 196640 | tf_op jit(solution)/shard_map/ppermute | solution.py:322
  121.3 1.7 %shard_map.84 = (f32[1,2,192,512]{3,2,1,0:T(8,128)}, f32[1,2,192]{2,1,0:T(2,128)}) custom-call(s32[5]{0:T(128)S(1)} %stack.23.meta_ref, f32[192,512]{1,0:T(8,128)S(1)} %get-tuple-element.29.own_ref, f32[8,192]{1,0:T(8,128)S(1)} %get-tuple-element.30.rhs_ref, bf16[208,512]{1,0:T(8,128)(2,1)S(1)} %collective-permute-done.11.part_ref, ...), custom_call_target="tpu_custom_call" | custom-call | bytes 6291456 | tf_op jit(solution)/shard_map/pallas_call | solution.py:288
  (53 shorter events, 6.6 us)
Async XLA Ops:
  2.3 15.2 %collective-permute-start = (bf16[64,1024]{1,0:T(8,128)(2,1)}, bf16[64,1024]{1,0:T(8,128)(2,1)S(1)}, u32[]{:S(2)}, u32[]{:S(2)}) collective-permute-start(bf16[64,1024]{1,0:T(8,128)(2,1)} %get-tuple-element.21), channel_id=1, source_target_pairs={{0,12},{2,14},{4,0},{6,2},{8,4},{10,6},{12,8},{14,10},{1,13},{3,15... | collective-permute-start | bytes 393224 | tf_op jit(solution)/shard_map/ppermute | solution.py:312
  2.7 14.8 %collective-permute-start.1 = (bf16[64,1024]{1,0:T(8,128)(2,1)}, bf16[64,1024]{1,0:T(8,128)(2,1)S(1)}, u32[]{:S(2)}, u32[]{:S(2)}) collective-permute-start(bf16[64,1024]{1,0:T(8,128)(2,1)} %get-tuple-element.21), channel_id=1, source_target_pairs={{0,8},{2,10},{4,12},{6,14},{8,0},{10,2},{12,4},{14,6},{1,9},{3,11}... | collective-permute-start | bytes 393224 | tf_op jit(solution)/shard_map/ppermute | solution.py:312
  5.6 11.9 %collective-permute-start.2 = (bf16[64,1024]{1,0:T(8,128)(2,1)}, bf16[64,1024]{1,0:T(8,128)(2,1)S(1)}, u32[]{:S(2)}, u32[]{:S(2)}) collective-permute-start(bf16[64,1024]{1,0:T(8,128)(2,1)} %get-tuple-element.21), channel_id=1, source_target_pairs={{0,4},{2,6},{4,8},{6,10},{8,12},{10,14},{12,0},{14,2},{1,5},{3,7},... | collective-permute-start | bytes 393224 | tf_op jit(solution)/shard_map/ppermute | solution.py:312
  7.0 10.7 %collective-permute-start.12 = (bf16[64,1024]{1,0:T(8,128)(2,1)}, bf16[64,1024]{1,0:T(8,128)(2,1)S(1)}, u32[]{:S(2)}, u32[]{:S(2)}) collective-permute-start(bf16[64,1024]{1,0:T(8,128)(2,1)} %get-tuple-element.21), channel_id=1, source_target_pairs={{0,1},{1,0},{2,3},{3,2},{4,5},{5,4},{6,7},{7,6},{8,9},{9,8},{10,11... | collective-permute-start | bytes 393224 | tf_op jit(solution)/shard_map/ppermute | solution.py:322
  9.6 2.8 %copy-start.2 = (bf16[1024,3072]{1,0:T(8,128)(2,1)S(1)}, bf16[1024,3072]{1,0:T(8,128)(2,1)}, u32[]{:S(2)}) copy-start(bf16[1024,3072]{1,0:T(8,128)(2,1)} %rows_ref.1) | copy-start | bytes 18874372
  12.4 5.1 %copy-start.3 = (bf16[64,1024]{1,0:T(8,128)(2,1)S(1)}, bf16[64,1024]{1,0:T(8,128)(2,1)}, u32[]{:S(2)}) copy-start(bf16[64,1024]{1,0:T(8,128)(2,1)} %get-tuple-element.21) | copy-start | bytes 393220
  14.7 2.7 %copy-start = (bf16[8,1024,384]{2,1,0:T(8,128)(2,1)}, bf16[8,1024,384]{2,1,0:T(8,128)(2,1)S(1)}, u32[]{:S(2)}) copy-start(bf16[8,1024,384]{2,1,0:T(8,128)(2,1)S(1)} %shard_map.68.rows_ref) | copy-start | bytes 18874372
  17.5 12.4 %collective-permute-start.3 = (bf16[256,1024]{1,0:T(8,128)(2,1)S(1)}, bf16[256,1024]{1,0:T(8,128)(2,1)S(1)}, u32[]{:S(2)}, u32[]{:S(2)}) collective-permute-start(bf16[256,1024]{1,0:T(8,128)(2,1)S(1)} %pad_maximum_fusion), channel_id=1, source_target_pairs={{0,2},{2,0},{4,6},{6,4},{8,10},{10,8},{12,14},{14,12},{1,3},{3,1},... | collective-permute-start | bytes 1572872 | tf_op jit(solution)/shard_map/ppermute | solution.py:318
  17.7 8.3 %collective-permute-start.13 = (bf16[64,1024]{1,0:T(8,128)(2,1)S(1)}, bf16[64,1024]{1,0:T(8,128)(2,1)S(1)}, u32[]{:S(2)}, u32[]{:S(2)}) collective-permute-start(bf16[64,1024]{1,0:T(8,128)(2,1)S(1)} %collective-permute-done.12), channel_id=1, source_target_pairs={{0,12},{2,14},{4,0},{6,2},{8,4},{10,6},{12,8},{14,10},{1,13},{3,15... | collective-permute-start | bytes 393224 | tf_op jit(solution)/shard_map/ppermute | solution.py:312
  19.8 8.0 %collective-permute-start.14 = (bf16[64,1024]{1,0:T(8,128)(2,1)S(1)}, bf16[64,1024]{1,0:T(8,128)(2,1)S(1)}, u32[]{:S(2)}, u32[]{:S(2)}) collective-permute-start(bf16[64,1024]{1,0:T(8,128)(2,1)S(1)} %collective-permute-done.12), channel_id=1, source_target_pairs={{0,8},{2,10},{4,12},{6,14},{8,0},{10,2},{12,4},{14,6},{1,9},{3,11}... | collective-permute-start | bytes 393224 | tf_op jit(solution)/shard_map/ppermute | solution.py:312
  21.7 8.0 %collective-permute-start.15 = (bf16[64,1024]{1,0:T(8,128)(2,1)S(1)}, bf16[64,1024]{1,0:T(8,128)(2,1)S(1)}, u32[]{:S(2)}, u32[]{:S(2)}) collective-permute-start(bf16[64,1024]{1,0:T(8,128)(2,1)S(1)} %collective-permute-done.12), channel_id=1, source_target_pairs={{0,4},{2,6},{4,8},{6,10},{8,12},{10,14},{12,0},{14,2},{1,5},{3,7},... | collective-permute-start | bytes 393224 | tf_op jit(solution)/shard_map/ppermute | solution.py:312
  29.8 2.0 %collective-permute-start.16 = (bf16[256,1024]{1,0:T(8,128)(2,1)S(1)}, bf16[256,1024]{1,0:T(8,128)(2,1)S(1)}, u32[]{:S(2)}, u32[]{:S(2)}) collective-permute-start(bf16[256,1024]{1,0:T(8,128)(2,1)S(1)} %pad_maximum_fusion.1), channel_id=1, source_target_pairs={{0,2},{2,0},{4,6},{6,4},{8,10},{10,8},{12,14},{14,12},{1,3},{3,1},... | collective-permute-start | bytes 1572872 | tf_op jit(solution)/shard_map/ppermute | solution.py:318
  29.9 1.9 %copy-start.4 = (bf16[16,1024]{1,0:T(8,128)(2,1)S(1)}, bf16[16,1024]{1,0:T(8,128)(2,1)}, u32[]{:S(2)}) copy-start(bf16[16,1024]{1,0:T(8,128)(2,1)} %get-tuple-element.22) | copy-start | bytes 98308
  31.8 2.8 %copy-start.1 = (bf16[8,1024,384]{2,1,0:T(8,128)(2,1)S(1)}, bf16[8,1024,384]{2,1,0:T(8,128)(2,1)}, u32[]{:S(2)}) copy-start(bf16[8,1024,384]{2,1,0:T(8,128)(2,1)} %copy-done) | copy-start | bytes 18874372
  35.9 14.9 %collective-permute-start.4 = (bf16[528,384]{1,0:T(8,128)(2,1)S(1)}, bf16[528,384]{1,0:T(8,128)(2,1)S(1)}, u32[]{:S(2)}, u32[]{:S(2)}) collective-permute-start(bf16[528,384]{1,0:T(8,128)(2,1)S(1)} %shard_map.70), channel_id=1, source_target_pairs={{0,112},{16,0},{32,16},{48,32},{64,48},{80,64},{96,80},{112,96},{1... | collective-permute-start | bytes 1216520 | tf_op jit(solution)/shard_map/ppermute | solution.py:300
  52.6 14.1 %collective-permute-start.5 = (bf16[528,384]{1,0:T(8,128)(2,1)S(1)}, bf16[528,384]{1,0:T(8,128)(2,1)S(1)}, u32[]{:S(2)}, u32[]{:S(2)}) collective-permute-start(bf16[528,384]{1,0:T(8,128)(2,1)S(1)} %get-tuple-element.23), channel_id=1, source_target_pairs={{0,112},{16,0},{32,16},{48,32},{64,48},{80,64},{96,80},{112,96},{1... | collective-permute-start | bytes 1216520 | tf_op jit(solution)/shard_map/ppermute | solution.py:300
  56.4 12.8 %collective-permute-start.6 = (bf16[528,384]{1,0:T(8,128)(2,1)S(1)}, bf16[528,384]{1,0:T(8,128)(2,1)S(1)}, u32[]{:S(2)}, u32[]{:S(2)}) collective-permute-start(bf16[528,384]{1,0:T(8,128)(2,1)S(1)} %get-tuple-element.24), channel_id=1, source_target_pairs={{0,16},{16,32},{32,48},{48,64},{64,80},{80,96},{96,112},{112,0},{1... | collective-permute-start | bytes 1216520 | tf_op jit(solution)/shard_map/ppermute | solution.py:300
  57.4 8.2 %collective-permute-start.20 = (bf16[1,272,384]{2,1,0:T(8,128)(2,1)S(1)}, bf16[1,272,384]{2,1,0:T(8,128)(2,1)S(1)}, u32[]{:S(2)}, u32[]{:S(2)}) collective-permute-start(bf16[1,272,384]{2,1,0:T(8,128)(2,1)S(1)} %shard_map.78), channel_id=1, source_target_pairs={{0,128},{16,144},{32,160},{48,176},{64,192},{80,208},{96,224},{112... | collective-permute-start | bytes 626696 | tf_op jit(solution)/shard_map/ppermute | solution.py:306
  59.4 16.5 %collective-permute-start.19 = (bf16[2,272,384]{2,1,0:T(8,128)(2,1)S(1)}, bf16[2,272,384]{2,1,0:T(8,128)(2,1)S(1)}, u32[]{:S(2)}, u32[]{:S(2)}) collective-permute-start(bf16[2,272,384]{2,1,0:T(8,128)(2,1)S(1)} %shard_map.77), channel_id=1, source_target_pairs={{0,128},{16,144},{32,160},{48,176},{64,192},{80,208},{96,224},{112... | collective-permute-start | bytes 1253384 | tf_op jit(solution)/shard_map/ppermute | solution.py:306
  62.2 21.3 %collective-permute-start.18 = (bf16[2,272,384]{2,1,0:T(8,128)(2,1)S(1)}, bf16[2,272,384]{2,1,0:T(8,128)(2,1)S(1)}, u32[]{:S(2)}, u32[]{:S(2)}) collective-permute-start(bf16[2,272,384]{2,1,0:T(8,128)(2,1)S(1)} %shard_map.76), channel_id=1, source_target_pairs={{0,128},{16,144},{32,160},{48,176},{64,192},{80,208},{96,224},{112... | collective-permute-start | bytes 1253384 | tf_op jit(solution)/shard_map/ppermute | solution.py:306
  66.6 8.8 %collective-permute-start.21 = (bf16[272,384]{1,0:T(8,128)(2,1)S(1)}, bf16[272,384]{1,0:T(8,128)(2,1)S(1)}, u32[]{:S(2)}, u32[]{:S(2)}) collective-permute-start(bf16[272,384]{1,0:T(8,128)(2,1)S(1)} %shard_map.79), channel_id=1, source_target_pairs={{0,16},{16,32},{32,48},{48,64},{64,80},{80,96},{96,112},{112,0},{1... | collective-permute-start | bytes 626696 | tf_op jit(solution)/shard_map/ppermute | solution.py:300
  71.0 24.5 %collective-permute-start.7 = (bf16[528,384]{1,0:T(8,128)(2,1)S(1)}, bf16[528,384]{1,0:T(8,128)(2,1)S(1)}, u32[]{:S(2)}, u32[]{:S(2)}) collective-permute-start(bf16[528,384]{1,0:T(8,128)(2,1)S(1)} %get-tuple-element.25), channel_id=1, source_target_pairs={{0,112},{16,0},{32,16},{48,32},{64,48},{80,64},{96,80},{112,96},{1... | collective-permute-start | bytes 1216520 | tf_op jit(solution)/shard_map/ppermute | solution.py:300
  71.9 23.6 %collective-permute-start.8 = (bf16[528,384]{1,0:T(8,128)(2,1)S(1)}, bf16[528,384]{1,0:T(8,128)(2,1)S(1)}, u32[]{:S(2)}, u32[]{:S(2)}) collective-permute-start(bf16[528,384]{1,0:T(8,128)(2,1)S(1)} %get-tuple-element.26), channel_id=1, source_target_pairs={{0,16},{16,32},{32,48},{48,64},{64,80},{80,96},{96,112},{112,0},{1... | collective-permute-start | bytes 1216520 | tf_op jit(solution)/shard_map/ppermute | solution.py:300
  75.4 25.2 %collective-permute-start.17 = (bf16[3,272,384]{2,1,0:T(8,128)(2,1)S(1)}, bf16[3,272,384]{2,1,0:T(8,128)(2,1)S(1)}, u32[]{:S(2)}, u32[]{:S(2)}) collective-permute-start(bf16[3,272,384]{2,1,0:T(8,128)(2,1)S(1)} %shard_map.75), channel_id=1, source_target_pairs={{0,128},{16,144},{32,160},{48,176},{64,192},{80,208},{96,224},{112... | collective-permute-start | bytes 1880072 | tf_op jit(solution)/shard_map/ppermute | solution.py:306
  77.2 9.7 %collective-permute-start.22 = (bf16[272,384]{1,0:T(8,128)(2,1)S(1)}, bf16[272,384]{1,0:T(8,128)(2,1)S(1)}, u32[]{:S(2)}, u32[]{:S(2)}) collective-permute-start(bf16[272,384]{1,0:T(8,128)(2,1)S(1)} %get-tuple-element.32), channel_id=1, source_target_pairs={{0,16},{16,32},{32,48},{48,64},{64,80},{80,96},{96,112},{112,0},{1... | collective-permute-start | bytes 626696 | tf_op jit(solution)/shard_map/ppermute | solution.py:300
  83.5 6.6 %collective-permute-start.23 = (bf16[272,384]{1,0:T(8,128)(2,1)S(1)}, bf16[272,384]{1,0:T(8,128)(2,1)S(1)}, u32[]{:S(2)}, u32[]{:S(2)}) collective-permute-start(bf16[272,384]{1,0:T(8,128)(2,1)S(1)} %get-tuple-element.33), channel_id=1, source_target_pairs={{0,112},{16,0},{32,16},{48,32},{64,48},{80,64},{96,80},{112,96},{1... | collective-permute-start | bytes 626696 | tf_op jit(solution)/shard_map/ppermute | solution.py:300
  91.4 9.9 %collective-permute-start.24 = (bf16[272,384]{1,0:T(8,128)(2,1)S(1)}, bf16[272,384]{1,0:T(8,128)(2,1)S(1)}, u32[]{:S(2)}, u32[]{:S(2)}) collective-permute-start(bf16[272,384]{1,0:T(8,128)(2,1)S(1)} %get-tuple-element.34), channel_id=1, source_target_pairs={{0,16},{16,32},{32,48},{48,64},{64,80},{80,96},{96,112},{112,0},{1... | collective-permute-start | bytes 626696 | tf_op jit(solution)/shard_map/ppermute | solution.py:300
  91.5 9.8 %collective-permute-start.25 = (bf16[272,384]{1,0:T(8,128)(2,1)S(1)}, bf16[272,384]{1,0:T(8,128)(2,1)S(1)}, u32[]{:S(2)}, u32[]{:S(2)}) collective-permute-start(bf16[272,384]{1,0:T(8,128)(2,1)S(1)} %get-tuple-element.35), channel_id=1, source_target_pairs={{0,112},{16,0},{32,16},{48,32},{64,48},{80,64},{96,80},{112,96},{1... | collective-permute-start | bytes 626696 | tf_op jit(solution)/shard_map/ppermute | solution.py:300
  97.3 11.1 %collective-permute-start.10 = (bf16[528,384]{1,0:T(8,128)(2,1)S(1)}, bf16[528,384]{1,0:T(8,128)(2,1)S(1)}, u32[]{:S(2)}, u32[]{:S(2)}) collective-permute-start(bf16[528,384]{1,0:T(8,128)(2,1)S(1)} %get-tuple-element.28), channel_id=1, source_target_pairs={{0,16},{16,32},{32,48},{48,64},{64,80},{80,96},{96,112},{112,0},{1... | collective-permute-start | bytes 1216520 | tf_op jit(solution)/shard_map/ppermute | solution.py:300
  97.4 11.0 %collective-permute-start.9 = (bf16[528,384]{1,0:T(8,128)(2,1)S(1)}, bf16[528,384]{1,0:T(8,128)(2,1)S(1)}, u32[]{:S(2)}, u32[]{:S(2)}) collective-permute-start(bf16[528,384]{1,0:T(8,128)(2,1)S(1)} %get-tuple-element.27), channel_id=1, source_target_pairs={{0,112},{16,0},{32,16},{48,32},{64,48},{80,64},{96,80},{112,96},{1... | collective-permute-start | bytes 1216520 | tf_op jit(solution)/shard_map/ppermute | solution.py:300
  102.6 8.4 %collective-permute-start.26 = (bf16[272,384]{1,0:T(8,128)(2,1)S(1)}, bf16[272,384]{1,0:T(8,128)(2,1)S(1)}, u32[]{:S(2)}, u32[]{:S(2)}) collective-permute-start(bf16[272,384]{1,0:T(8,128)(2,1)S(1)} %get-tuple-element.36), channel_id=1, source_target_pairs={{0,16},{16,32},{32,48},{48,64},{64,80},{80,96},{96,112},{112,0},{1... | collective-permute-start | bytes 626696 | tf_op jit(solution)/shard_map/ppermute | solution.py:300
  102.7 8.3 %collective-permute-start.27 = (bf16[272,384]{1,0:T(8,128)(2,1)S(1)}, bf16[272,384]{1,0:T(8,128)(2,1)S(1)}, u32[]{:S(2)}, u32[]{:S(2)}) collective-permute-start(bf16[272,384]{1,0:T(8,128)(2,1)S(1)} %get-tuple-element.37), channel_id=1, source_target_pairs={{0,112},{16,0},{32,16},{48,32},{64,48},{80,64},{96,80},{112,96},{1... | collective-permute-start | bytes 626696 | tf_op jit(solution)/shard_map/ppermute | solution.py:300
  109.9 11.4 %collective-permute-start.11 = (bf16[208,512]{1,0:T(8,128)(2,1)S(1)}, bf16[208,512]{1,0:T(8,128)(2,1)S(1)}, u32[]{:S(2)}, u32[]{:S(2)}) collective-permute-start(bf16[208,512]{1,0:T(8,128)(2,1)S(1)} %get-tuple-element.31), channel_id=1, source_target_pairs={{0,128},{16,144},{32,160},{48,176},{64,192},{80,208},{96,224},{112... | collective-permute-start | bytes 638984 | tf_op jit(solution)/shard_map/ppermute | solution.py:306
  112.2 9.2 %collective-permute-start.29 = (f32[200,256]{1,0:T(8,128)S(1)}, f32[200,256]{1,0:T(8,128)S(1)}, u32[]{:S(2)}, u32[]{:S(2)}) collective-permute-start(f32[200,256]{1,0:T(8,128)S(1)} %get-tuple-element.39), channel_id=1, source_target_pairs={{0,129},{1,128},{16,145},{17,144},{32,161},{33,160},{48,177},{49,1... | collective-permute-start | bytes 614408 | tf_op jit(solution)/shard_map/ppermute | solution.py:331
  113.4 7.3 %collective-permute-start.28 = (f32[192,256]{1,0:T(8,128)S(1)}, f32[192,256]{1,0:T(8,128)S(1)}, u32[]{:S(2)}, u32[]{:S(2)}) collective-permute-start(f32[192,256]{1,0:T(8,128)S(1)} %get-tuple-element.38), channel_id=1, source_target_pairs={{0,1},{1,0},{2,3},{3,2},{4,5},{5,4},{6,7},{7,6},{8,9},{9,8},{10,11... | collective-permute-start | bytes 589832 | tf_op jit(solution)/shard_map/ppermute | solution.py:322

commit v2 on v1

v2 whole, which is shorter than its diff:
```python
import functools

import jax
import jax.numpy as jnp
from jax import lax
from jax.experimental import pallas as pl
from jax.experimental.pallas import tpu as pltpu
from jax.sharding import PartitionSpec as P

NZ = 8
ROWS = 192
PAIR = 2 * ROWS
HALF = 512
PART = 256
TAIL = 16
BF16, F32 = jnp.bfloat16, jnp.float32
IN_VMEM = pl.BlockSpec(memory_space=pltpu.VMEM)
IN_SMEM = pl.BlockSpec(memory_space=pltpu.SMEM)


def call(kernel, out_shape, args, after=(), scratch=(), cost=4e9):
    n, extra = len(args), len(after)

    def body(*refs):
        kernel(*refs[:n], *refs[n + extra :])

    return pl.pallas_call(
        body,
        out_shape=out_shape,
        in_specs=[IN_SMEM] + [IN_VMEM] * (n - 1 + extra),
        out_specs=[IN_VMEM] * len(out_shape),
        scratch_shapes=list(scratch),
        compiler_params=pltpu.CompilerParams(vmem_limit_bytes=16 * 2**20),
        cost_estimate=pl.CostEstimate(flops=int(cost), bytes_accessed=1, transcendentals=0),
    )(*args, *after)


def weigh_kernel(sigma_ref, panel_ref, obs_ref, ids_ref, panel_out, obs_out):
    ids = ids_ref[...]
    sigma = jnp.full(ids.shape, sigma_ref[0], F32)
    for g in range(1, sigma_ref.shape[0]):
        sigma = jnp.where(ids == g, sigma_ref[g], sigma)
    weights = 1.0 / (sigma * sigma)
    panel_out[...] = (weights * panel_ref[...].astype(F32)).astype(BF16)
    weighted = (weights * obs_ref[...]).astype(BF16)
    obs_out[...] = jnp.broadcast_to(weighted, obs_out.shape)


def weigh(panel_t, observations, group_ids, group_sigma):
    cols, points = panel_t.shape
    flat = pl.BlockSpec((1, points), lambda i: (0, 0))
    return pl.pallas_call(
        weigh_kernel,
        grid=(1,),
        out_shape=(
            jax.ShapeDtypeStruct((cols, points), BF16),
            jax.ShapeDtypeStruct((TAIL, points), BF16),
        ),
        in_specs=[IN_SMEM, pl.BlockSpec((cols, points), lambda i: (0, 0)), flat, flat],
        out_specs=[IN_VMEM, IN_VMEM],
    )(group_sigma, panel_t, observations.reshape(1, -1), group_ids.reshape(1, -1))


def pair_kernel(meta_ref, first_ref, second_ref, out_ref):
    e = pl.program_id(0)
    for half in range(2):
        lanes = slice(half * ROWS, (half + 1) * ROWS)
        out_ref[2 * e + half] = jnp.concatenate(
            [first_ref[:, lanes], second_ref[:, lanes]], axis=1
        )


def pair_up(meta, design_rows):
    points = design_rows.shape[0]
    return pl.pallas_call(
        pair_kernel,
        grid=(NZ // 2,),
        out_shape=jax.ShapeDtypeStruct((NZ, points, PAIR), BF16),
        in_specs=[
            IN_SMEM,
            pl.BlockSpec((points, PAIR), lambda e: (0, e)),
            pl.BlockSpec((points, PAIR), lambda e: (0, e + NZ // 2)),
        ],
        out_specs=IN_VMEM,
        compiler_params=pltpu.CompilerParams(vmem_limit_bytes=12 * 2**20),
        cost_estimate=pl.CostEstimate(
            flops=0, bytes_accessed=4 * design_rows.size, transcendentals=0
        ),
    )(meta, design_rows, design_rows)


def collect_kernel(meta_ref, *refs):
    at = 0
    for ref in refs[:-1]:
        refs[-1][at : at + ref.shape[0], :] = ref[...]
        at += ref.shape[0]


def collect(meta, blocks, after):
    rows = sum(b.shape[0] for b in blocks)
    return call(
        collect_kernel,
        [jax.ShapeDtypeStruct((rows, blocks[0].shape[1]), BF16)],
        (meta, *blocks),
        after,
        cost=1e9,
    )[0]


def product(left, right):
    return jnp.dot(left, right, preferred_element_type=F32)


def plus(total, received):
    return total + received[...].astype(F32)


def plus_tailed(total, received):
    main = total[:-TAIL] + received[:-TAIL, :].astype(F32)
    tail = received[-TAIL:, :].astype(F32)
    more = tail[: TAIL // 2] + tail[TAIL // 2 :]
    return jnp.concatenate([main, total[-TAIL:] + jnp.concatenate([more, more], axis=0)], axis=0)


def split(value):
    high = value.astype(BF16).astype(F32)
    return high, value - high


def packed(total):
    high, low = split(total[-TAIL // 2 :])
    return jnp.concatenate([total[:-TAIL], high, low], axis=0).astype(BF16)


def place(meta_ref, dz):
    return (meta_ref[0] + dz) & (NZ - 1)


def x_rows(panel_ref, which):
    at = pl.multiple_of(which * PART, PART)
    return jnp.concatenate([panel_ref[pl.ds(at, PART), :], panel_ref[HALF:, :]], axis=0)


def z_kernel(steps, meta_ref, rows_ref, panel_ref, *refs):
    received, outs = refs[: -len(steps)], refs[-len(steps) :]
    left = panel_ref[:HALF, :]
    for i, dz in enumerate(steps):
        total = product(left, rows_ref[place(meta_ref, dz)])
        if i < len(received):
            total = plus(total, received[i])
        outs[i][...] = total.astype(BF16)


def z_step(meta, rows, panel, steps, received, after):
    return call(
        functools.partial(z_kernel, steps),
        [jax.ShapeDtypeStruct((HALF, PAIR), BF16)] * len(steps),
        (meta, rows, panel, *received),
        after,
    )


def over_kernel(steps, meta_ref, rows_ref, panel_ref, out_ref):
    left = x_rows(panel_ref, 1 - meta_ref[1])
    for i, dz in enumerate(steps):
        out_ref[i] = packed(product(left, rows_ref[place(meta_ref, dz)]))


def over_x(meta, rows, panel, steps, after):
    return call(
        functools.partial(over_kernel, steps),
        [jax.ShapeDtypeStruct((len(steps), PART + TAIL, PAIR), BF16)],
        (meta, rows, panel),
        after,
    )


def x_kernel(steps, picks, n_over, meta_ref, rows_ref, panel_ref, *refs):
    over, refs = refs[:n_over], refs[n_over:]
    received, outs = refs[: -len(steps)], refs[-len(steps) :]
    left = x_rows(panel_ref, meta_ref[1])
    for i, dz in enumerate(steps):
        total = product(left, rows_ref[place(meta_ref, dz)])
        which, at = picks[i]
        total = plus_tailed(total, over[which].at[at])
        if i < len(received):
            total = plus_tailed(total, received[i])
        outs[i][...] = packed(total)


def x_step(meta, rows, panel, steps, over, received, after):
    arrays, picks = [], []
    for dz in steps:
        array, at = over[dz]
        known = [a is array for a in arrays]
        if not any(known):
            known.append(True)
            arrays.append(array)
        picks.append((known.index(True), at))
    return call(
        functools.partial(x_kernel, steps, tuple(picks), len(arrays)),
        [jax.ShapeDtypeStruct((PART + TAIL, PAIR), BF16)] * len(steps),
        (meta, rows, panel, *arrays, *received),
        after,
    )


def halves(total):
    cols = total.shape[0]
    return [
        jnp.concatenate([total[c : c + 64] for c in range(first, cols, 128)], axis=0).T
        for first in (0, 64)
    ]


def last_kernel(
    at, meta_ref, rows_ref, near_ref, other_ref, over, x_up, x_down, z_down, z_up,
    own_x, own_z, rhs, beside, cross, across, x_this, x_that, z_this, z_that,
):
    side = meta_ref[1]
    right = rows_ref[meta_ref[0]]
    total = product(x_rows(near_ref, side), right)
    total = plus_tailed(plus_tailed(plus_tailed(total, over.at[at]), x_up), x_down)
    x_this[...], x_that[...] = halves(total[:PART])
    tail = total[PART:]
    total = plus(plus(product(other_ref[:HALF, :], right), z_down), z_up)
    z_this[...], z_that[...] = halves(total)
    mine = pl.ds(pl.multiple_of(side * ROWS, ROWS), ROWS)
    theirs = pl.ds(pl.multiple_of((1 - side) * ROWS, ROWS), ROWS)
    own_x[...] = x_this[mine, :]
    own_z[...] = z_this[mine, :]
    for out, x, z, where in (
        (beside, x_this, z_this, theirs),
        (cross, x_that, z_that, theirs),
        (across, x_that, z_that, mine),
    ):
        high, low = split(x[where, :])
        out[:ROWS, :] = jnp.concatenate([high, low, z[where, :]], axis=1).astype(BF16)
    lower, upper = tail[: TAIL // 2, :ROWS], tail[: TAIL // 2, ROWS:]
    rhs[...] = jnp.where(side == 0, lower, upper)
    high, low = split(jnp.where(side == 0, upper, lower))
    sent = jnp.concatenate([high, low], axis=0)
    zeros = jnp.zeros((TAIL, HALF - ROWS), F32)
    cross[ROWS:, :] = jnp.concatenate([sent, zeros], axis=1).astype(BF16)


def last(meta, rows, near, other, over, x_got, z_got, after):
    array, at = over
    message = jax.ShapeDtypeStruct((ROWS, HALF), BF16)
    return call(
        functools.partial(last_kernel, at),
        [
            jax.ShapeDtypeStruct((ROWS, PART // 2), F32),
            jax.ShapeDtypeStruct((ROWS, PART), F32),
            jax.ShapeDtypeStruct((TAIL // 2, ROWS), F32),
            message,
            jax.ShapeDtypeStruct((ROWS + TAIL, HALF), BF16),
            message,
        ],
        (meta, rows, near, other, array, *x_got, *z_got),
        after,
        scratch=[pltpu.VMEM((PAIR, n), F32) for n in (PART // 2, PART // 2, PART, PART)],
    )


def parts(message_ref):
    value = message_ref[:ROWS, :].astype(F32)
    quarter = HALF // 4
    return value[:, :quarter] + value[:, quarter : 2 * quarter], value[:, 2 * quarter :]


def finish_kernel(
    meta_ref, own_x, own_z, rhs_ref, beside_ref, cross_ref, across_ref, out_ref, rhs_out
):
    side, y, core, half = meta_ref[1], meta_ref[2], meta_ref[3], meta_ref[4]
    (beside_x, beside_z), (cross_x, cross_z), (across_x, across_z) = (
        parts(r) for r in (beside_ref, cross_ref, across_ref)
    )
    for where_to, here, there, other in (
        (half, own_x[...], beside_x, own_z[...] + beside_z),
        (1 - half, across_x, cross_x, cross_z + across_z),
    ):
        near = jnp.concatenate(
            [jnp.where(side == 0, here, there), jnp.where(side == 0, there, here)], axis=1
        )
        first = jnp.where(core == 0, near, other)
        second = jnp.where(core == 0, other, near)
        for dy in range(4):
            lanes = slice(dy * 64, dy * 64 + 64)
            at = pl.multiple_of(((y + dy) & 3) * 128, 128)
            out_ref[0, where_to, :, pl.ds(at, 128)] = jnp.concatenate(
                [first[:, lanes], second[:, lanes]], axis=1
            )
    tail = cross_ref[ROWS:, :].astype(F32)[:, :ROWS]
    mine = rhs_ref[...][:1]
    other = (tail[: TAIL // 2] + tail[TAIL // 2 :])[:1]
    rhs_out[0] = jnp.concatenate(
        [jnp.where(half == 0, mine, other), jnp.where(half == 0, other, mine)], axis=0
    )


def finish(meta, *args):
    return call(
        finish_kernel,
        [
            jax.ShapeDtypeStruct((1, 2, ROWS, HALF), F32),
            jax.ShapeDtypeStruct((1, 2, ROWS), F32),
        ],
        (meta, *args),
    )


def z_shift(x, d):
    return lax.ppermute(
        x, "rep", [(a * NZ + z, a * NZ + (z + d) % NZ) for a in range(2) for z in range(NZ)]
    )


def x_swap(x):
    return lax.ppermute(
        x, "rep", [(a * NZ + z, (1 - a) * NZ + z) for a in range(2) for z in range(NZ)]
    )


def y_shift(x, d):
    return lax.ppermute(
        x, "row", [(y * 2 + c, (y + d) % 4 * 2 + c) for y in range(4) for c in range(2)]
    )


def core_swap(x):
    return lax.ppermute(x, "row", [(i, i ^ 1) for i in range(8)])


def half_swap(x):
    return lax.ppermute(x, "col", [(0, 1), (1, 0)])


def cross_swap(x):
    pairs = []
    for a in range(2):
        for z in range(NZ):
            for h in range(2):
                pairs.append(((a * NZ + z) * 2 + h, ((1 - a) * NZ + z) * 2 + 1 - h))
    return lax.ppermute(x, ("rep", "col"), pairs)


def per_device(design_rows, design_panel, observations, group_ids, group_sigma):
    rep, row, half = (lax.axis_index(n) for n in ("rep", "row", "col"))
    meta = jnp.stack([rep & (NZ - 1), rep >> 3, row >> 1, row & 1, half]).astype(jnp.int32)
    points = design_rows.shape[0]
    panel_t = jnp.transpose(design_panel.reshape(points, -1))
    mine, weighted_obs = weigh(panel_t, observations, group_ids, group_sigma)
    rows = pair_up(meta, design_rows)

    foreign = half_swap(mine)
    blocks = [mine, foreign]
    for d in (1, 2, 3):
        blocks.append(y_shift(mine, -d))
    for d in (1, 2, 3):
        blocks.append(y_shift(foreign, -d))
    near = collect(meta, blocks[:2] + [blocks[i] for i in (2, 5, 3, 6, 4, 7)] + [weighted_obs], (rows,))
    other = core_swap(near)

    over, z_got, x_got, after = {}, (), (), ()

    def piece(*steps):
        nonlocal after
        (sent,) = over_x(meta, rows, near, steps, after)
        after = (sent,)
        got = x_swap(sent)
        for i, dz in enumerate(steps):
            over[dz] = (got, i)

    def z_next(s):
        nonlocal after, z_got
        steps = (-s,) if s == 4 else (-s, s)
        sent = z_step(meta, rows, other, steps, z_got, after)
        after = (sent[0],)
        z_got = (z_shift(sent[0], -1),) + tuple(z_shift(v, 1) for v in sent[1:])

    def x_next(s):
        nonlocal after, x_got
        steps = (s,) if s == 4 else (s, -s)
        sent = x_step(meta, rows, near, steps, over, x_got, after)
        after = (sent[0],)
        x_got = (z_shift(sent[0], 1),) + tuple(z_shift(v, -1) for v in sent[1:])

    piece(4)
    piece(3, -3)
    z_next(4)
    x_next(4)
    piece(2, -2)
    piece(1, -1, 0)
    z_next(3)
    x_next(3)
    z_next(2)
    x_next(2)
    z_next(1)
    x_next(1)
    own_x, own_z, rhs_own, beside, cross, across = last(
        meta, rows, near, other, over[0], x_got, z_got, after
    )
    return finish(
        meta, own_x, own_z, rhs_own, x_swap(beside), cross_swap(cross), half_swap(across)
    )


def solution(mesh):
    in_specs = (P("rep", ("row", "col")), P("rep", "col", "row"), P("rep"), P("rep"), P())
    out_specs = (P("row", None, "rep", "col"), P("row", None, "rep"))
    return jax.shard_map(
        per_device, mesh=mesh, in_specs=in_specs, out_specs=out_specs, check_vma=False
    )
```

time: 124 us -> 106 us (0.85)
  waiting for transfers between devices: 42.5 us -> 29.3 us
  local copies, waits for them, and re-layouts: 9.42 us -> 2.88 us
  starting transfers between devices: 44.9 us -> 47.2 us
    ppermute x5, waiting for transfers between devices: 8.93 us -> 1.14 us  [x_swap(): lax.ppermute(x, 'rep', [(a * NZ + z, (1 - a) * NZ + z) for a in range(2)...]
    ppermute x6, waiting for transfers between devices: 7.63 us -> 0.02 us  [y_shift(): lax.ppermute(x, 'row', [(y * 2 + c, (y + d) % 4 * 2 + c) for y in range(4...]
    unnamed x20 -> x6, local copies, waits for them, and re-layouts: 9.33 us -> 2.79 us
    ppermute x14, waiting for transfers between devices: 18.2 us -> 23 us  [z_shift(): lax.ppermute(x, 'rep', [(a * NZ + z, a * NZ + (z + d) % NZ) for a in rang...]
    ppermute x2, starting transfers between devices: 3.7 us -> 7.07 us  [half_swap(): return lax.ppermute(x, 'col', [(0, 1), (1, 0)])]
    ppermute x6, starting transfers between devices: 9.1 us -> 12.1 us  [y_shift(): lax.ppermute(x, 'row', [(y * 2 + c, (y + d) % 4 * 2 + c) for y in range(4...]
    ppermute x14, starting transfers between devices: 26.3 us -> 24.4 us  [z_shift(): lax.ppermute(x, 'rep', [(a * NZ + z, a * NZ + (z + d) % NZ) for a in rang...]
    ppermute x2 -> x1, waiting for transfers between devices: 1.76 us -> 0.01 us  [core_swap(): return lax.ppermute(x, 'row', [(i, i ^ 1) for i in range(8)])]
  transfers between devices with their start and end apart: 30 -> 29, of which waited for: 15 -> 10; matrix products, arithmetic and copies ran while one was open for 1% -> 0% of each run, Pallas kernels for 15% -> 18%
where the time goes in v2:
time: 106 us; the launch traced here: 105 us
  starting transfers between devices  47.2 us (45%)
  waiting for transfers between devices  29.3 us (28%)
  Pallas kernels  25.1 us (24%)
  local copies, waits for them, and re-layouts  2.88 us (3%)
    ppermute x14, starting transfers between devices, z_shift(): lax.ppermute(x, 'rep', [(a * NZ + z, a * NZ + (z + d) % NZ) for a in rang...  24.4 us
    ppermute x14, waiting for transfers between devices, z_shift(): lax.ppermute(x, 'rep', [(a * NZ + z, a * NZ + (z + d) % NZ) for a in rang...  23 us
    pallas_call x15, Pallas kernels, call(): pl.pallas_call(body, out_shape=out_shape, in_specs=[IN_SMEM] + [IN_VMEM]...  20.9 us
    ppermute x6, starting transfers between devices, y_shift(): lax.ppermute(x, 'row', [(y * 2 + c, (y + d) % 4 * 2 + c) for y in range(4...  12.1 us
    ppermute x2, starting transfers between devices, half_swap(): return lax.ppermute(x, 'col', [(0, 1), (1, 0)])  7.07 us
    ppermute x2, waiting for transfers between devices, half_swap(): return lax.ppermute(x, 'col', [(0, 1), (1, 0)])  5.19 us
    ppermute x5, starting transfers between devices, x_swap(): lax.ppermute(x, 'rep', [(a * NZ + z, (1 - a) * NZ + z) for a in range(2)...  3.3 us
    unnamed x6, local copies, waits for them, and re-layouts  2.79 us
  transfers between devices with their start and end apart: 29, of which 10 were waited for; matrix products, arithmetic and copies ran while one was open for 0% of the time, Pallas kernels for 18%

profile of v2, /device:TPU:16, one launch (start us, length us, event | category | flops | bytes accessed | tf_op | source)
XLA Modules:
  0.0 105.4 jit_solution(16247526787005070122)
XLA Ops:
  0.6 1.6 %shard_map.69 = (bf16[64,1024]{1,0:T(8,128)(2,1)}, bf16[16,1024]{1,0:T(8,128)(2,1)}) custom-call(f32[8]{0:T(128)} %sigma_ref.1, bf16[64,1024]{1,0:T(8,128)(2,1)} %bitcast.10, f32[1,1024]{1,0:T(1,128)} %bitcast.11, s32[1,1024]{1,0:T(1,128)} %bitcast.12), custom_call_target="tpu_custom_call" | custom-call | tf_op jit(solution)/shard_map/pallas_call | solution.py:52
  2.3 3.0 %collective-permute-start = (bf16[64,1024]{1,0:T(8,128)(2,1)}, bf16[64,1024]{1,0:T(8,128)(2,1)S(1)}, u32[]{:S(2)}, u32[]{:S(2)}) collective-permute-start(bf16[64,1024]{1,0:T(8,128)(2,1)} %get-tuple-element.22.refs_1_), channel_id=1, source_target_pairs={{0,1},{1,0},{2,3},{3,2},{4,5},{5,4},{6,7},{7,6},{8,9},{9,8},{10,11... | collective-permute-start | bytes 393224 | tf_op jit(solution)/shard_map/ppermute | solution.py:336
  5.3 0.4 collective-permute-start.1
  5.7 2.9 %collective-permute-start.3 = (bf16[64,1024]{1,0:T(8,128)(2,1)}, bf16[64,1024]{1,0:T(8,128)(2,1)S(1)}, u32[]{:S(2)}, u32[]{:S(2)}) collective-permute-start(bf16[64,1024]{1,0:T(8,128)(2,1)} %get-tuple-element.22.refs_1_), channel_id=1, source_target_pairs={{0,8},{2,10},{4,12},{6,14},{8,0},{10,2},{12,4},{14,6},{1,9},{3,11}... | collective-permute-start | bytes 393224 | tf_op jit(solution)/shard_map/ppermute | solution.py:326
  8.6 0.6 collective-permute-done.refs_2_
  9.2 1.5 %collective-permute-start.2 = (bf16[64,1024]{1,0:T(8,128)(2,1)S(1)}, bf16[64,1024]{1,0:T(8,128)(2,1)S(1)}, u32[]{:S(2)}, u32[]{:S(2)}) collective-permute-start(bf16[64,1024]{1,0:T(8,128)(2,1)S(1)} %collective-permute-done.refs_2_), channel_id=1, source_target_pairs={{0,12},{2,14},{4,0},{6,2},{8,4},{10,6},{12,8},{14,10},{1,13},{3,15... | collective-permute-start | bytes 393224 | tf_op jit(solution)/shard_map/ppermute | solution.py:326
  10.7 1.9 %collective-permute-start.4 = (bf16[64,1024]{1,0:T(8,128)(2,1)S(1)}, bf16[64,1024]{1,0:T(8,128)(2,1)S(1)}, u32[]{:S(2)}, u32[]{:S(2)}) collective-permute-start(bf16[64,1024]{1,0:T(8,128)(2,1)S(1)} %collective-permute-done.refs_2_), channel_id=1, source_target_pairs={{0,8},{2,10},{4,12},{6,14},{8,0},{10,2},{12,4},{14,6},{1,9},{3,11}... | collective-permute-start | bytes 393224 | tf_op jit(solution)/shard_map/ppermute | solution.py:326
  12.6 5.4 %collective-permute-start.6 = (bf16[64,1024]{1,0:T(8,128)(2,1)S(1)}, bf16[64,1024]{1,0:T(8,128)(2,1)S(1)}, u32[]{:S(2)}, u32[]{:S(2)}) collective-permute-start(bf16[64,1024]{1,0:T(8,128)(2,1)S(1)} %collective-permute-done.refs_2_), channel_id=1, source_target_pairs={{0,4},{2,6},{4,8},{6,10},{8,12},{10,14},{12,0},{14,2},{1,5},{3,7},... | collective-permute-start | bytes 393224 | tf_op jit(solution)/shard_map/ppermute | solution.py:326
  18.1 2.8 %copy-done = bf16[1024,3072]{1,0:T(8,128)(2,1)S(1)} copy-done((bf16[1024,3072]{1,0:T(8,128)(2,1)S(1)}, bf16[1024,3072]{1,0:T(8,128)(2,1)}, u32[]{:S(2)}) %copy-start) | copy-done | bytes 6291480
  20.9 2.6 %shard_map.68.refs_10_.refs_1_ = bf16[8,1024,384]{2,1,0:T(8,128)(2,1)S(1)} custom-call(s32[5]{0:T(128)S(1)} %stack.23.meta_ref.refs_0_, bf16[1024,3072]{1,0:T(8,128)(2,1)S(1)} %copy-done, bf16[1024,3072]{1,0:T(8,128)(2,1)S(1)} %copy-done), custom_call_target="tpu_custom_call" | custom-call | bytes 12582912 | tf_op jit(solution)/shard_map/pallas_call | solution.py:75
  23.6 0.6 shard_map.70.refs_2_
  24.3 1.0 shard_map.71.refs_3_
  25.5 1.3 %shard_map.72.refs_3_ = bf16[2,272,384]{2,1,0:T(8,128)(2,1)S(1)} custom-call(s32[5]{0:T(128)S(1)} %stack.23.meta_ref.refs_0_, bf16[8,1024,384]{2,1,0:T(8,128)(2,1)S(1)} %shard_map.68.refs_10_.refs_1_, bf16[528,1024]{1,0:T(8,128)(2,1)S(1)} %shard_map.70.refs_2_, bf16[1,272,384]{2,1,0:T(8,128)(2,1)S(1)} %shard_map.71.refs_3_), custom_call_target="tpu_custom_call" | custom-call | flops 4000000000 | bytes 1 | tf_op jit(solution)/shard_map/pallas_call | solution.py:27
  26.7 2.0 %collective-permute-start.11 = (bf16[2,272,384]{2,1,0:T(8,128)(2,1)S(1)}, bf16[2,272,384]{2,1,0:T(8,128)(2,1)S(1)}, u32[]{:S(2)}, u32[]{:S(2)}) collective-permute-start(bf16[2,272,384]{2,1,0:T(8,128)(2,1)S(1)} %shard_map.72.refs_3_), channel_id=1, source_target_pairs={{0,128},{16,144},{32,160},{48,176},{64,192},{80,208},{96,224},{112... | collective-permute-start | bytes 1253384 | tf_op jit(solution)/shard_map/ppermute | solution.py:320
  28.8 1.3 %shard_map.73.refs_4_ = bf16[512,384]{1,0:T(8,128)(2,1)S(1)} custom-call(s32[5]{0:T(128)S(1)} %stack.23.meta_ref.refs_0_, bf16[8,1024,384]{2,1,0:T(8,128)(2,1)S(1)} %shard_map.68.refs_10_.refs_1_, bf16[528,1024]{1,0:T(8,128)(2,1)S(1)} %collective-permute-done.7.refs_2_.refs_3_, bf16[2,272,384]{2,1,0:T(8,128)(2,1)S(1)} %shard_map.72.refs_3_), custom_call_target="tpu_custom_call" | custom-call | flops 4000000000 | bytes 1 | tf_op jit(solution)/shard_map/pallas_call | solution.py:27
  30.0 5.9 %collective-permute-start.13 = (bf16[512,384]{1,0:T(8,128)(2,1)S(1)}, bf16[512,384]{1,0:T(8,128)(2,1)S(1)}, u32[]{:S(2)}, u32[]{:S(2)}) collective-permute-start(bf16[512,384]{1,0:T(8,128)(2,1)S(1)} %shard_map.73.refs_4_), channel_id=1, source_target_pairs={{0,112},{16,0},{32,16},{48,32},{64,48},{80,64},{96,80},{112,96},{1... | collective-permute-start | bytes 1179656 | tf_op jit(solution)/shard_map/ppermute | solution.py:314
  36.0 1.0 shard_map.74.refs_3_
  37.0 1.3 %shard_map.75.refs_3_ = bf16[2,272,384]{2,1,0:T(8,128)(2,1)S(1)} custom-call(s32[5]{0:T(128)S(1)} %stack.23.meta_ref.refs_0_, bf16[8,1024,384]{2,1,0:T(8,128)(2,1)S(1)} %shard_map.68.refs_10_.refs_1_, bf16[528,1024]{1,0:T(8,128)(2,1)S(1)} %shard_map.70.refs_2_, bf16[272,384]{1,0:T(8,128)(2,1)S(1)} %shard_map.74.refs_3_), custom_call_target="tpu_custom_call" | custom-call | flops 4000000000 | bytes 1 | tf_op jit(solution)/shard_map/pallas_call | solution.py:27
  38.3 0.3 collective-permute-start.12
  38.6 1.6 %shard_map.76.refs_4_ = bf16[3,272,384]{2,1,0:T(8,128)(2,1)S(1)} custom-call(s32[5]{0:T(128)S(1)} %stack.23.meta_ref.refs_0_, bf16[8,1024,384]{2,1,0:T(8,128)(2,1)S(1)} %shard_map.68.refs_10_.refs_1_, bf16[528,1024]{1,0:T(8,128)(2,1)S(1)} %shard_map.70.refs_2_, bf16[2,272,384]{2,1,0:T(8,128)(2,1)S(1)} %shard_map.75.refs_3_), custom_call_target="tpu_custom_call" | custom-call | flops 4000000000 | bytes 1 | tf_op jit(solution)/shard_map/pallas_call | solution.py:27
  40.2 4.3 %collective-permute-done.13.refs_3_ = bf16[512,384]{1,0:T(8,128)(2,1)S(1)} collective-permute-done((bf16[512,384]{1,0:T(8,128)(2,1)S(1)}, bf16[512,384]{1,0:T(8,128)(2,1)S(1)}, u32[]{:S(2)}, u32[]{:S(2)}) %collective-permute-start.13) | collective-permute-done | bytes 393248 | tf_op jit(solution)/shard_map/ppermute | solution.py:314
  44.5 1.8 %shard_map.77 = (bf16[512,384]{1,0:T(8,128)(2,1)S(1)}, bf16[512,384]{1,0:T(8,128)(2,1)S(1)}) custom-call(s32[5]{0:T(128)S(1)} %stack.23.meta_ref.refs_0_, bf16[8,1024,384]{2,1,0:T(8,128)(2,1)S(1)} %shard_map.68.refs_10_.refs_1_, bf16[528,1024]{1,0:T(8,128)(2,1)S(1)} %collective-permute-done.7.refs_2_.refs_3_, ...), custom_call_target="tpu_custom_call" | custom-call | flops 4000000000 | bytes 1 | tf_op jit(solution)/shard_map/pallas_call | solution.py:27
  46.3 3.8 %collective-permute-start.16 = (bf16[512,384]{1,0:T(8,128)(2,1)S(1)}, bf16[512,384]{1,0:T(8,128)(2,1)S(1)}, u32[]{:S(2)}, u32[]{:S(2)}) collective-permute-start(bf16[512,384]{1,0:T(8,128)(2,1)S(1)} %get-tuple-element.24.refs_5_), channel_id=1, source_target_pairs={{0,112},{16,0},{32,16},{48,32},{64,48},{80,64},{96,80},{112,96},{1... | collective-permute-start | bytes 1179656 | tf_op jit(solution)/shard_map/ppermute | solution.py:314
  50.0 0.3 collective-permute-start.10
  50.3 1.3 %shard_map.78 = (bf16[272,384]{1,0:T(8,128)(2,1)S(1)}, bf16[272,384]{1,0:T(8,128)(2,1)S(1)}) custom-call(s32[5]{0:T(128)S(1)} %stack.23.meta_ref.refs_0_, bf16[8,1024,384]{2,1,0:T(8,128)(2,1)S(1)} %shard_map.68.refs_10_.refs_1_, bf16[528,1024]{1,0:T(8,128)(2,1)S(1)} %shard_map.70.refs_2_, bf16[2,272,384]{2,1,0:T(8,128)(2,1)S(1)} %collective-permute-done.11.refs_3_, ...), custom_call_target="tpu_custom_call" | custom-call | flops 4000000000 | bytes 1 | tf_op jit(solution)/shard_map/pallas_call | solution.py:27
  51.7 3.3 %collective-permute-start.15 = (bf16[272,384]{1,0:T(8,128)(2,1)S(1)}, bf16[272,384]{1,0:T(8,128)(2,1)S(1)}, u32[]{:S(2)}, u32[]{:S(2)}) collective-permute-start(bf16[272,384]{1,0:T(8,128)(2,1)S(1)} %get-tuple-element.26), channel_id=1, source_target_pairs={{0,112},{16,0},{32,16},{48,32},{64,48},{80,64},{96,80},{112,96},{1... | collective-permute-start | bytes 626696 | tf_op jit(solution)/shard_map/ppermute | solution.py:314
  55.1 4.5 %collective-permute-done.16.refs_3_ = bf16[512,384]{1,0:T(8,128)(2,1)S(1)} collective-permute-done((bf16[512,384]{1,0:T(8,128)(2,1)S(1)}, bf16[512,384]{1,0:T(8,128)(2,1)S(1)}, u32[]{:S(2)}, u32[]{:S(2)}) %collective-permute-start.16) | collective-permute-done | bytes 393248 | tf_op jit(solution)/shard_map/ppermute | solution.py:314
  59.6 3.7 %collective-permute-done.17.refs_4_ = bf16[512,384]{1,0:T(8,128)(2,1)S(1)} collective-permute-done((bf16[512,384]{1,0:T(8,128)(2,1)S(1)}, bf16[512,384]{1,0:T(8,128)(2,1)S(1)}, u32[]{:S(2)}, u32[]{:S(2)}) %collective-permute-start.17) | collective-permute-done | bytes 393248 | tf_op jit(solution)/shard_map/ppermute | solution.py:314
  63.3 1.8 %shard_map.79 = (bf16[512,384]{1,0:T(8,128)(2,1)S(1)}, bf16[512,384]{1,0:T(8,128)(2,1)S(1)}) custom-call(s32[5]{0:T(128)S(1)} %stack.23.meta_ref.refs_0_, bf16[8,1024,384]{2,1,0:T(8,128)(2,1)S(1)} %shard_map.68.refs_10_.refs_1_, bf16[528,1024]{1,0:T(8,128)(2,1)S(1)} %collective-permute-done.7.refs_2_.refs_3_, ...), custom_call_target="tpu_custom_call" | custom-call | flops 4000000000 | bytes 1 | tf_op jit(solution)/shard_map/pallas_call | solution.py:27
  65.2 2.0 %collective-permute-start.21 = (bf16[512,384]{1,0:T(8,128)(2,1)S(1)}, bf16[512,384]{1,0:T(8,128)(2,1)S(1)}, u32[]{:S(2)}, u32[]{:S(2)}) collective-permute-start(bf16[512,384]{1,0:T(8,128)(2,1)S(1)} %get-tuple-element.31), channel_id=1, source_target_pairs={{0,16},{16,32},{32,48},{48,64},{64,80},{80,96},{96,112},{112,0},{1... | collective-permute-start | bytes 1179656 | tf_op jit(solution)/shard_map/ppermute | solution.py:314
  67.2 0.3 collective-permute-start.9
  67.5 1.3 %shard_map.80 = (bf16[272,384]{1,0:T(8,128)(2,1)S(1)}, bf16[272,384]{1,0:T(8,128)(2,1)S(1)}) custom-call(s32[5]{0:T(128)S(1)} %stack.23.meta_ref.refs_0_, bf16[8,1024,384]{2,1,0:T(8,128)(2,1)S(1)} %shard_map.68.refs_10_.refs_1_, bf16[528,1024]{1,0:T(8,128)(2,1)S(1)} %shard_map.70.refs_2_, bf16[2,272,384]{2,1,0:T(8,128)(2,1)S(1)} %collective-permute-done.10.refs_3_, ...), custom_call_target="tpu_custom_call" | custom-call | flops 4000000000 | bytes 1 | tf_op jit(solution)/shard_map/pallas_call | solution.py:27
  68.9 3.2 %collective-permute-start.19 = (bf16[272,384]{1,0:T(8,128)(2,1)S(1)}, bf16[272,384]{1,0:T(8,128)(2,1)S(1)}, u32[]{:S(2)}, u32[]{:S(2)}) collective-permute-start(bf16[272,384]{1,0:T(8,128)(2,1)S(1)} %get-tuple-element.30), channel_id=1, source_target_pairs={{0,112},{16,0},{32,16},{48,32},{64,48},{80,64},{96,80},{112,96},{1... | collective-permute-start | bytes 626696 | tf_op jit(solution)/shard_map/ppermute | solution.py:314
  72.1 1.9 %collective-permute-done.20.refs_3_ = bf16[512,384]{1,0:T(8,128)(2,1)S(1)} collective-permute-done((bf16[512,384]{1,0:T(8,128)(2,1)S(1)}, bf16[512,384]{1,0:T(8,128)(2,1)S(1)}, u32[]{:S(2)}, u32[]{:S(2)}) %collective-permute-start.20) | collective-permute-done | bytes 393248 | tf_op jit(solution)/shard_map/ppermute | solution.py:314
  74.1 2.5 %collective-permute-done.21.refs_4_ = bf16[512,384]{1,0:T(8,128)(2,1)S(1)} collective-permute-done((bf16[512,384]{1,0:T(8,128)(2,1)S(1)}, bf16[512,384]{1,0:T(8,128)(2,1)S(1)}, u32[]{:S(2)}, u32[]{:S(2)}) %collective-permute-start.21) | collective-permute-done | bytes 393248 | tf_op jit(solution)/shard_map/ppermute | solution.py:314
  76.5 1.8 %shard_map.81 = (bf16[512,384]{1,0:T(8,128)(2,1)S(1)}, bf16[512,384]{1,0:T(8,128)(2,1)S(1)}) custom-call(s32[5]{0:T(128)S(1)} %stack.23.meta_ref.refs_0_, bf16[8,1024,384]{2,1,0:T(8,128)(2,1)S(1)} %shard_map.68.refs_10_.refs_1_, bf16[528,1024]{1,0:T(8,128)(2,1)S(1)} %collective-permute-done.7.refs_2_.refs_3_, ...), custom_call_target="tpu_custom_call" | custom-call | flops 4000000000 | bytes 1 | tf_op jit(solution)/shard_map/pallas_call | solution.py:27
  78.3 0.6 collective-permute-start.24
  79.0 1.7 %collective-permute-start.25 = (bf16[512,384]{1,0:T(8,128)(2,1)S(1)}, bf16[512,384]{1,0:T(8,128)(2,1)S(1)}, u32[]{:S(2)}, u32[]{:S(2)}) collective-permute-start(bf16[512,384]{1,0:T(8,128)(2,1)S(1)} %get-tuple-element.35), channel_id=1, source_target_pairs={{0,16},{16,32},{32,48},{48,64},{64,80},{80,96},{96,112},{112,0},{1... | collective-permute-start | bytes 1179656 | tf_op jit(solution)/shard_map/ppermute | solution.py:314
  80.7 0.3 collective-permute-done.18.refs_4_
  81.0 1.3 %shard_map.82 = (bf16[272,384]{1,0:T(8,128)(2,1)S(1)}, bf16[272,384]{1,0:T(8,128)(2,1)S(1)}) custom-call(s32[5]{0:T(128)S(1)} %stack.23.meta_ref.refs_0_, bf16[8,1024,384]{2,1,0:T(8,128)(2,1)S(1)} %shard_map.68.refs_10_.refs_1_, bf16[528,1024]{1,0:T(8,128)(2,1)S(1)} %shard_map.70.refs_2_, bf16[3,272,384]{2,1,0:T(8,128)(2,1)S(1)} %collective-permute-done.9.refs_3_.refs_4_, ...), custom_call_target="tpu_custom_call" | custom-call | flops 4000000000 | bytes 1 | tf_op jit(solution)/shard_map/pallas_call | solution.py:27
  82.4 3.2 %collective-permute-start.23 = (bf16[272,384]{1,0:T(8,128)(2,1)S(1)}, bf16[272,384]{1,0:T(8,128)(2,1)S(1)}, u32[]{:S(2)}, u32[]{:S(2)}) collective-permute-start(bf16[272,384]{1,0:T(8,128)(2,1)S(1)} %get-tuple-element.34), channel_id=1, source_target_pairs={{0,112},{16,0},{32,16},{48,32},{64,48},{80,64},{96,80},{112,96},{1... | collective-permute-start | bytes 626696 | tf_op jit(solution)/shard_map/ppermute | solution.py:314
  85.7 5.7 %collective-permute-done.22.refs_5_ = bf16[272,384]{1,0:T(8,128)(2,1)S(1)} collective-permute-done((bf16[272,384]{1,0:T(8,128)(2,1)S(1)}, bf16[272,384]{1,0:T(8,128)(2,1)S(1)}, u32[]{:S(2)}, u32[]{:S(2)}) %collective-permute-start.22) | collective-permute-done | bytes 208928 | tf_op jit(solution)/shard_map/ppermute | solution.py:314
  91.3 1.8 %shard_map.83 = (f32[192,128]{1,0:T(8,128)S(1)}, f32[192,256]{1,0:T(8,128)S(1)}, f32[8,192]{1,0:T(8,128)S(1)}, bf16[192,512]{1,0:T(8,128)(2,1)S(1)}, bf16[208,51...) custom-call(s32[5]{0:T(128)S(1)} %stack.23.meta_ref.refs_0_, bf16[8,1024,384]{2,1,0:T(8,128)(2,1)S(1)} %shard_map.68.refs_10_.refs_1_, ...), custom_call_target="tpu_custom_call" | custom-call | flops 4000000000 | bytes 1 | tf_op jit(solution)/shard_map/pallas_call | solution.py:27
  93.4 0.5 collective-permute-start.26
  93.9 4.0 %collective-permute-start.28 = (bf16[192,512]{1,0:T(8,128)(2,1)S(1)}, bf16[192,512]{1,0:T(8,128)(2,1)S(1)}, u32[]{:S(2)}, u32[]{:S(2)}) collective-permute-start(bf16[192,512]{1,0:T(8,128)(2,1)S(1)} %get-tuple-element.41), channel_id=1, source_target_pairs={{0,1},{1,0},{2,3},{3,2},{4,5},{5,4},{6,7},{7,6},{8,9},{9,8},{10,11... | collective-permute-start | bytes 589832 | tf_op jit(solution)/shard_map/ppermute | solution.py:336
  97.9 1.1 %collective-permute-done.26.refs_4_ = bf16[192,512]{1,0:T(8,128)(2,1)S(1)} collective-permute-done((bf16[192,512]{1,0:T(8,128)(2,1)S(1)}, bf16[192,512]{1,0:T(8,128)(2,1)S(1)}, u32[]{:S(2)}, u32[]{:S(2)}) %collective-permute-start.26) | collective-permute-done | bytes 196640 | tf_op jit(solution)/shard_map/ppermute | solution.py:320
  99.1 4.6 %collective-permute-done.28.refs_6_ = bf16[192,512]{1,0:T(8,128)(2,1)S(1)} collective-permute-done((bf16[192,512]{1,0:T(8,128)(2,1)S(1)}, bf16[192,512]{1,0:T(8,128)(2,1)S(1)}, u32[]{:S(2)}, u32[]{:S(2)}) %collective-permute-start.28) | collective-permute-done | bytes 196640 | tf_op jit(solution)/shard_map/ppermute | solution.py:336
  103.7 1.7 %shard_map.84 = (f32[1,2,192,512]{3,2,1,0:T(8,128)}, f32[1,2,192]{2,1,0:T(2,128)}) custom-call(s32[5]{0:T(128)S(1)} %stack.23.meta_ref.refs_0_, f32[192,128]{1,0:T(8,128)S(1)} %get-tuple-element.36.refs_1_, f32[192,256]{1,0:T(8,128)S(1)} %get-tuple-element.37.refs_2_, f32[8,192]{1,0:T(8,128)S(1)} %get-tuple-element.38.refs_3_, ...), custom_call_target="tpu_custom_call" | custom-call | flops 4000000000 | bytes 1 | tf_op jit(solution)/shard_map/pallas_call | solution.py:27
  (34 shorter events, 1.0 us)
Async XLA Ops:
  2.3 7.0 %collective-permute-start = (bf16[64,1024]{1,0:T(8,128)(2,1)}, bf16[64,1024]{1,0:T(8,128)(2,1)S(1)}, u32[]{:S(2)}, u32[]{:S(2)}) collective-permute-start(bf16[64,1024]{1,0:T(8,128)(2,1)} %get-tuple-element.22.refs_1_), channel_id=1, source_target_pairs={{0,1},{1,0},{2,3},{3,2},{4,5},{5,4},{6,7},{7,6},{8,9},{9,8},{10,11... | collective-permute-start | bytes 393224 | tf_op jit(solution)/shard_map/ppermute | solution.py:336
  5.3 7.3 %collective-permute-start.1 = (bf16[64,1024]{1,0:T(8,128)(2,1)}, bf16[64,1024]{1,0:T(8,128)(2,1)S(1)}, u32[]{:S(2)}, u32[]{:S(2)}) collective-permute-start(bf16[64,1024]{1,0:T(8,128)(2,1)} %get-tuple-element.22.refs_1_), channel_id=1, source_target_pairs={{0,12},{2,14},{4,0},{6,2},{8,4},{10,6},{12,8},{14,10},{1,13},{3,15... | collective-permute-start | bytes 393224 | tf_op jit(solution)/shard_map/ppermute | solution.py:326
  5.7 17.8 %collective-permute-start.3 = (bf16[64,1024]{1,0:T(8,128)(2,1)}, bf16[64,1024]{1,0:T(8,128)(2,1)S(1)}, u32[]{:S(2)}, u32[]{:S(2)}) collective-permute-start(bf16[64,1024]{1,0:T(8,128)(2,1)} %get-tuple-element.22.refs_1_), channel_id=1, source_target_pairs={{0,8},{2,10},{4,12},{6,14},{8,0},{10,2},{12,4},{14,6},{1,9},{3,11}... | collective-permute-start | bytes 393224 | tf_op jit(solution)/shard_map/ppermute | solution.py:326
  8.6 14.9 %collective-permute-start.5 = (bf16[64,1024]{1,0:T(8,128)(2,1)}, bf16[64,1024]{1,0:T(8,128)(2,1)S(1)}, u32[]{:S(2)}, u32[]{:S(2)}) collective-permute-start(bf16[64,1024]{1,0:T(8,128)(2,1)} %get-tuple-element.22.refs_1_), channel_id=1, source_target_pairs={{0,4},{2,6},{4,8},{6,10},{8,12},{10,14},{12,0},{14,2},{1,5},{3,7},... | collective-permute-start | bytes 393224 | tf_op jit(solution)/shard_map/ppermute | solution.py:326
  9.2 14.3 %collective-permute-start.2 = (bf16[64,1024]{1,0:T(8,128)(2,1)S(1)}, bf16[64,1024]{1,0:T(8,128)(2,1)S(1)}, u32[]{:S(2)}, u32[]{:S(2)}) collective-permute-start(bf16[64,1024]{1,0:T(8,128)(2,1)S(1)} %collective-permute-done.refs_2_), channel_id=1, source_target_pairs={{0,12},{2,14},{4,0},{6,2},{8,4},{10,6},{12,8},{14,10},{1,13},{3,15... | collective-permute-start | bytes 393224 | tf_op jit(solution)/shard_map/ppermute | solution.py:326
  10.7 12.9 %collective-permute-start.4 = (bf16[64,1024]{1,0:T(8,128)(2,1)S(1)}, bf16[64,1024]{1,0:T(8,128)(2,1)S(1)}, u32[]{:S(2)}, u32[]{:S(2)}) collective-permute-start(bf16[64,1024]{1,0:T(8,128)(2,1)S(1)} %collective-permute-done.refs_2_), channel_id=1, source_target_pairs={{0,8},{2,10},{4,12},{6,14},{8,0},{10,2},{12,4},{14,6},{1,9},{3,11}... | collective-permute-start | bytes 393224 | tf_op jit(solution)/shard_map/ppermute | solution.py:326
  12.6 11.0 %collective-permute-start.6 = (bf16[64,1024]{1,0:T(8,128)(2,1)S(1)}, bf16[64,1024]{1,0:T(8,128)(2,1)S(1)}, u32[]{:S(2)}, u32[]{:S(2)}) collective-permute-start(bf16[64,1024]{1,0:T(8,128)(2,1)S(1)} %collective-permute-done.refs_2_), channel_id=1, source_target_pairs={{0,4},{2,6},{4,8},{6,10},{8,12},{10,14},{12,0},{14,2},{1,5},{3,7},... | collective-permute-start | bytes 393224 | tf_op jit(solution)/shard_map/ppermute | solution.py:326
  18.1 2.8 %copy-start = (bf16[1024,3072]{1,0:T(8,128)(2,1)S(1)}, bf16[1024,3072]{1,0:T(8,128)(2,1)}, u32[]{:S(2)}) copy-start(bf16[1024,3072]{1,0:T(8,128)(2,1)} %second_ref.1) | copy-start | bytes 18874372
  20.9 2.7 %copy-start.1 = (bf16[64,1024]{1,0:T(8,128)(2,1)S(1)}, bf16[64,1024]{1,0:T(8,128)(2,1)}, u32[]{:S(2)}) copy-start(bf16[64,1024]{1,0:T(8,128)(2,1)} %get-tuple-element.22.refs_1_) | copy-start | bytes 393220
  20.9 2.7 %copy-start.2 = (bf16[16,1024]{1,0:T(8,128)(2,1)S(1)}, bf16[16,1024]{1,0:T(8,128)(2,1)}, u32[]{:S(2)}) copy-start(bf16[16,1024]{1,0:T(8,128)(2,1)} %get-tuple-element.23.refs_9_) | copy-start | bytes 98308
  24.2 4.6 %collective-permute-start.7 = (bf16[528,1024]{1,0:T(8,128)(2,1)S(1)}, bf16[528,1024]{1,0:T(8,128)(2,1)S(1)}, u32[]{:S(2)}, u32[]{:S(2)}) collective-permute-start(bf16[528,1024]{1,0:T(8,128)(2,1)S(1)} %shard_map.70.refs_2_), channel_id=1, source_target_pairs={{0,2},{2,0},{4,6},{6,4},{8,10},{10,8},{12,14},{14,12},{1,3},{3,1},... | collective-permute-start | bytes 3244040 | tf_op jit(solution)/shard_map/ppermute | solution.py:332
  25.3 10.7 %collective-permute-start.8 = (bf16[1,272,384]{2,1,0:T(8,128)(2,1)S(1)}, bf16[1,272,384]{2,1,0:T(8,128)(2,1)S(1)}, u32[]{:S(2)}, u32[]{:S(2)}) collective-permute-start(bf16[1,272,384]{2,1,0:T(8,128)(2,1)S(1)} %shard_map.71.refs_3_), channel_id=1, source_target_pairs={{0,128},{16,144},{32,160},{48,176},{64,192},{80,208},{96,224},{112... | collective-permute-start | bytes 626696 | tf_op jit(solution)/shard_map/ppermute | solution.py:320
  26.7 23.6 %collective-permute-start.11 = (bf16[2,272,384]{2,1,0:T(8,128)(2,1)S(1)}, bf16[2,272,384]{2,1,0:T(8,128)(2,1)S(1)}, u32[]{:S(2)}, u32[]{:S(2)}) collective-permute-start(bf16[2,272,384]{2,1,0:T(8,128)(2,1)S(1)} %shard_map.72.refs_3_), channel_id=1, source_target_pairs={{0,128},{16,144},{32,160},{48,176},{64,192},{80,208},{96,224},{112... | collective-permute-start | bytes 1253384 | tf_op jit(solution)/shard_map/ppermute | solution.py:320
  30.0 14.4 %collective-permute-start.13 = (bf16[512,384]{1,0:T(8,128)(2,1)S(1)}, bf16[512,384]{1,0:T(8,128)(2,1)S(1)}, u32[]{:S(2)}, u32[]{:S(2)}) collective-permute-start(bf16[512,384]{1,0:T(8,128)(2,1)S(1)} %shard_map.73.refs_4_), channel_id=1, source_target_pairs={{0,112},{16,0},{32,16},{48,32},{64,48},{80,64},{96,80},{112,96},{1... | collective-permute-start | bytes 1179656 | tf_op jit(solution)/shard_map/ppermute | solution.py:314
  38.3 12.0 %collective-permute-start.12 = (bf16[272,384]{1,0:T(8,128)(2,1)S(1)}, bf16[272,384]{1,0:T(8,128)(2,1)S(1)}, u32[]{:S(2)}, u32[]{:S(2)}) collective-permute-start(bf16[272,384]{1,0:T(8,128)(2,1)S(1)} %shard_map.74.refs_3_), channel_id=1, source_target_pairs={{0,16},{16,32},{32,48},{48,64},{64,80},{80,96},{96,112},{112,0},{1... | collective-permute-start | bytes 626696 | tf_op jit(solution)/shard_map/ppermute | solution.py:314
  46.3 13.3 %collective-permute-start.16 = (bf16[512,384]{1,0:T(8,128)(2,1)S(1)}, bf16[512,384]{1,0:T(8,128)(2,1)S(1)}, u32[]{:S(2)}, u32[]{:S(2)}) collective-permute-start(bf16[512,384]{1,0:T(8,128)(2,1)S(1)} %get-tuple-element.24.refs_5_), channel_id=1, source_target_pairs={{0,112},{16,0},{32,16},{48,32},{64,48},{80,64},{96,80},{112,96},{1... | collective-permute-start | bytes 1179656 | tf_op jit(solution)/shard_map/ppermute | solution.py:314
  50.0 13.3 %collective-permute-start.17 = (bf16[512,384]{1,0:T(8,128)(2,1)S(1)}, bf16[512,384]{1,0:T(8,128)(2,1)S(1)}, u32[]{:S(2)}, u32[]{:S(2)}) collective-permute-start(bf16[512,384]{1,0:T(8,128)(2,1)S(1)} %get-tuple-element.27), channel_id=1, source_target_pairs={{0,16},{16,32},{32,48},{48,64},{64,80},{80,96},{96,112},{112,0},{1... | collective-permute-start | bytes 1179656 | tf_op jit(solution)/shard_map/ppermute | solution.py:314
  50.0 17.2 %collective-permute-start.10 = (bf16[2,272,384]{2,1,0:T(8,128)(2,1)S(1)}, bf16[2,272,384]{2,1,0:T(8,128)(2,1)S(1)}, u32[]{:S(2)}, u32[]{:S(2)}) collective-permute-start(bf16[2,272,384]{2,1,0:T(8,128)(2,1)S(1)} %shard_map.75.refs_3_), channel_id=1, source_target_pairs={{0,128},{16,144},{32,160},{48,176},{64,192},{80,208},{96,224},{112... | collective-permute-start | bytes 1253384 | tf_op jit(solution)/shard_map/ppermute | solution.py:320
  51.7 15.8 %collective-permute-start.14 = (bf16[272,384]{1,0:T(8,128)(2,1)S(1)}, bf16[272,384]{1,0:T(8,128)(2,1)S(1)}, u32[]{:S(2)}, u32[]{:S(2)}) collective-permute-start(bf16[272,384]{1,0:T(8,128)(2,1)S(1)} %get-tuple-element.25.refs_5_), channel_id=1, source_target_pairs={{0,16},{16,32},{32,48},{48,64},{64,80},{80,96},{96,112},{112,0},{1... | collective-permute-start | bytes 626696 | tf_op jit(solution)/shard_map/ppermute | solution.py:314
  51.7 15.8 %collective-permute-start.15 = (bf16[272,384]{1,0:T(8,128)(2,1)S(1)}, bf16[272,384]{1,0:T(8,128)(2,1)S(1)}, u32[]{:S(2)}, u32[]{:S(2)}) collective-permute-start(bf16[272,384]{1,0:T(8,128)(2,1)S(1)} %get-tuple-element.26), channel_id=1, source_target_pairs={{0,112},{16,0},{32,16},{48,32},{64,48},{80,64},{96,80},{112,96},{1... | collective-permute-start | bytes 626696 | tf_op jit(solution)/shard_map/ppermute | solution.py:314
  65.1 9.0 %collective-permute-start.20 = (bf16[512,384]{1,0:T(8,128)(2,1)S(1)}, bf16[512,384]{1,0:T(8,128)(2,1)S(1)}, u32[]{:S(2)}, u32[]{:S(2)}) collective-permute-start(bf16[512,384]{1,0:T(8,128)(2,1)S(1)} %get-tuple-element.28.refs_6_), channel_id=1, source_target_pairs={{0,112},{16,0},{32,16},{48,32},{64,48},{80,64},{96,80},{112,96},{1... | collective-permute-start | bytes 1179656 | tf_op jit(solution)/shard_map/ppermute | solution.py:314
  65.2 11.4 %collective-permute-start.21 = (bf16[512,384]{1,0:T(8,128)(2,1)S(1)}, bf16[512,384]{1,0:T(8,128)(2,1)S(1)}, u32[]{:S(2)}, u32[]{:S(2)}) collective-permute-start(bf16[512,384]{1,0:T(8,128)(2,1)S(1)} %get-tuple-element.31), channel_id=1, source_target_pairs={{0,16},{16,32},{32,48},{48,64},{64,80},{80,96},{96,112},{112,0},{1... | collective-permute-start | bytes 1179656 | tf_op jit(solution)/shard_map/ppermute | solution.py:314
  67.2 13.5 %collective-permute-start.9 = (bf16[3,272,384]{2,1,0:T(8,128)(2,1)S(1)}, bf16[3,272,384]{2,1,0:T(8,128)(2,1)S(1)}, u32[]{:S(2)}, u32[]{:S(2)}) collective-permute-start(bf16[3,272,384]{2,1,0:T(8,128)(2,1)S(1)} %shard_map.76.refs_4_), channel_id=1, source_target_pairs={{0,128},{16,144},{32,160},{48,176},{64,192},{80,208},{96,224},{112... | collective-permute-start | bytes 1880072 | tf_op jit(solution)/shard_map/ppermute | solution.py:320
  68.8 12.2 %collective-permute-start.18 = (bf16[272,384]{1,0:T(8,128)(2,1)S(1)}, bf16[272,384]{1,0:T(8,128)(2,1)S(1)}, u32[]{:S(2)}, u32[]{:S(2)}) collective-permute-start(bf16[272,384]{1,0:T(8,128)(2,1)S(1)} %get-tuple-element.29.refs_5_), channel_id=1, source_target_pairs={{0,16},{16,32},{32,48},{48,64},{64,80},{80,96},{96,112},{112,0},{1... | collective-permute-start | bytes 626696 | tf_op jit(solution)/shard_map/ppermute | solution.py:314
  68.9 12.1 %collective-permute-start.19 = (bf16[272,384]{1,0:T(8,128)(2,1)S(1)}, bf16[272,384]{1,0:T(8,128)(2,1)S(1)}, u32[]{:S(2)}, u32[]{:S(2)}) collective-permute-start(bf16[272,384]{1,0:T(8,128)(2,1)S(1)} %get-tuple-element.30), channel_id=1, source_target_pairs={{0,112},{16,0},{32,16},{48,32},{64,48},{80,64},{96,80},{112,96},{1... | collective-permute-start | bytes 626696 | tf_op jit(solution)/shard_map/ppermute | solution.py:314
  78.3 13.0 %collective-permute-start.24 = (bf16[512,384]{1,0:T(8,128)(2,1)S(1)}, bf16[512,384]{1,0:T(8,128)(2,1)S(1)}, u32[]{:S(2)}, u32[]{:S(2)}) collective-permute-start(bf16[512,384]{1,0:T(8,128)(2,1)S(1)} %get-tuple-element.32.refs_6_), channel_id=1, source_target_pairs={{0,112},{16,0},{32,16},{48,32},{64,48},{80,64},{96,80},{112,96},{1... | collective-permute-start | bytes 1179656 | tf_op jit(solution)/shard_map/ppermute | solution.py:314
  79.0 12.4 %collective-permute-start.25 = (bf16[512,384]{1,0:T(8,128)(2,1)S(1)}, bf16[512,384]{1,0:T(8,128)(2,1)S(1)}, u32[]{:S(2)}, u32[]{:S(2)}) collective-permute-start(bf16[512,384]{1,0:T(8,128)(2,1)S(1)} %get-tuple-element.35), channel_id=1, source_target_pairs={{0,16},{16,32},{32,48},{48,64},{64,80},{80,96},{96,112},{112,0},{1... | collective-permute-start | bytes 1179656 | tf_op jit(solution)/shard_map/ppermute | solution.py:314
  82.3 9.0 %collective-permute-start.22 = (bf16[272,384]{1,0:T(8,128)(2,1)S(1)}, bf16[272,384]{1,0:T(8,128)(2,1)S(1)}, u32[]{:S(2)}, u32[]{:S(2)}) collective-permute-start(bf16[272,384]{1,0:T(8,128)(2,1)S(1)} %get-tuple-element.33.refs_9_), channel_id=1, source_target_pairs={{0,16},{16,32},{32,48},{48,64},{64,80},{80,96},{96,112},{112,0},{1... | collective-permute-start | bytes 626696 | tf_op jit(solution)/shard_map/ppermute | solution.py:314
  82.4 8.9 %collective-permute-start.23 = (bf16[272,384]{1,0:T(8,128)(2,1)S(1)}, bf16[272,384]{1,0:T(8,128)(2,1)S(1)}, u32[]{:S(2)}, u32[]{:S(2)}) collective-permute-start(bf16[272,384]{1,0:T(8,128)(2,1)S(1)} %get-tuple-element.34), channel_id=1, source_target_pairs={{0,112},{16,0},{32,16},{48,32},{64,48},{80,64},{96,80},{112,96},{1... | collective-permute-start | bytes 626696 | tf_op jit(solution)/shard_map/ppermute | solution.py:314
  93.2 10.5 %collective-permute-start.27 = (bf16[208,512]{1,0:T(8,128)(2,1)S(1)}, bf16[208,512]{1,0:T(8,128)(2,1)S(1)}, u32[]{:S(2)}, u32[]{:S(2)}) collective-permute-start(bf16[208,512]{1,0:T(8,128)(2,1)S(1)} %get-tuple-element.40), channel_id=1, source_target_pairs={{0,129},{1,128},{16,145},{17,144},{32,161},{33,160},{48,177},{49,1... | collective-permute-start | bytes 638984 | tf_op jit(solution)/shard_map/ppermute | solution.py:345
  93.4 5.7 %collective-permute-start.26 = (bf16[192,512]{1,0:T(8,128)(2,1)S(1)}, bf16[192,512]{1,0:T(8,128)(2,1)S(1)}, u32[]{:S(2)}, u32[]{:S(2)}) collective-permute-start(bf16[192,512]{1,0:T(8,128)(2,1)S(1)} %get-tuple-element.39), channel_id=1, source_target_pairs={{0,128},{16,144},{32,160},{48,176},{64,192},{80,208},{96,224},{112... | collective-permute-start | bytes 589832 | tf_op jit(solution)/shard_map/ppermute | solution.py:320
  93.9 9.8 %collective-permute-start.28 = (bf16[192,512]{1,0:T(8,128)(2,1)S(1)}, bf16[192,512]{1,0:T(8,128)(2,1)S(1)}, u32[]{:S(2)}, u32[]{:S(2)}) collective-permute-start(bf16[192,512]{1,0:T(8,128)(2,1)S(1)} %get-tuple-element.41), channel_id=1, source_target_pairs={{0,1},{1,0},{2,3},{3,2},{4,5},{5,4},{6,7},{7,6},{8,9},{9,8},{10,11... | collective-permute-start | bytes 589832 | tf_op jit(solution)/shard_map/ppermute | solution.py:336

commit v3 on v2

--- a/solution.py
+++ b/solution.py
@@ -27,7 +27,7 @@
     return pl.pallas_call(
         body,
         out_shape=out_shape,
-        in_specs=[IN_SMEM] + [IN_VMEM] * (n - 1 + extra),
+        in_specs=[IN_VMEM] * (n + extra),
         out_specs=[IN_VMEM] * len(out_shape),
         scratch_shapes=list(scratch),
         compiler_params=pltpu.CompilerParams(vmem_limit_bytes=16 * 2**20),
@@ -35,33 +35,34 @@
     )(*args, *after)
 
 
-def weigh_kernel(sigma_ref, panel_ref, obs_ref, ids_ref, panel_out, obs_out):
+def weigh_kernel(sigma_ref, obs_ref, ids_ref, weights_out, obs_out):
     ids = ids_ref[...]
     sigma = jnp.full(ids.shape, sigma_ref[0], F32)
     for g in range(1, sigma_ref.shape[0]):
         sigma = jnp.where(ids == g, sigma_ref[g], sigma)
     weights = 1.0 / (sigma * sigma)
-    panel_out[...] = (weights * panel_ref[...].astype(F32)).astype(BF16)
+    weights_out[...] = jnp.broadcast_to(weights, weights_out.shape)
     weighted = (weights * obs_ref[...]).astype(BF16)
     obs_out[...] = jnp.broadcast_to(weighted, obs_out.shape)
 
 
-def weigh(panel_t, observations, group_ids, group_sigma):
-    cols, points = panel_t.shape
+def weigh(observations, group_ids, group_sigma):
+    points = observations.shape[0]
     flat = pl.BlockSpec((1, points), lambda i: (0, 0))
     return pl.pallas_call(
         weigh_kernel,
         grid=(1,),
         out_shape=(
-            jax.ShapeDtypeStruct((cols, points), BF16),
+            jax.ShapeDtypeStruct((8, points), F32),
             jax.ShapeDtypeStruct((TAIL, points), BF16),
         ),
-        in_specs=[IN_SMEM, pl.BlockSpec((cols, points), lambda i: (0, 0)), flat, flat],
+        in_specs=[IN_SMEM, flat, flat],
         out_specs=[IN_VMEM, IN_VMEM],
-    )(group_sigma, panel_t, observations.reshape(1, -1), group_ids.reshape(1, -1))
-
-
-def pair_kernel(meta_ref, first_ref, second_ref, out_ref):
+        compiler_params=pltpu.CompilerParams(vmem_limit_bytes=2 * 2**20),
+    )(group_sigma, observations.reshape(1, -1), group_ids.reshape(1, -1))
+
+
+def pair_kernel(first_ref, second_ref, out_ref):
     e = pl.program_id(0)
     for half in range(2):
         lanes = slice(half * ROWS, (half + 1) * ROWS)
@@ -70,14 +71,13 @@
         )
 
 
-def pair_up(meta, design_rows):
+def pair_up(design_rows):
     points = design_rows.shape[0]
     return pl.pallas_call(
         pair_kernel,
         grid=(NZ // 2,),
         out_shape=jax.ShapeDtypeStruct((NZ, points, PAIR), BF16),
         in_specs=[
-            IN_SMEM,
             pl.BlockSpec((points, PAIR), lambda e: (0, e)),
             pl.BlockSpec((points, PAIR), lambda e: (0, e + NZ // 2)),
         ],
@@ -86,22 +86,25 @@
         cost_estimate=pl.CostEstimate(
             flops=0, bytes_accessed=4 * design_rows.size, transcendentals=0
         ),
-    )(meta, design_rows, design_rows)
-
-
-def collect_kernel(meta_ref, *refs):
-    at = 0
+    )(design_rows, design_rows)
+
+
+def collect_kernel(weights_ref, obs_ref, *refs):
+    weights = weights_ref[:1, :]
+    out, at = refs[-1], 0
     for ref in refs[:-1]:
-        refs[-1][at : at + ref.shape[0], :] = ref[...]
+        value = weights * ref[...].astype(F32)
+        out[at : at + ref.shape[0], :] = value.astype(BF16)
         at += ref.shape[0]
-
-
-def collect(meta, blocks, after):
-    rows = sum(b.shape[0] for b in blocks)
+    out[at:, :] = obs_ref[...]
+
+
+def collect(weights, weighted_obs, blocks, after):
+    rows = sum(b.shape[0] for b in blocks) + weighted_obs.shape[0]
     return call(
         collect_kernel,
-        [jax.ShapeDtypeStruct((rows, blocks[0].shape[1]), BF16)],
-        (meta, *blocks),
+        [jax.ShapeDtypeStruct((rows, weights.shape[1]), BF16)],
+        (weights, weighted_obs, *blocks),
         after,
         cost=1e9,
     )[0]
@@ -132,8 +135,12 @@
     return jnp.concatenate([total[:-TAIL], high, low], axis=0).astype(BF16)
 
 
-def place(meta_ref, dz):
-    return (meta_ref[0] + dz) & (NZ - 1)
+def place(dz):
+    return (lax.axis_index("rep") + dz) & (NZ - 1)
+
+
+def x_place():
+    return lax.axis_index("rep") >> 3
 
 
 def x_rows(panel_ref, which):
@@ -141,46 +148,66 @@
     return jnp.concatenate([panel_ref[pl.ds(at, PART), :], panel_ref[HALF:, :]], axis=0)
 
 
-def z_kernel(steps, meta_ref, rows_ref, panel_ref, *refs):
+def z_first_kernel(rows_ref, panel_ref, down, up):
+    total = product(panel_ref[:HALF, :], rows_ref[place(NZ // 2)]).astype(BF16)
+    down[...] = total[: HALF // 2]
+    up[...] = total[HALF // 2 :]
+
+
+def z_first(rows, panel, after):
+    return call(
+        z_first_kernel,
+        [jax.ShapeDtypeStruct((HALF // 2, PAIR), BF16)] * 2,
+        (rows, panel),
+        after,
+    )
+
+
+def z_kernel(steps, rows_ref, panel_ref, *refs):
     received, outs = refs[: -len(steps)], refs[-len(steps) :]
     left = panel_ref[:HALF, :]
     for i, dz in enumerate(steps):
-        total = product(left, rows_ref[place(meta_ref, dz)])
-        if i < len(received):
+        total = product(left, rows_ref[place(dz)])
+        count = received[i].shape[0]
+        if count == HALF:
             total = plus(total, received[i])
+        elif dz < 0:
+            total = jnp.concatenate([plus(total[:count], received[i]), total[count:]], axis=0)
+        else:
+            total = jnp.concatenate([total[:-count], plus(total[-count:], received[i])], axis=0)
         outs[i][...] = total.astype(BF16)
 
 
-def z_step(meta, rows, panel, steps, received, after):
+def z_step(rows, panel, steps, received, after):
     return call(
         functools.partial(z_kernel, steps),
         [jax.ShapeDtypeStruct((HALF, PAIR), BF16)] * len(steps),
-        (meta, rows, panel, *received),
-        after,
-    )
-
-
-def over_kernel(steps, meta_ref, rows_ref, panel_ref, out_ref):
-    left = x_rows(panel_ref, 1 - meta_ref[1])
+        (rows, panel, *received),
+        after,
+    )
+
+
+def over_kernel(steps, rows_ref, panel_ref, out_ref):
+    left = x_rows(panel_ref, 1 - x_place())
     for i, dz in enumerate(steps):
-        out_ref[i] = packed(product(left, rows_ref[place(meta_ref, dz)]))
-
-
-def over_x(meta, rows, panel, steps, after):
+        out_ref[i] = packed(product(left, rows_ref[place(dz)]))
+
+
+def over_x(rows, panel, steps, after):
     return call(
         functools.partial(over_kernel, steps),
         [jax.ShapeDtypeStruct((len(steps), PART + TAIL, PAIR), BF16)],
-        (meta, rows, panel),
-        after,
-    )
-
-
-def x_kernel(steps, picks, n_over, meta_ref, rows_ref, panel_ref, *refs):
+        (rows, panel),
+        after,
+    )
+
+
+def x_kernel(steps, picks, n_over, rows_ref, panel_ref, *refs):
     over, refs = refs[:n_over], refs[n_over:]
     received, outs = refs[: -len(steps)], refs[-len(steps) :]
-    left = x_rows(panel_ref, meta_ref[1])
+    left = x_rows(panel_ref, x_place())
     for i, dz in enumerate(steps):
-        total = product(left, rows_ref[place(meta_ref, dz)])
+        total = product(left, rows_ref[place(dz)])
         which, at = picks[i]
         total = plus_tailed(total, over[which].at[at])
         if i < len(received):
@@ -188,7 +215,7 @@
         outs[i][...] = packed(total)
 
 
-def x_step(meta, rows, panel, steps, over, received, after):
+def x_step(rows, panel, steps, over, received, after):
     arrays, picks = [], []
     for dz in steps:
         array, at = over[dz]
@@ -200,7 +227,7 @@
     return call(
         functools.partial(x_kernel, steps, tuple(picks), len(arrays)),
         [jax.ShapeDtypeStruct((PART + TAIL, PAIR), BF16)] * len(steps),
-        (meta, rows, panel, *arrays, *received),
+        (rows, panel, *arrays, *received),
         after,
     )
 
@@ -214,11 +241,11 @@
 
 
 def last_kernel(
-    at, meta_ref, rows_ref, near_ref, other_ref, over, x_up, x_down, z_down, z_up,
+    at, rows_ref, near_ref, other_ref, over, x_up, x_down, z_down, z_up,
     own_x, own_z, rhs, beside, cross, across, x_this, x_that, z_this, z_that,
 ):
-    side = meta_ref[1]
-    right = rows_ref[meta_ref[0]]
+    side = x_place()
+    right = rows_ref[place(0)]
     total = product(x_rows(near_ref, side), right)
     total = plus_tailed(plus_tailed(plus_tailed(total, over.at[at]), x_up), x_down)
     x_this[...], x_that[...] = halves(total[:PART])
@@ -244,7 +271,7 @@
     cross[ROWS:, :] = jnp.concatenate([sent, zeros], axis=1).astype(BF16)
 
 
-def last(meta, rows, near, other, over, x_got, z_got, after):
+def last(rows, near, other, over, x_got, z_got, after):
     array, at = over
     message = jax.ShapeDtypeStruct((ROWS, HALF), BF16)
     return call(
@@ -257,7 +284,7 @@
             jax.ShapeDtypeStruct((ROWS + TAIL, HALF), BF16),
             message,
         ],
-        (meta, rows, near, other, array, *x_got, *z_got),
+        (rows, near, other, array, *x_got, *z_got),
         after,
         scratch=[pltpu.VMEM((PAIR, n), F32) for n in (PART // 2, PART // 2, PART, PART)],
     )
@@ -270,9 +297,10 @@
 
 
 def finish_kernel(
-    meta_ref, own_x, own_z, rhs_ref, beside_ref, cross_ref, across_ref, out_ref, rhs_out
+    own_x, own_z, rhs_ref, beside_ref, cross_ref, across_ref, out_ref, rhs_out
 ):
-    side, y, core, half = meta_ref[1], meta_ref[2], meta_ref[3], meta_ref[4]
+    side, row, half = x_place(), lax.axis_index("row"), lax.axis_index("col")
+    y, core = row >> 1, row & 1
     (beside_x, beside_z), (cross_x, cross_z), (across_x, across_z) = (
         parts(r) for r in (beside_ref, cross_ref, across_ref)
     )
@@ -299,14 +327,14 @@
     )
 
 
-def finish(meta, *args):
+def finish(*args):
     return call(
         finish_kernel,
         [
             jax.ShapeDtypeStruct((1, 2, ROWS, HALF), F32),
             jax.ShapeDtypeStruct((1, 2, ROWS), F32),
         ],
-        (meta, *args),
+        args,
     )
 
 
@@ -346,12 +374,10 @@
 
 
 def per_device(design_rows, design_panel, observations, group_ids, group_sigma):
-    rep, row, half = (lax.axis_index(n) for n in ("rep", "row", "col"))
-    meta = jnp.stack([rep & (NZ - 1), rep >> 3, row >> 1, row & 1, half]).astype(jnp.int32)
     points = design_rows.shape[0]
-    panel_t = jnp.transpose(design_panel.reshape(points, -1))
-    mine, weighted_obs = weigh(panel_t, observations, group_ids, group_sigma)
-    rows = pair_up(meta, design_rows)
+    mine = jnp.transpose(design_panel.reshape(points, -1))
+    weights, weighted_obs = weigh(observations, group_ids, group_sigma)
+    rows = pair_up(design_rows)
 
     foreign = half_swap(mine)
     blocks = [mine, foreign]
@@ -359,14 +385,15 @@
         blocks.append(y_shift(mine, -d))
     for d in (1, 2, 3):
         blocks.append(y_shift(foreign, -d))
-    near = collect(meta, blocks[:2] + [blocks[i] for i in (2, 5, 3, 6, 4, 7)] + [weighted_obs], (rows,))
+    blocks = [blocks[i] for i in (0, 1, 2, 5, 3, 6, 4, 7)]
+    near = collect(weights, weighted_obs, blocks, (rows,))
     other = core_swap(near)
 
     over, z_got, x_got, after = {}, (), (), ()
 
     def piece(*steps):
         nonlocal after
-        (sent,) = over_x(meta, rows, near, steps, after)
+        (sent,) = over_x(rows, near, steps, after)
         after = (sent,)
         got = x_swap(sent)
         for i, dz in enumerate(steps):
@@ -374,15 +401,17 @@
 
     def z_next(s):
         nonlocal after, z_got
-        steps = (-s,) if s == 4 else (-s, s)
-        sent = z_step(meta, rows, other, steps, z_got, after)
+        if s == NZ // 2:
+            sent = z_first(rows, other, after)
+        else:
+            sent = z_step(rows, other, (-s, s), z_got, after)
         after = (sent[0],)
-        z_got = (z_shift(sent[0], -1),) + tuple(z_shift(v, 1) for v in sent[1:])
+        z_got = (z_shift(sent[0], -1), z_shift(sent[1], 1))
 
     def x_next(s):
         nonlocal after, x_got
         steps = (s,) if s == 4 else (s, -s)
-        sent = x_step(meta, rows, near, steps, over, x_got, after)
+        sent = x_step(rows, near, steps, over, x_got, after)
         after = (sent[0],)
         x_got = (z_shift(sent[0], 1),) + tuple(z_shift(v, -1) for v in sent[1:])
 
@@ -390,19 +419,19 @@
     piece(3, -3)
     z_next(4)
     x_next(4)
+    z_next(3)
     piece(2, -2)
+    x_next(3)
     piece(1, -1, 0)
-    z_next(3)
-    x_next(3)
     z_next(2)
     x_next(2)
     z_next(1)
     x_next(1)
     own_x, own_z, rhs_own, beside, cross, across = last(
-        meta, rows, near, other, over[0], x_got, z_got, after
+        rows, near, other, over[0], x_got, z_got, after
     )
     return finish(
-        meta, own_x, own_z, rhs_own, x_swap(beside), cross_swap(cross), half_swap(across)
+        own_x, own_z, rhs_own, x_swap(beside), cross_swap(cross), half_swap(across)
     )
 
 

time: 106 us -> 91.6 us (0.86)
  Pallas kernels: 25.1 us -> 15.8 us
  starting transfers between devices: 47.2 us -> 43.9 us
  waiting for transfers between devices: 29.3 us -> 27.7 us
    pallas_call x15, Pallas kernels: 20.9 us -> 13 us  [call(): pl.pallas_call(body, out_shape=out_shape, in_specs=[IN_VMEM] * (n + extra...]
    ppermute x6, starting transfers between devices: 12.1 us -> 7.84 us  [y_shift(): lax.ppermute(x, 'row', [(y * 2 + c, (y + d) % 4 * 2 + c) for y in range(4...]
    ppermute x14 -> x15, waiting for transfers between devices: 23 us -> 20.1 us  [z_shift(): lax.ppermute(x, 'rep', [(a * NZ + z, a * NZ + (z + d) % NZ) for a in rang...]
    pallas_call x1, Pallas kernels: 1.62 us -> 0.56 us  [weigh(): pl.pallas_call(weigh_kernel, grid=(1,), out_shape=(jax.ShapeDtypeStruct((...]
    ppermute x14 -> x15, starting transfers between devices: 24.4 us -> 24.6 us  [z_shift(): lax.ppermute(x, 'rep', [(a * NZ + z, a * NZ + (z + d) % NZ) for a in rang...]
    unnamed x6 -> x10, local copies, waits for them, and re-layouts: 2.79 us -> 2.8 us
  transfers between devices with their start and end apart: 29 -> 30, of which waited for: 10 -> 9; matrix products, arithmetic and copies ran while one was open for 0% -> 0% of each run, Pallas kernels for 18% -> 14%
where the time goes in v3:
time: 91.6 us; the launch traced here: 91.1 us
  starting transfers between devices  43.9 us (48%)
  waiting for transfers between devices  27.7 us (30%)
  Pallas kernels  15.8 us (17%)
  local copies, waits for them, and re-layouts  2.8 us (3%)
    ppermute x15, starting transfers between devices, z_shift(): lax.ppermute(x, 'rep', [(a * NZ + z, a * NZ + (z + d) % NZ) for a in rang...  24.6 us
    ppermute x15, waiting for transfers between devices, z_shift(): lax.ppermute(x, 'rep', [(a * NZ + z, a * NZ + (z + d) % NZ) for a in rang...  20.1 us
    pallas_call x15, Pallas kernels, call(): pl.pallas_call(body, out_shape=out_shape, in_specs=[IN_VMEM] * (n + extra...  13 us
    ppermute x6, starting transfers between devices, y_shift(): lax.ppermute(x, 'row', [(y * 2 + c, (y + d) % 4 * 2 + c) for y in range(4...  7.84 us
    ppermute x2, starting transfers between devices, half_swap(): return lax.ppermute(x, 'col', [(0, 1), (1, 0)])  6.68 us
    ppermute x2, waiting for transfers between devices, half_swap(): return lax.ppermute(x, 'col', [(0, 1), (1, 0)])  4.61 us
    ppermute x5, starting transfers between devices, x_swap(): lax.ppermute(x, 'rep', [(a * NZ + z, (1 - a) * NZ + z) for a in range(2)...  3.4 us
    unnamed x10, local copies, waits for them, and re-layouts  2.8 us
  transfers between devices with their start and end apart: 30, of which 9 were waited for; matrix products, arithmetic and copies ran while one was open for 0% of the time, Pallas kernels for 14%

profile of v3, /device:TPU:16, one launch (start us, length us, event | category | flops | bytes accessed | tf_op | source)
XLA Modules:
  0.0 91.1 jit_solution(490040339421762015)
XLA Ops:
  0.6 3.1 %collective-permute-start = (bf16[64,1024]{1,0:T(8,128)(2,1)}, bf16[64,1024]{1,0:T(8,128)(2,1)S(1)}, u32[]{:S(2)}, u32[]{:S(2)}) collective-permute-start(bf16[64,1024]{1,0:T(8,128)(2,1)} %bitcast.5), channel_id=1, source_target_pairs={{0,1},{1,0},{2,3},{3,2},{4,5},{5,4},{6,7},{7,6},{8,9},{9,8},{10,11... | collective-permute-start | bytes 393224 | tf_op jit(solution)/shard_map/ppermute | solution.py:364
  3.8 1.3 %collective-permute-start.5 = (bf16[64,1024]{1,0:T(8,128)(2,1)}, bf16[64,1024]{1,0:T(8,128)(2,1)S(1)}, u32[]{:S(2)}, u32[]{:S(2)}) collective-permute-start(bf16[64,1024]{1,0:T(8,128)(2,1)} %bitcast.6), channel_id=1, source_target_pairs={{0,4},{2,6},{4,8},{6,10},{8,12},{10,14},{12,0},{14,2},{1,5},{3,7},... | collective-permute-start | bytes 393224 | tf_op jit(solution)/shard_map/ppermute | solution.py:354
  5.0 0.6 collective-permute-start.3
  5.7 1.1 %collective-permute-start.1 = (bf16[64,1024]{1,0:T(8,128)(2,1)}, bf16[64,1024]{1,0:T(8,128)(2,1)S(1)}, u32[]{:S(2)}, u32[]{:S(2)}) collective-permute-start(bf16[64,1024]{1,0:T(8,128)(2,1)} %bitcast.8), channel_id=1, source_target_pairs={{0,12},{2,14},{4,0},{6,2},{8,4},{10,6},{12,8},{14,10},{1,13},{3,15... | collective-permute-start | bytes 393224 | tf_op jit(solution)/shard_map/ppermute | solution.py:354
  6.7 1.0 %collective-permute-done.refs_3_ = bf16[64,1024]{1,0:T(8,128)(2,1)S(1)} collective-permute-done((bf16[64,1024]{1,0:T(8,128)(2,1)}, bf16[64,1024]{1,0:T(8,128)(2,1)S(1)}, u32[]{:S(2)}, u32[]{:S(2)}) %collective-permute-start) | collective-permute-done | bytes 131104 | tf_op jit(solution)/shard_map/ppermute | solution.py:364
  7.7 1.3 %collective-permute-start.6 = (bf16[64,1024]{1,0:T(8,128)(2,1)S(1)}, bf16[64,1024]{1,0:T(8,128)(2,1)S(1)}, u32[]{:S(2)}, u32[]{:S(2)}) collective-permute-start(bf16[64,1024]{1,0:T(8,128)(2,1)S(1)} %collective-permute-done.refs_3_), channel_id=1, source_target_pairs={{0,4},{2,6},{4,8},{6,10},{8,12},{10,14},{12,0},{14,2},{1,5},{3,7},... | collective-permute-start | bytes 393224 | tf_op jit(solution)/shard_map/ppermute | solution.py:354
  9.0 1.6 %collective-permute-start.4 = (bf16[64,1024]{1,0:T(8,128)(2,1)S(1)}, bf16[64,1024]{1,0:T(8,128)(2,1)S(1)}, u32[]{:S(2)}, u32[]{:S(2)}) collective-permute-start(bf16[64,1024]{1,0:T(8,128)(2,1)S(1)} %collective-permute-done.refs_3_), channel_id=1, source_target_pairs={{0,8},{2,10},{4,12},{6,14},{8,0},{10,2},{12,4},{14,6},{1,9},{3,11}... | collective-permute-start | bytes 393224 | tf_op jit(solution)/shard_map/ppermute | solution.py:354
  10.6 2.0 %collective-permute-start.2 = (bf16[64,1024]{1,0:T(8,128)(2,1)S(1)}, bf16[64,1024]{1,0:T(8,128)(2,1)S(1)}, u32[]{:S(2)}, u32[]{:S(2)}) collective-permute-start(bf16[64,1024]{1,0:T(8,128)(2,1)S(1)} %collective-permute-done.refs_3_), channel_id=1, source_target_pairs={{0,12},{2,14},{4,0},{6,2},{8,4},{10,6},{12,8},{14,10},{1,13},{3,15... | collective-permute-start | bytes 393224 | tf_op jit(solution)/shard_map/ppermute | solution.py:354
  12.6 2.8 %copy-done = bf16[1024,3072]{1,0:T(8,128)(2,1)S(1)} copy-done((bf16[1024,3072]{1,0:T(8,128)(2,1)S(1)}, bf16[1024,3072]{1,0:T(8,128)(2,1)}, u32[]{:S(2)}) %copy-start) | copy-done | bytes 6291480
  15.3 2.3 %shard_map.68.refs_10_.refs_0_ = bf16[8,1024,384]{2,1,0:T(8,128)(2,1)S(1)} custom-call(bf16[1024,3072]{1,0:T(8,128)(2,1)S(1)} %copy-done, bf16[1024,3072]{1,0:T(8,128)(2,1)S(1)} %copy-done), custom_call_target="tpu_custom_call" | custom-call | bytes 12582912 | tf_op jit(solution)/shard_map/pallas_call | solution.py:76
  17.6 0.6 shard_map.69
  18.3 0.9 %collective-permute-done.2.refs_5_ = bf16[64,1024]{1,0:T(8,128)(2,1)S(1)} collective-permute-done((bf16[64,1024]{1,0:T(8,128)(2,1)S(1)}, bf16[64,1024]{1,0:T(8,128)(2,1)S(1)}, u32[]{:S(2)}, u32[]{:S(2)}) %collective-permute-start.2) | collective-permute-done | bytes 131104 | tf_op jit(solution)/shard_map/ppermute | solution.py:354
  19.9 0.7 collective-permute-start.9
  20.6 0.7 shard_map.72.refs_2_
  21.4 1.5 %collective-permute-start.8 = (bf16[2,272,384]{2,1,0:T(8,128)(2,1)S(1)}, bf16[2,272,384]{2,1,0:T(8,128)(2,1)S(1)}, u32[]{:S(2)}, u32[]{:S(2)}) collective-permute-start(bf16[2,272,384]{2,1,0:T(8,128)(2,1)S(1)} %shard_map.72.refs_2_), channel_id=1, source_target_pairs={{0,128},{16,144},{32,160},{48,176},{64,192},{80,208},{96,224},{112... | collective-permute-start | bytes 1253384 | tf_op jit(solution)/shard_map/ppermute | solution.py:348
  22.9 0.7 shard_map.73
  23.6 2.0 %collective-permute-start.12 = (bf16[256,384]{1,0:T(8,128)(2,1)S(1)}, bf16[256,384]{1,0:T(8,128)(2,1)S(1)}, u32[]{:S(2)}, u32[]{:S(2)}) collective-permute-start(bf16[256,384]{1,0:T(8,128)(2,1)S(1)} %get-tuple-element.27), channel_id=1, source_target_pairs={{0,16},{16,32},{32,48},{48,64},{64,80},{80,96},{96,112},{112,0},{1... | collective-permute-start | bytes 589832 | tf_op jit(solution)/shard_map/ppermute | solution.py:342
  25.6 4.0 %collective-permute-start.11 = (bf16[256,384]{1,0:T(8,128)(2,1)S(1)}, bf16[256,384]{1,0:T(8,128)(2,1)S(1)}, u32[]{:S(2)}, u32[]{:S(2)}) collective-permute-start(bf16[256,384]{1,0:T(8,128)(2,1)S(1)} %get-tuple-element.26.refs_3_), channel_id=1, source_target_pairs={{0,112},{16,0},{32,16},{48,32},{64,48},{80,64},{96,80},{112,96},{1... | collective-permute-start | bytes 589832 | tf_op jit(solution)/shard_map/ppermute | solution.py:342
  30.1 0.5 collective-permute-start.10
  30.6 3.9 %collective-permute-done.12.refs_3_ = bf16[256,384]{1,0:T(8,128)(2,1)S(1)} collective-permute-done((bf16[256,384]{1,0:T(8,128)(2,1)S(1)}, bf16[256,384]{1,0:T(8,128)(2,1)S(1)}, u32[]{:S(2)}, u32[]{:S(2)}) %collective-permute-start.12) | collective-permute-done | bytes 196640 | tf_op jit(solution)/shard_map/ppermute | solution.py:342
  34.5 1.3 %shard_map.75 = (bf16[512,384]{1,0:T(8,128)(2,1)S(1)}, bf16[512,384]{1,0:T(8,128)(2,1)S(1)}) custom-call(bf16[8,1024,384]{2,1,0:T(8,128)(2,1)S(1)} %shard_map.68.refs_10_.refs_0_, bf16[528,1024]{1,0:T(8,128)(2,1)S(1)} %collective-permute-done.7.refs_1_.refs_2_, bf16[256,384]{1,0:T(8,128)(2,1)S(1)} %collective-permute-done.11.refs_2_, ...), custom_call_target="tpu_custom_call" | custom-call | flops 4000000000 | bytes 1 | tf_op jit(solution)/shard_map/pallas_call | solution.py:27
  35.9 3.2 %collective-permute-start.17 = (bf16[512,384]{1,0:T(8,128)(2,1)S(1)}, bf16[512,384]{1,0:T(8,128)(2,1)S(1)}, u32[]{:S(2)}, u32[]{:S(2)}) collective-permute-start(bf16[512,384]{1,0:T(8,128)(2,1)S(1)} %get-tuple-element.28.refs_2_), channel_id=1, source_target_pairs={{0,112},{16,0},{32,16},{48,32},{64,48},{80,64},{96,80},{112,96},{1... | collective-permute-start | bytes 1179656 | tf_op jit(solution)/shard_map/ppermute | solution.py:342
  39.1 0.7 shard_map.76.refs_4_
  39.9 0.7 collective-permute-start.14
  40.6 0.8 shard_map.77
  41.4 1.0 %shard_map.78.refs_4_ = bf16[3,272,384]{2,1,0:T(8,128)(2,1)S(1)} custom-call(bf16[8,1024,384]{2,1,0:T(8,128)(2,1)S(1)} %shard_map.68.refs_10_.refs_0_, bf16[528,1024]{1,0:T(8,128)(2,1)S(1)} %shard_map.70.refs_1_, bf16[272,384]{1,0:T(8,128)(2,1)S(1)} %get-tuple-element.29.refs_2_), custom_call_target="tpu_custom_call" | custom-call | flops 4000000000 | bytes 1 | tf_op jit(solution)/shard_map/pallas_call | solution.py:27
  42.5 3.3 %collective-permute-start.16 = (bf16[272,384]{1,0:T(8,128)(2,1)S(1)}, bf16[272,384]{1,0:T(8,128)(2,1)S(1)}, u32[]{:S(2)}, u32[]{:S(2)}) collective-permute-start(bf16[272,384]{1,0:T(8,128)(2,1)S(1)} %get-tuple-element.30), channel_id=1, source_target_pairs={{0,112},{16,0},{32,16},{48,32},{64,48},{80,64},{96,80},{112,96},{1... | collective-permute-start | bytes 626696 | tf_op jit(solution)/shard_map/ppermute | solution.py:342
  45.8 3.4 %collective-permute-done.18.refs_3_ = bf16[512,384]{1,0:T(8,128)(2,1)S(1)} collective-permute-done((bf16[512,384]{1,0:T(8,128)(2,1)S(1)}, bf16[512,384]{1,0:T(8,128)(2,1)S(1)}, u32[]{:S(2)}, u32[]{:S(2)}) %collective-permute-start.18) | collective-permute-done | bytes 393248 | tf_op jit(solution)/shard_map/ppermute | solution.py:342
  49.1 1.3 %shard_map.79 = (bf16[512,384]{1,0:T(8,128)(2,1)S(1)}, bf16[512,384]{1,0:T(8,128)(2,1)S(1)}) custom-call(bf16[8,1024,384]{2,1,0:T(8,128)(2,1)S(1)} %shard_map.68.refs_10_.refs_0_, bf16[528,1024]{1,0:T(8,128)(2,1)S(1)} %collective-permute-done.7.refs_1_.refs_2_, bf16[512,384]{1,0:T(8,128)(2,1)S(1)} %collective-permute-done.17.refs_2_, ...), custom_call_target="tpu_custom_call" | custom-call | flops 4000000000 | bytes 1 | tf_op jit(solution)/shard_map/pallas_call | solution.py:27
  50.4 2.5 %collective-permute-start.22 = (bf16[512,384]{1,0:T(8,128)(2,1)S(1)}, bf16[512,384]{1,0:T(8,128)(2,1)S(1)}, u32[]{:S(2)}, u32[]{:S(2)}) collective-permute-start(bf16[512,384]{1,0:T(8,128)(2,1)S(1)} %get-tuple-element.35), channel_id=1, source_target_pairs={{0,16},{16,32},{32,48},{48,64},{64,80},{80,96},{96,112},{112,0},{1... | collective-permute-start | bytes 1179656 | tf_op jit(solution)/shard_map/ppermute | solution.py:342
  52.9 0.9 collective-permute-start.21
  53.8 0.5 collective-permute-start.13
  54.3 0.8 shard_map.80
  55.1 1.9 %collective-permute-start.20 = (bf16[272,384]{1,0:T(8,128)(2,1)S(1)}, bf16[272,384]{1,0:T(8,128)(2,1)S(1)}, u32[]{:S(2)}, u32[]{:S(2)}) collective-permute-start(bf16[272,384]{1,0:T(8,128)(2,1)S(1)} %get-tuple-element.34), channel_id=1, source_target_pairs={{0,112},{16,0},{32,16},{48,32},{64,48},{80,64},{96,80},{112,96},{1... | collective-permute-start | bytes 626696 | tf_op jit(solution)/shard_map/ppermute | solution.py:342
  57.2 5.8 %collective-permute-done.22.refs_3_ = bf16[512,384]{1,0:T(8,128)(2,1)S(1)} collective-permute-done((bf16[512,384]{1,0:T(8,128)(2,1)S(1)}, bf16[512,384]{1,0:T(8,128)(2,1)S(1)}, u32[]{:S(2)}, u32[]{:S(2)}) %collective-permute-start.22) | collective-permute-done | bytes 393248 | tf_op jit(solution)/shard_map/ppermute | solution.py:342
  63.0 1.3 %shard_map.81 = (bf16[512,384]{1,0:T(8,128)(2,1)S(1)}, bf16[512,384]{1,0:T(8,128)(2,1)S(1)}) custom-call(bf16[8,1024,384]{2,1,0:T(8,128)(2,1)S(1)} %shard_map.68.refs_10_.refs_0_, bf16[528,1024]{1,0:T(8,128)(2,1)S(1)} %collective-permute-done.7.refs_1_.refs_2_, bf16[512,384]{1,0:T(8,128)(2,1)S(1)} %collective-permute-done.21.refs_2_, ...), custom_call_target="tpu_custom_call" | custom-call | flops 4000000000 | bytes 1 | tf_op jit(solution)/shard_map/pallas_call | solution.py:27
  64.2 2.2 %collective-permute-start.26 = (bf16[512,384]{1,0:T(8,128)(2,1)S(1)}, bf16[512,384]{1,0:T(8,128)(2,1)S(1)}, u32[]{:S(2)}, u32[]{:S(2)}) collective-permute-start(bf16[512,384]{1,0:T(8,128)(2,1)S(1)} %get-tuple-element.39), channel_id=1, source_target_pairs={{0,16},{16,32},{32,48},{48,64},{64,80},{80,96},{96,112},{112,0},{1... | collective-permute-start | bytes 1179656 | tf_op jit(solution)/shard_map/ppermute | solution.py:342
  66.4 1.1 %collective-permute-start.25 = (bf16[512,384]{1,0:T(8,128)(2,1)S(1)}, bf16[512,384]{1,0:T(8,128)(2,1)S(1)}, u32[]{:S(2)}, u32[]{:S(2)}) collective-permute-start(bf16[512,384]{1,0:T(8,128)(2,1)S(1)} %get-tuple-element.36.refs_5_), channel_id=1, source_target_pairs={{0,112},{16,0},{32,16},{48,32},{64,48},{80,64},{96,80},{112,96},{1... | collective-permute-start | bytes 1179656 | tf_op jit(solution)/shard_map/ppermute | solution.py:342
  67.6 0.8 shard_map.82
  68.3 2.6 %collective-permute-start.24 = (bf16[272,384]{1,0:T(8,128)(2,1)S(1)}, bf16[272,384]{1,0:T(8,128)(2,1)S(1)}, u32[]{:S(2)}, u32[]{:S(2)}) collective-permute-start(bf16[272,384]{1,0:T(8,128)(2,1)S(1)} %get-tuple-element.38), channel_id=1, source_target_pairs={{0,112},{16,0},{32,16},{48,32},{64,48},{80,64},{96,80},{112,96},{1... | collective-permute-start | bytes 626696 | tf_op jit(solution)/shard_map/ppermute | solution.py:342
  70.9 6.1 %collective-permute-done.24.refs_5_ = bf16[272,384]{1,0:T(8,128)(2,1)S(1)} collective-permute-done((bf16[272,384]{1,0:T(8,128)(2,1)S(1)}, bf16[272,384]{1,0:T(8,128)(2,1)S(1)}, u32[]{:S(2)}, u32[]{:S(2)}) %collective-permute-start.24) | collective-permute-done | bytes 208928 | tf_op jit(solution)/shard_map/ppermute | solution.py:342
  77.0 0.9 %collective-permute-done.23.refs_4_ = bf16[272,384]{1,0:T(8,128)(2,1)S(1)} collective-permute-done((bf16[272,384]{1,0:T(8,128)(2,1)S(1)}, bf16[272,384]{1,0:T(8,128)(2,1)S(1)}, u32[]{:S(2)}, u32[]{:S(2)}) %collective-permute-start.23) | collective-permute-done | bytes 208928 | tf_op jit(solution)/shard_map/ppermute | solution.py:342
  78.0 1.4 %shard_map.83 = (f32[192,128]{1,0:T(8,128)S(1)}, f32[192,256]{1,0:T(8,128)S(1)}, f32[8,192]{1,0:T(8,128)S(1)}, bf16[192,512]{1,0:T(8,128)(2,1)S(1)}, bf16[208,51...) custom-call(bf16[8,1024,384]{2,1,0:T(8,128)(2,1)S(1)} %shard_map.68.refs_10_.refs_0_, ...), custom_call_target="tpu_custom_call" | custom-call | flops 4000000000 | bytes 1 | tf_op jit(solution)/shard_map/pallas_call | solution.py:27
  79.3 1.2 %collective-permute-start.28 = (bf16[208,512]{1,0:T(8,128)(2,1)S(1)}, bf16[208,512]{1,0:T(8,128)(2,1)S(1)}, u32[]{:S(2)}, u32[]{:S(2)}) collective-permute-start(bf16[208,512]{1,0:T(8,128)(2,1)S(1)} %get-tuple-element.44), channel_id=1, source_target_pairs={{0,129},{1,128},{16,145},{17,144},{32,161},{33,160},{48,177},{49,1... | collective-permute-start | bytes 638984 | tf_op jit(solution)/shard_map/ppermute | solution.py:373
  80.6 3.6 %collective-permute-start.29 = (bf16[192,512]{1,0:T(8,128)(2,1)S(1)}, bf16[192,512]{1,0:T(8,128)(2,1)S(1)}, u32[]{:S(2)}, u32[]{:S(2)}) collective-permute-start(bf16[192,512]{1,0:T(8,128)(2,1)S(1)} %get-tuple-element.45), channel_id=1, source_target_pairs={{0,1},{1,0},{2,3},{3,2},{4,5},{5,4},{6,7},{7,6},{8,9},{9,8},{10,11... | collective-permute-start | bytes 589832 | tf_op jit(solution)/shard_map/ppermute | solution.py:364
  84.1 2.1 %collective-permute-done.27.refs_3_ = bf16[192,512]{1,0:T(8,128)(2,1)S(1)} collective-permute-done((bf16[192,512]{1,0:T(8,128)(2,1)S(1)}, bf16[192,512]{1,0:T(8,128)(2,1)S(1)}, u32[]{:S(2)}, u32[]{:S(2)}) %collective-permute-start.27) | collective-permute-done | bytes 196640 | tf_op jit(solution)/shard_map/ppermute | solution.py:348
  86.2 3.6 %collective-permute-done.29.refs_5_ = bf16[192,512]{1,0:T(8,128)(2,1)S(1)} collective-permute-done((bf16[192,512]{1,0:T(8,128)(2,1)S(1)}, bf16[192,512]{1,0:T(8,128)(2,1)S(1)}, u32[]{:S(2)}, u32[]{:S(2)}) %collective-permute-start.29) | collective-permute-done | bytes 196640 | tf_op jit(solution)/shard_map/ppermute | solution.py:364
  89.9 1.2 %shard_map.84 = (f32[1,2,192,512]{3,2,1,0:T(8,128)}, f32[1,2,192]{2,1,0:T(2,128)}) custom-call(f32[192,128]{1,0:T(8,128)S(1)} %get-tuple-element.40.refs_0_, f32[192,256]{1,0:T(8,128)S(1)} %get-tuple-element.41.refs_1_, f32[8,192]{1,0:T(8,128)S(1)} %get-tuple-element.42.refs_2_, bf16[192,512]{1,0:T(8,128)(2,1)S(1)} %collective-permute-done.27.refs_3_, ...), custom_call_target="tpu_custom_call" | custom-call | flops 4000000000 | bytes 1 | tf_op jit(solution)/shard_map/pallas_call | solution.py:27
  (39 shorter events, 1.7 us)
Async XLA Ops:
  0.6 17.0 %copy-start.4 = (f32[8]{0:T(128)S(1)}, f32[8]{0:T(128)}, u32[]{:S(2)}) copy-start(f32[8]{0:T(128)} %sigma_ref.1) | copy-start | bytes 100
  0.6 7.0 %collective-permute-start = (bf16[64,1024]{1,0:T(8,128)(2,1)}, bf16[64,1024]{1,0:T(8,128)(2,1)S(1)}, u32[]{:S(2)}, u32[]{:S(2)}) collective-permute-start(bf16[64,1024]{1,0:T(8,128)(2,1)} %bitcast.5), channel_id=1, source_target_pairs={{0,1},{1,0},{2,3},{3,2},{4,5},{5,4},{6,7},{7,6},{8,9},{9,8},{10,11... | collective-permute-start | bytes 393224 | tf_op jit(solution)/shard_map/ppermute | solution.py:364
  3.8 6.8 %collective-permute-start.5 = (bf16[64,1024]{1,0:T(8,128)(2,1)}, bf16[64,1024]{1,0:T(8,128)(2,1)S(1)}, u32[]{:S(2)}, u32[]{:S(2)}) collective-permute-start(bf16[64,1024]{1,0:T(8,128)(2,1)} %bitcast.6), channel_id=1, source_target_pairs={{0,4},{2,6},{4,8},{6,10},{8,12},{10,14},{12,0},{14,2},{1,5},{3,7},... | collective-permute-start | bytes 393224 | tf_op jit(solution)/shard_map/ppermute | solution.py:354
  5.0 13.2 %collective-permute-start.3 = (bf16[64,1024]{1,0:T(8,128)(2,1)}, bf16[64,1024]{1,0:T(8,128)(2,1)S(1)}, u32[]{:S(2)}, u32[]{:S(2)}) collective-permute-start(bf16[64,1024]{1,0:T(8,128)(2,1)} %bitcast.7), channel_id=1, source_target_pairs={{0,8},{2,10},{4,12},{6,14},{8,0},{10,2},{12,4},{14,6},{1,9},{3,11}... | collective-permute-start | bytes 393224 | tf_op jit(solution)/shard_map/ppermute | solution.py:354
  5.7 12.6 %collective-permute-start.1 = (bf16[64,1024]{1,0:T(8,128)(2,1)}, bf16[64,1024]{1,0:T(8,128)(2,1)S(1)}, u32[]{:S(2)}, u32[]{:S(2)}) collective-permute-start(bf16[64,1024]{1,0:T(8,128)(2,1)} %bitcast.8), channel_id=1, source_target_pairs={{0,12},{2,14},{4,0},{6,2},{8,4},{10,6},{12,8},{14,10},{1,13},{3,15... | collective-permute-start | bytes 393224 | tf_op jit(solution)/shard_map/ppermute | solution.py:354
  7.7 10.6 %collective-permute-start.6 = (bf16[64,1024]{1,0:T(8,128)(2,1)S(1)}, bf16[64,1024]{1,0:T(8,128)(2,1)S(1)}, u32[]{:S(2)}, u32[]{:S(2)}) collective-permute-start(bf16[64,1024]{1,0:T(8,128)(2,1)S(1)} %collective-permute-done.refs_3_), channel_id=1, source_target_pairs={{0,4},{2,6},{4,8},{6,10},{8,12},{10,14},{12,0},{14,2},{1,5},{3,7},... | collective-permute-start | bytes 393224 | tf_op jit(solution)/shard_map/ppermute | solution.py:354
  9.0 9.3 %collective-permute-start.4 = (bf16[64,1024]{1,0:T(8,128)(2,1)S(1)}, bf16[64,1024]{1,0:T(8,128)(2,1)S(1)}, u32[]{:S(2)}, u32[]{:S(2)}) collective-permute-start(bf16[64,1024]{1,0:T(8,128)(2,1)S(1)} %collective-permute-done.refs_3_), channel_id=1, source_target_pairs={{0,8},{2,10},{4,12},{6,14},{8,0},{10,2},{12,4},{14,6},{1,9},{3,11}... | collective-permute-start | bytes 393224 | tf_op jit(solution)/shard_map/ppermute | solution.py:354
  10.6 8.6 %collective-permute-start.2 = (bf16[64,1024]{1,0:T(8,128)(2,1)S(1)}, bf16[64,1024]{1,0:T(8,128)(2,1)S(1)}, u32[]{:S(2)}, u32[]{:S(2)}) collective-permute-start(bf16[64,1024]{1,0:T(8,128)(2,1)S(1)} %collective-permute-done.refs_3_), channel_id=1, source_target_pairs={{0,12},{2,14},{4,0},{6,2},{8,4},{10,6},{12,8},{14,10},{1,13},{3,15... | collective-permute-start | bytes 393224 | tf_op jit(solution)/shard_map/ppermute | solution.py:354
  12.6 2.8 %copy-start = (bf16[1024,3072]{1,0:T(8,128)(2,1)S(1)}, bf16[1024,3072]{1,0:T(8,128)(2,1)}, u32[]{:S(2)}) copy-start(bf16[1024,3072]{1,0:T(8,128)(2,1)} %second_ref.1) | copy-start | bytes 18874372
  15.3 2.3 %copy-start.2 = (f32[1024]{0:T(1024)S(1)}, f32[1024]{0:T(1024)}, u32[]{:S(2)}) copy-start(f32[1024]{0:T(1024)} %param.7) | copy-start | bytes 12292
  15.3 2.3 %copy-start.3 = (s32[1024]{0:T(1024)S(1)}, s32[1024]{0:T(1024)}, u32[]{:S(2)}) copy-start(s32[1024]{0:T(1024)} %param.8) | copy-start | bytes 12292
  15.3 3.8 %copy-start.1 = (bf16[1024,1,64]{0,2,1:T(8,128)(2,1)S(1)}, bf16[1024,1,64]{0,2,1:T(8,128)(2,1)}, u32[]{:S(2)}) copy-start(bf16[1024,1,64]{0,2,1:T(8,128)(2,1)} %param.6) | copy-start | bytes 393220
  19.4 3.5 %collective-permute-start.7 = (bf16[528,1024]{1,0:T(8,128)(2,1)S(1)}, bf16[528,1024]{1,0:T(8,128)(2,1)S(1)}, u32[]{:S(2)}, u32[]{:S(2)}) collective-permute-start(bf16[528,1024]{1,0:T(8,128)(2,1)S(1)} %shard_map.70.refs_1_), channel_id=1, source_target_pairs={{0,2},{2,0},{4,6},{6,4},{8,10},{10,8},{12,14},{14,12},{1,3},{3,1},... | collective-permute-start | bytes 3244040 | tf_op jit(solution)/shard_map/ppermute | solution.py:360
  19.9 9.7 %collective-permute-start.9 = (bf16[1,272,384]{2,1,0:T(8,128)(2,1)S(1)}, bf16[1,272,384]{2,1,0:T(8,128)(2,1)S(1)}, u32[]{:S(2)}, u32[]{:S(2)}) collective-permute-start(bf16[1,272,384]{2,1,0:T(8,128)(2,1)S(1)} %shard_map.71.refs_2_), channel_id=1, source_target_pairs={{0,128},{16,144},{32,160},{48,176},{64,192},{80,208},{96,224},{112... | collective-permute-start | bytes 626696 | tf_op jit(solution)/shard_map/ppermute | solution.py:348
  21.4 19.2 %collective-permute-start.8 = (bf16[2,272,384]{2,1,0:T(8,128)(2,1)S(1)}, bf16[2,272,384]{2,1,0:T(8,128)(2,1)S(1)}, u32[]{:S(2)}, u32[]{:S(2)}) collective-permute-start(bf16[2,272,384]{2,1,0:T(8,128)(2,1)S(1)} %shard_map.72.refs_2_), channel_id=1, source_target_pairs={{0,128},{16,144},{32,160},{48,176},{64,192},{80,208},{96,224},{112... | collective-permute-start | bytes 1253384 | tf_op jit(solution)/shard_map/ppermute | solution.py:348
  23.6 10.9 %collective-permute-start.12 = (bf16[256,384]{1,0:T(8,128)(2,1)S(1)}, bf16[256,384]{1,0:T(8,128)(2,1)S(1)}, u32[]{:S(2)}, u32[]{:S(2)}) collective-permute-start(bf16[256,384]{1,0:T(8,128)(2,1)S(1)} %get-tuple-element.27), channel_id=1, source_target_pairs={{0,16},{16,32},{32,48},{48,64},{64,80},{80,96},{96,112},{112,0},{1... | collective-permute-start | bytes 589832 | tf_op jit(solution)/shard_map/ppermute | solution.py:342
  25.6 8.9 %collective-permute-start.11 = (bf16[256,384]{1,0:T(8,128)(2,1)S(1)}, bf16[256,384]{1,0:T(8,128)(2,1)S(1)}, u32[]{:S(2)}, u32[]{:S(2)}) collective-permute-start(bf16[256,384]{1,0:T(8,128)(2,1)S(1)} %get-tuple-element.26.refs_3_), channel_id=1, source_target_pairs={{0,112},{16,0},{32,16},{48,32},{64,48},{80,64},{96,80},{112,96},{1... | collective-permute-start | bytes 589832 | tf_op jit(solution)/shard_map/ppermute | solution.py:342
  30.1 10.5 %collective-permute-start.10 = (bf16[272,384]{1,0:T(8,128)(2,1)S(1)}, bf16[272,384]{1,0:T(8,128)(2,1)S(1)}, u32[]{:S(2)}, u32[]{:S(2)}) collective-permute-start(bf16[272,384]{1,0:T(8,128)(2,1)S(1)} %shard_map.74.refs_4_), channel_id=1, source_target_pairs={{0,16},{16,32},{32,48},{48,64},{64,80},{80,96},{96,112},{112,0},{1... | collective-permute-start | bytes 626696 | tf_op jit(solution)/shard_map/ppermute | solution.py:342
  35.8 13.3 %collective-permute-start.18 = (bf16[512,384]{1,0:T(8,128)(2,1)S(1)}, bf16[512,384]{1,0:T(8,128)(2,1)S(1)}, u32[]{:S(2)}, u32[]{:S(2)}) collective-permute-start(bf16[512,384]{1,0:T(8,128)(2,1)S(1)} %get-tuple-element.31), channel_id=1, source_target_pairs={{0,16},{16,32},{32,48},{48,64},{64,80},{80,96},{96,112},{112,0},{1... | collective-permute-start | bytes 1179656 | tf_op jit(solution)/shard_map/ppermute | solution.py:342
  35.9 13.3 %collective-permute-start.17 = (bf16[512,384]{1,0:T(8,128)(2,1)S(1)}, bf16[512,384]{1,0:T(8,128)(2,1)S(1)}, u32[]{:S(2)}, u32[]{:S(2)}) collective-permute-start(bf16[512,384]{1,0:T(8,128)(2,1)S(1)} %get-tuple-element.28.refs_2_), channel_id=1, source_target_pairs={{0,112},{16,0},{32,16},{48,32},{64,48},{80,64},{96,80},{112,96},{1... | collective-permute-start | bytes 1179656 | tf_op jit(solution)/shard_map/ppermute | solution.py:342
  39.9 14.5 %collective-permute-start.14 = (bf16[2,272,384]{2,1,0:T(8,128)(2,1)S(1)}, bf16[2,272,384]{2,1,0:T(8,128)(2,1)S(1)}, u32[]{:S(2)}, u32[]{:S(2)}) collective-permute-start(bf16[2,272,384]{2,1,0:T(8,128)(2,1)S(1)} %shard_map.76.refs_4_), channel_id=1, source_target_pairs={{0,128},{16,144},{32,160},{48,176},{64,192},{80,208},{96,224},{112... | collective-permute-start | bytes 1253384 | tf_op jit(solution)/shard_map/ppermute | solution.py:348
  41.3 13.0 %collective-permute-start.15 = (bf16[272,384]{1,0:T(8,128)(2,1)S(1)}, bf16[272,384]{1,0:T(8,128)(2,1)S(1)}, u32[]{:S(2)}, u32[]{:S(2)}) collective-permute-start(bf16[272,384]{1,0:T(8,128)(2,1)S(1)} %get-tuple-element.29.refs_2_), channel_id=1, source_target_pairs={{0,16},{16,32},{32,48},{48,64},{64,80},{80,96},{96,112},{112,0},{1... | collective-permute-start | bytes 626696 | tf_op jit(solution)/shard_map/ppermute | solution.py:342
  42.5 11.3 %collective-permute-start.16 = (bf16[272,384]{1,0:T(8,128)(2,1)S(1)}, bf16[272,384]{1,0:T(8,128)(2,1)S(1)}, u32[]{:S(2)}, u32[]{:S(2)}) collective-permute-start(bf16[272,384]{1,0:T(8,128)(2,1)S(1)} %get-tuple-element.30), channel_id=1, source_target_pairs={{0,112},{16,0},{32,16},{48,32},{64,48},{80,64},{96,80},{112,96},{1... | collective-permute-start | bytes 626696 | tf_op jit(solution)/shard_map/ppermute | solution.py:342
  50.4 12.5 %collective-permute-start.22 = (bf16[512,384]{1,0:T(8,128)(2,1)S(1)}, bf16[512,384]{1,0:T(8,128)(2,1)S(1)}, u32[]{:S(2)}, u32[]{:S(2)}) collective-permute-start(bf16[512,384]{1,0:T(8,128)(2,1)S(1)} %get-tuple-element.35), channel_id=1, source_target_pairs={{0,16},{16,32},{32,48},{48,64},{64,80},{80,96},{96,112},{112,0},{1... | collective-permute-start | bytes 1179656 | tf_op jit(solution)/shard_map/ppermute | solution.py:342
  52.9 10.1 %collective-permute-start.21 = (bf16[512,384]{1,0:T(8,128)(2,1)S(1)}, bf16[512,384]{1,0:T(8,128)(2,1)S(1)}, u32[]{:S(2)}, u32[]{:S(2)}) collective-permute-start(bf16[512,384]{1,0:T(8,128)(2,1)S(1)} %get-tuple-element.32.refs_5_), channel_id=1, source_target_pairs={{0,112},{16,0},{32,16},{48,32},{64,48},{80,64},{96,80},{112,96},{1... | collective-permute-start | bytes 1179656 | tf_op jit(solution)/shard_map/ppermute | solution.py:342
  53.8 13.7 %collective-permute-start.13 = (bf16[3,272,384]{2,1,0:T(8,128)(2,1)S(1)}, bf16[3,272,384]{2,1,0:T(8,128)(2,1)S(1)}, u32[]{:S(2)}, u32[]{:S(2)}) collective-permute-start(bf16[3,272,384]{2,1,0:T(8,128)(2,1)S(1)} %shard_map.78.refs_4_), channel_id=1, source_target_pairs={{0,128},{16,144},{32,160},{48,176},{64,192},{80,208},{96,224},{112... | collective-permute-start | bytes 1880072 | tf_op jit(solution)/shard_map/ppermute | solution.py:348
  55.1 12.4 %collective-permute-start.20 = (bf16[272,384]{1,0:T(8,128)(2,1)S(1)}, bf16[272,384]{1,0:T(8,128)(2,1)S(1)}, u32[]{:S(2)}, u32[]{:S(2)}) collective-permute-start(bf16[272,384]{1,0:T(8,128)(2,1)S(1)} %get-tuple-element.34), channel_id=1, source_target_pairs={{0,112},{16,0},{32,16},{48,32},{64,48},{80,64},{96,80},{112,96},{1... | collective-permute-start | bytes 626696 | tf_op jit(solution)/shard_map/ppermute | solution.py:342
  57.0 10.6 %collective-permute-start.19 = (bf16[272,384]{1,0:T(8,128)(2,1)S(1)}, bf16[272,384]{1,0:T(8,128)(2,1)S(1)}, u32[]{:S(2)}, u32[]{:S(2)}) collective-permute-start(bf16[272,384]{1,0:T(8,128)(2,1)S(1)} %get-tuple-element.33.refs_4_), channel_id=1, source_target_pairs={{0,16},{16,32},{32,48},{48,64},{64,80},{80,96},{96,112},{112,0},{1... | collective-permute-start | bytes 626696 | tf_op jit(solution)/shard_map/ppermute | solution.py:342
  64.2 13.7 %collective-permute-start.26 = (bf16[512,384]{1,0:T(8,128)(2,1)S(1)}, bf16[512,384]{1,0:T(8,128)(2,1)S(1)}, u32[]{:S(2)}, u32[]{:S(2)}) collective-permute-start(bf16[512,384]{1,0:T(8,128)(2,1)S(1)} %get-tuple-element.39), channel_id=1, source_target_pairs={{0,16},{16,32},{32,48},{48,64},{64,80},{80,96},{96,112},{112,0},{1... | collective-permute-start | bytes 1179656 | tf_op jit(solution)/shard_map/ppermute | solution.py:342
  66.4 11.5 %collective-permute-start.25 = (bf16[512,384]{1,0:T(8,128)(2,1)S(1)}, bf16[512,384]{1,0:T(8,128)(2,1)S(1)}, u32[]{:S(2)}, u32[]{:S(2)}) collective-permute-start(bf16[512,384]{1,0:T(8,128)(2,1)S(1)} %get-tuple-element.36.refs_5_), channel_id=1, source_target_pairs={{0,112},{16,0},{32,16},{48,32},{64,48},{80,64},{96,80},{112,96},{1... | collective-permute-start | bytes 1179656 | tf_op jit(solution)/shard_map/ppermute | solution.py:342
  68.3 8.7 %collective-permute-start.24 = (bf16[272,384]{1,0:T(8,128)(2,1)S(1)}, bf16[272,384]{1,0:T(8,128)(2,1)S(1)}, u32[]{:S(2)}, u32[]{:S(2)}) collective-permute-start(bf16[272,384]{1,0:T(8,128)(2,1)S(1)} %get-tuple-element.38), channel_id=1, source_target_pairs={{0,112},{16,0},{32,16},{48,32},{64,48},{80,64},{96,80},{112,96},{1... | collective-permute-start | bytes 626696 | tf_op jit(solution)/shard_map/ppermute | solution.py:342
  70.9 7.0 %collective-permute-start.23 = (bf16[272,384]{1,0:T(8,128)(2,1)S(1)}, bf16[272,384]{1,0:T(8,128)(2,1)S(1)}, u32[]{:S(2)}, u32[]{:S(2)}) collective-permute-start(bf16[272,384]{1,0:T(8,128)(2,1)S(1)} %get-tuple-element.37.refs_8_), channel_id=1, source_target_pairs={{0,16},{16,32},{32,48},{48,64},{64,80},{80,96},{96,112},{112,0},{1... | collective-permute-start | bytes 626696 | tf_op jit(solution)/shard_map/ppermute | solution.py:342
  79.3 10.5 %collective-permute-start.28 = (bf16[208,512]{1,0:T(8,128)(2,1)S(1)}, bf16[208,512]{1,0:T(8,128)(2,1)S(1)}, u32[]{:S(2)}, u32[]{:S(2)}) collective-permute-start(bf16[208,512]{1,0:T(8,128)(2,1)S(1)} %get-tuple-element.44), channel_id=1, source_target_pairs={{0,129},{1,128},{16,145},{17,144},{32,161},{33,160},{48,177},{49,1... | collective-permute-start | bytes 638984 | tf_op jit(solution)/shard_map/ppermute | solution.py:373
  80.6 5.7 %collective-permute-start.27 = (bf16[192,512]{1,0:T(8,128)(2,1)S(1)}, bf16[192,512]{1,0:T(8,128)(2,1)S(1)}, u32[]{:S(2)}, u32[]{:S(2)}) collective-permute-start(bf16[192,512]{1,0:T(8,128)(2,1)S(1)} %get-tuple-element.43), channel_id=1, source_target_pairs={{0,128},{16,144},{32,160},{48,176},{64,192},{80,208},{96,224},{112... | collective-permute-start | bytes 589832 | tf_op jit(solution)/shard_map/ppermute | solution.py:348
  80.6 9.3 %collective-permute-start.29 = (bf16[192,512]{1,0:T(8,128)(2,1)S(1)}, bf16[192,512]{1,0:T(8,128)(2,1)S(1)}, u32[]{:S(2)}, u32[]{:S(2)}) collective-permute-start(bf16[192,512]{1,0:T(8,128)(2,1)S(1)} %get-tuple-element.45), channel_id=1, source_target_pairs={{0,1},{1,0},{2,3},{3,2},{4,5},{5,4},{6,7},{7,6},{8,9},{9,8},{10,11... | collective-permute-start | bytes 589832 | tf_op jit(solution)/shard_map/ppermute | solution.py:364

commit v4 on v3

--- a/solution.py
+++ b/solution.py
@@ -160,30 +160,46 @@
         [jax.ShapeDtypeStruct((HALF // 2, PAIR), BF16)] * 2,
         (rows, panel),
         after,
-    )
-
-
-def z_kernel(steps, rows_ref, panel_ref, *refs):
-    received, outs = refs[: -len(steps)], refs[-len(steps) :]
+        cost=3000000000.0,
+    )
+
+
+def z_product_kernel(steps, rows_ref, panel_ref, *outs):
     left = panel_ref[:HALF, :]
-    for i, dz in enumerate(steps):
-        total = product(left, rows_ref[place(dz)])
-        count = received[i].shape[0]
+    for out, dz in zip(outs, steps):
+        out[...] = product(left, rows_ref[place(dz)])
+
+
+def z_product(rows, panel, steps, after):
+    return call(
+        functools.partial(z_product_kernel, steps),
+        [jax.ShapeDtypeStruct((HALF, PAIR), F32)] * len(steps),
+        (rows, panel),
+        after,
+        cost=1000000000.0,
+    )
+
+
+def z_add_kernel(*refs):
+    n = len(refs) // 3
+    for i, (ready, received, out) in enumerate(zip(refs[:n], refs[n : 2 * n], refs[2 * n :])):
+        count = received.shape[0]
         if count == HALF:
-            total = plus(total, received[i])
-        elif dz < 0:
-            total = jnp.concatenate([plus(total[:count], received[i]), total[count:]], axis=0)
-        else:
-            total = jnp.concatenate([total[:-count], plus(total[-count:], received[i])], axis=0)
-        outs[i][...] = total.astype(BF16)
-
-
-def z_step(rows, panel, steps, received, after):
-    return call(
-        functools.partial(z_kernel, steps),
-        [jax.ShapeDtypeStruct((HALF, PAIR), BF16)] * len(steps),
-        (rows, panel, *received),
-        after,
+            out[...] = plus(ready[...], received).astype(BF16)
+            continue
+        low = slice(0, count) if i == 0 else slice(HALF - count, HALF)
+        rest = slice(count, HALF) if i == 0 else slice(0, HALF - count)
+        out[low, :] = plus(ready[low, :], received).astype(BF16)
+        out[rest, :] = ready[rest, :].astype(BF16)
+
+
+def z_step(ready, received, after):
+    return call(
+        z_add_kernel,
+        [jax.ShapeDtypeStruct((HALF, PAIR), BF16)] * 2,
+        (*ready, *received),
+        after,
+        cost=3000000000.0,
     )
 
 
@@ -199,6 +215,7 @@
         [jax.ShapeDtypeStruct((len(steps), PART + TAIL, PAIR), BF16)],
         (rows, panel),
         after,
+        cost=2000000000.0,
     )
 
 
@@ -229,6 +246,7 @@
         [jax.ShapeDtypeStruct((PART + TAIL, PAIR), BF16)] * len(steps),
         (rows, panel, *arrays, *received),
         after,
+        cost=3000000000.0,
     )
 
 
@@ -240,73 +258,120 @@
     ]
 
 
-def last_kernel(
-    at, rows_ref, near_ref, other_ref, over, x_up, x_down, z_down, z_up,
-    own_x, own_z, rhs, beside, cross, across, x_this, x_that, z_this, z_that,
-):
+def own_and_theirs():
     side = x_place()
+    return (
+        pl.ds(pl.multiple_of(side * ROWS, ROWS), ROWS),
+        pl.ds(pl.multiple_of((1 - side) * ROWS, ROWS), ROWS),
+    )
+
+
+def ahead_kernel(at, rows_ref, near_ref, other_ref, over, ready_x, ready_z):
     right = rows_ref[place(0)]
-    total = product(x_rows(near_ref, side), right)
-    total = plus_tailed(plus_tailed(plus_tailed(total, over.at[at]), x_up), x_down)
-    x_this[...], x_that[...] = halves(total[:PART])
+    ready_x[...] = plus_tailed(product(x_rows(near_ref, x_place()), right), over.at[at])
+    ready_z[...] = product(other_ref[:HALF, :], right)
+
+
+def last_ahead(rows, near, other, over, after):
+    array, at = over
+    return call(
+        functools.partial(ahead_kernel, at),
+        [
+            jax.ShapeDtypeStruct((PART + TAIL, PAIR), F32),
+            jax.ShapeDtypeStruct((HALF, PAIR), F32),
+        ],
+        (rows, near, other, array),
+        after,
+        cost=1e9,
+    )
+
+
+def z_last_kernel(ready, z_down, z_up, own, beside, cross, across, this, that):
+    this[...], that[...] = halves(plus(plus(ready[...], z_down), z_up))
+    mine, theirs = own_and_theirs()
+    own[...] = this[mine, :]
+    beside[...] = this[theirs, :].astype(BF16)
+    cross[...] = that[theirs, :].astype(BF16)
+    across[...] = that[mine, :].astype(BF16)
+
+
+def z_last(ready, z_got):
+    message = jax.ShapeDtypeStruct((ROWS, PART), BF16)
+    return call(
+        z_last_kernel,
+        [jax.ShapeDtypeStruct((ROWS, PART), F32), message, message, message],
+        (ready, *z_got),
+        scratch=[pltpu.VMEM((PAIR, PART), F32)] * 2,
+        cost=3e9,
+    )
+
+
+def x_last_kernel(ready, z_beside, up, down, own, rhs, beside, cross, across, this, that):
+    side = x_place()
+    total = plus_tailed(plus_tailed(ready[...], up), down)
+    this[...], that[...] = halves(total[:PART])
+    mine, theirs = own_and_theirs()
+    own[...] = this[mine, :]
+    for out, value in (
+        (beside, this[theirs, :]),
+        (cross, that[theirs, :]),
+        (across, that[mine, :]),
+    ):
+        out[:ROWS, :PART] = jnp.concatenate(split(value), axis=1).astype(BF16)
+    beside[:, PART:] = z_beside[...]
     tail = total[PART:]
-    total = plus(plus(product(other_ref[:HALF, :], right), z_down), z_up)
-    z_this[...], z_that[...] = halves(total)
-    mine = pl.ds(pl.multiple_of(side * ROWS, ROWS), ROWS)
-    theirs = pl.ds(pl.multiple_of((1 - side) * ROWS, ROWS), ROWS)
-    own_x[...] = x_this[mine, :]
-    own_z[...] = z_this[mine, :]
-    for out, x, z, where in (
-        (beside, x_this, z_this, theirs),
-        (cross, x_that, z_that, theirs),
-        (across, x_that, z_that, mine),
-    ):
-        high, low = split(x[where, :])
-        out[:ROWS, :] = jnp.concatenate([high, low, z[where, :]], axis=1).astype(BF16)
     lower, upper = tail[: TAIL // 2, :ROWS], tail[: TAIL // 2, ROWS:]
     rhs[...] = jnp.where(side == 0, lower, upper)
-    high, low = split(jnp.where(side == 0, upper, lower))
-    sent = jnp.concatenate([high, low], axis=0)
-    zeros = jnp.zeros((TAIL, HALF - ROWS), F32)
+    sent = jnp.concatenate(split(jnp.where(side == 0, upper, lower)), axis=0)
+    zeros = jnp.zeros((TAIL, PART - ROWS), F32)
     cross[ROWS:, :] = jnp.concatenate([sent, zeros], axis=1).astype(BF16)
 
 
-def last(rows, near, other, over, x_got, z_got, after):
-    array, at = over
-    message = jax.ShapeDtypeStruct((ROWS, HALF), BF16)
-    return call(
-        functools.partial(last_kernel, at),
+def x_last(ready, z_beside, x_got, after):
+    return call(
+        x_last_kernel,
         [
             jax.ShapeDtypeStruct((ROWS, PART // 2), F32),
-            jax.ShapeDtypeStruct((ROWS, PART), F32),
             jax.ShapeDtypeStruct((TAIL // 2, ROWS), F32),
-            message,
-            jax.ShapeDtypeStruct((ROWS + TAIL, HALF), BF16),
-            message,
+            jax.ShapeDtypeStruct((ROWS, HALF), BF16),
+            jax.ShapeDtypeStruct((ROWS + TAIL, PART), BF16),
+            jax.ShapeDtypeStruct((ROWS, PART), BF16),
         ],
-        (rows, near, other, array, *x_got, *z_got),
-        after,
-        scratch=[pltpu.VMEM((PAIR, n), F32) for n in (PART // 2, PART // 2, PART, PART)],
-    )
-
-
-def parts(message_ref):
-    value = message_ref[:ROWS, :].astype(F32)
-    quarter = HALF // 4
-    return value[:, :quarter] + value[:, quarter : 2 * quarter], value[:, 2 * quarter :]
+        (ready, z_beside, *x_got),
+        after,
+        cost=8e9,
+        scratch=[pltpu.VMEM((PAIR, PART // 2), F32)] * 2,
+    )
+
+
+def foreign_kernel(first, second, out):
+    out[...] = plus(first[...].astype(F32), second)
+
+
+def foreign_z(first, second, after):
+    return call(
+        foreign_kernel,
+        [jax.ShapeDtypeStruct(first.shape, F32)],
+        (first, second),
+        after,
+        cost=3e9,
+    )[0]
+
+
+def whole(message_ref):
+    value = message_ref[:ROWS, :PART].astype(F32)
+    return value[:, : PART // 2] + value[:, PART // 2 :]
 
 
 def finish_kernel(
-    own_x, own_z, rhs_ref, beside_ref, cross_ref, across_ref, out_ref, rhs_out
+    own_x, own_z, rhs_ref, there_z, beside, cross, across, out_ref, rhs_out
 ):
     side, row, half = x_place(), lax.axis_index("row"), lax.axis_index("col")
     y, core = row >> 1, row & 1
-    (beside_x, beside_z), (cross_x, cross_z), (across_x, across_z) = (
-        parts(r) for r in (beside_ref, cross_ref, across_ref)
-    )
+    beside_z = beside[:, PART:].astype(F32)
     for where_to, here, there, other in (
-        (half, own_x[...], beside_x, own_z[...] + beside_z),
-        (1 - half, across_x, cross_x, cross_z + across_z),
+        (half, own_x[...], whole(beside), own_z[...] + beside_z),
+        (1 - half, whole(across), whole(cross), there_z[...]),
     ):
         near = jnp.concatenate(
             [jnp.where(side == 0, here, there), jnp.where(side == 0, there, here)], axis=1
@@ -319,7 +384,7 @@
             out_ref[0, where_to, :, pl.ds(at, 128)] = jnp.concatenate(
                 [first[:, lanes], second[:, lanes]], axis=1
             )
-    tail = cross_ref[ROWS:, :].astype(F32)[:, :ROWS]
+    tail = cross[ROWS:, :].astype(F32)[:, :ROWS]
     mine = rhs_ref[...][:1]
     other = (tail[: TAIL // 2] + tail[TAIL // 2 :])[:1]
     rhs_out[0] = jnp.concatenate(
@@ -389,7 +454,7 @@
     near = collect(weights, weighted_obs, blocks, (rows,))
     other = core_swap(near)
 
-    over, z_got, x_got, after = {}, (), (), ()
+    over, z_got, x_got, ready, after = {}, (), (), (), ()
 
     def piece(*steps):
         nonlocal after
@@ -399,12 +464,17 @@
         for i, dz in enumerate(steps):
             over[dz] = (got, i)
 
+    def z_ahead(s):
+        nonlocal after, ready
+        ready = z_product(rows, other, (-s, s), after)
+        after = (ready[0],)
+
     def z_next(s):
         nonlocal after, z_got
         if s == NZ // 2:
             sent = z_first(rows, other, after)
         else:
-            sent = z_step(rows, other, (-s, s), z_got, after)
+            sent = z_step(ready, z_got, after)
         after = (sent[0],)
         z_got = (z_shift(sent[0], -1), z_shift(sent[1], 1))
 
@@ -419,19 +489,24 @@
     piece(3, -3)
     z_next(4)
     x_next(4)
+    z_ahead(3)
     z_next(3)
     piece(2, -2)
     x_next(3)
     piece(1, -1, 0)
+    z_ahead(2)
     z_next(2)
     x_next(2)
+    z_ahead(1)
     z_next(1)
     x_next(1)
-    own_x, own_z, rhs_own, beside, cross, across = last(
-        rows, near, other, over[0], x_got, z_got, after
-    )
+    ready_x, ready_z = last_ahead(rows, near, other, over[0], after)
+    own_z, beside_z, cross_z, across_z = z_last(ready_z, z_got)
+    across_z, cross_z = half_swap(across_z), cross_swap(cross_z)
+    own_x, rhs_own, beside, cross, across = x_last(ready_x, beside_z, x_got, (own_z,))
+    there_z = foreign_z(cross_z, across_z, (own_x,))
     return finish(
-        own_x, own_z, rhs_own, x_swap(beside), cross_swap(cross), half_swap(across)
+        own_x, own_z, rhs_own, there_z, x_swap(beside), cross_swap(cross), half_swap(across)
     )
 
 

time: 91.6 us -> 90.5 us (0.988)
  waiting for transfers between devices: 27.7 us -> 23.9 us
  starting transfers between devices: 43.9 us -> 45.9 us
    ppermute x15, waiting for transfers between devices: 20.1 us -> 16.3 us  [z_shift(): lax.ppermute(x, 'rep', [(a * NZ + z, a * NZ + (z + d) % NZ) for a in rang...]
    ppermute x1 -> x2, starting transfers between devices: 1.22 us -> 3.32 us  [cross_swap(): return lax.ppermute(x, ('rep', 'col'), pairs)]
    ppermute x1 -> x2, waiting for transfers between devices: 0.01 us -> 1.92 us  [cross_swap(): return lax.ppermute(x, ('rep', 'col'), pairs)]
    ppermute x2 -> x3, waiting for transfers between devices: 4.61 us -> 2.95 us  [half_swap(): return lax.ppermute(x, 'col', [(0, 1), (1, 0)])]
    pallas_call x15 -> x21, Pallas kernels: 13 us -> 13.9 us  [call(): pl.pallas_call(body, out_shape=out_shape, in_specs=[IN_VMEM] * (n + extra...]
    ppermute x2 -> x3, starting transfers between devices: 6.68 us -> 6.73 us  [half_swap(): return lax.ppermute(x, 'col', [(0, 1), (1, 0)])]
  transfers between devices with their start and end apart: 30 -> 32, of which waited for: 9 -> 14; matrix products, arithmetic and copies ran while one was open for 0% -> 0% of each run, Pallas kernels for 14% -> 17%
where the time goes in v4:
time: 90.5 us; the launch traced here: 90.2 us
  starting transfers between devices  45.9 us (51%)
  waiting for transfers between devices  23.9 us (26%)
  Pallas kernels  16.7 us (18%)
  local copies, waits for them, and re-layouts  2.8 us (3%)
    ppermute x15, starting transfers between devices, z_shift(): lax.ppermute(x, 'rep', [(a * NZ + z, a * NZ + (z + d) % NZ) for a in rang...  24.4 us
    ppermute x15, waiting for transfers between devices, z_shift(): lax.ppermute(x, 'rep', [(a * NZ + z, a * NZ + (z + d) % NZ) for a in rang...  16.3 us
    pallas_call x21, Pallas kernels, call(): pl.pallas_call(body, out_shape=out_shape, in_specs=[IN_VMEM] * (n + extra...  13.9 us
    ppermute x6, starting transfers between devices, y_shift(): lax.ppermute(x, 'row', [(y * 2 + c, (y + d) % 4 * 2 + c) for y in range(4...  7.84 us
    ppermute x3, starting transfers between devices, half_swap(): return lax.ppermute(x, 'col', [(0, 1), (1, 0)])  6.73 us
    ppermute x5, starting transfers between devices, x_swap(): lax.ppermute(x, 'rep', [(a * NZ + z, (1 - a) * NZ + z) for a in range(2)...  3.47 us
    ppermute x2, starting transfers between devices, cross_swap(): return lax.ppermute(x, ('rep', 'col'), pairs)  3.32 us
    ppermute x3, waiting for transfers between devices, half_swap(): return lax.ppermute(x, 'col', [(0, 1), (1, 0)])  2.95 us
  transfers between devices with their start and end apart: 32, of which 14 were waited for; matrix products, arithmetic and copies ran while one was open for 0% of the time, Pallas kernels for 17%

profile of v4, /device:TPU:16, one launch (start us, length us, event | category | flops | bytes accessed | tf_op | source)
XLA Modules:
  0.0 90.2 jit_solution(14335216838405517006)
XLA Ops:
  0.6 3.1 %collective-permute-start = (bf16[64,1024]{1,0:T(8,128)(2,1)}, bf16[64,1024]{1,0:T(8,128)(2,1)S(1)}, u32[]{:S(2)}, u32[]{:S(2)}) collective-permute-start(bf16[64,1024]{1,0:T(8,128)(2,1)} %bitcast.5), channel_id=1, source_target_pairs={{0,1},{1,0},{2,3},{3,2},{4,5},{5,4},{6,7},{7,6},{8,9},{9,8},{10,11... | collective-permute-start | bytes 393224 | tf_op jit(solution)/shard_map/ppermute | solution.py:429
  3.8 1.3 %collective-permute-start.5 = (bf16[64,1024]{1,0:T(8,128)(2,1)}, bf16[64,1024]{1,0:T(8,128)(2,1)S(1)}, u32[]{:S(2)}, u32[]{:S(2)}) collective-permute-start(bf16[64,1024]{1,0:T(8,128)(2,1)} %bitcast.6), channel_id=1, source_target_pairs={{0,4},{2,6},{4,8},{6,10},{8,12},{10,14},{12,0},{14,2},{1,5},{3,7},... | collective-permute-start | bytes 393224 | tf_op jit(solution)/shard_map/ppermute | solution.py:419
  5.7 1.1 %collective-permute-start.1 = (bf16[64,1024]{1,0:T(8,128)(2,1)}, bf16[64,1024]{1,0:T(8,128)(2,1)S(1)}, u32[]{:S(2)}, u32[]{:S(2)}) collective-permute-start(bf16[64,1024]{1,0:T(8,128)(2,1)} %bitcast.8), channel_id=1, source_target_pairs={{0,12},{2,14},{4,0},{6,2},{8,4},{10,6},{12,8},{14,10},{1,13},{3,15... | collective-permute-start | bytes 393224 | tf_op jit(solution)/shard_map/ppermute | solution.py:419
  6.7 1.0 %collective-permute-done.refs_3_ = bf16[64,1024]{1,0:T(8,128)(2,1)S(1)} collective-permute-done((bf16[64,1024]{1,0:T(8,128)(2,1)}, bf16[64,1024]{1,0:T(8,128)(2,1)S(1)}, u32[]{:S(2)}, u32[]{:S(2)}) %collective-permute-start) | collective-permute-done | bytes 131104 | tf_op jit(solution)/shard_map/ppermute | solution.py:429
  7.7 1.3 %collective-permute-start.6 = (bf16[64,1024]{1,0:T(8,128)(2,1)S(1)}, bf16[64,1024]{1,0:T(8,128)(2,1)S(1)}, u32[]{:S(2)}, u32[]{:S(2)}) collective-permute-start(bf16[64,1024]{1,0:T(8,128)(2,1)S(1)} %collective-permute-done.refs_3_), channel_id=1, source_target_pairs={{0,4},{2,6},{4,8},{6,10},{8,12},{10,14},{12,0},{14,2},{1,5},{3,7},... | collective-permute-start | bytes 393224 | tf_op jit(solution)/shard_map/ppermute | solution.py:419
  9.0 1.6 %collective-permute-start.4 = (bf16[64,1024]{1,0:T(8,128)(2,1)S(1)}, bf16[64,1024]{1,0:T(8,128)(2,1)S(1)}, u32[]{:S(2)}, u32[]{:S(2)}) collective-permute-start(bf16[64,1024]{1,0:T(8,128)(2,1)S(1)} %collective-permute-done.refs_3_), channel_id=1, source_target_pairs={{0,8},{2,10},{4,12},{6,14},{8,0},{10,2},{12,4},{14,6},{1,9},{3,11}... | collective-permute-start | bytes 393224 | tf_op jit(solution)/shard_map/ppermute | solution.py:419
  10.6 2.0 %collective-permute-start.2 = (bf16[64,1024]{1,0:T(8,128)(2,1)S(1)}, bf16[64,1024]{1,0:T(8,128)(2,1)S(1)}, u32[]{:S(2)}, u32[]{:S(2)}) collective-permute-start(bf16[64,1024]{1,0:T(8,128)(2,1)S(1)} %collective-permute-done.refs_3_), channel_id=1, source_target_pairs={{0,12},{2,14},{4,0},{6,2},{8,4},{10,6},{12,8},{14,10},{1,13},{3,15... | collective-permute-start | bytes 393224 | tf_op jit(solution)/shard_map/ppermute | solution.py:419
  12.6 2.8 %copy-done = bf16[1024,3072]{1,0:T(8,128)(2,1)S(1)} copy-done((bf16[1024,3072]{1,0:T(8,128)(2,1)S(1)}, bf16[1024,3072]{1,0:T(8,128)(2,1)}, u32[]{:S(2)}) %copy-start) | copy-done | bytes 6291480
  15.3 2.3 %shard_map.68.refs_10_.refs_0_ = bf16[8,1024,384]{2,1,0:T(8,128)(2,1)S(1)} custom-call(bf16[1024,3072]{1,0:T(8,128)(2,1)S(1)} %copy-done, bf16[1024,3072]{1,0:T(8,128)(2,1)S(1)} %copy-done), custom_call_target="tpu_custom_call" | custom-call | bytes 12582912 | tf_op jit(solution)/shard_map/pallas_call | solution.py:76
  18.3 0.9 %collective-permute-done.2.refs_5_ = bf16[64,1024]{1,0:T(8,128)(2,1)S(1)} collective-permute-done((bf16[64,1024]{1,0:T(8,128)(2,1)S(1)}, bf16[64,1024]{1,0:T(8,128)(2,1)S(1)}, u32[]{:S(2)}, u32[]{:S(2)}) %collective-permute-start.2) | collective-permute-done | bytes 131104 | tf_op jit(solution)/shard_map/ppermute | solution.py:419
  19.9 0.7 collective-permute-start.9
  20.6 0.8 shard_map.72.refs_2_
  21.4 1.5 %collective-permute-start.8 = (bf16[2,272,384]{2,1,0:T(8,128)(2,1)S(1)}, bf16[2,272,384]{2,1,0:T(8,128)(2,1)S(1)}, u32[]{:S(2)}, u32[]{:S(2)}) collective-permute-start(bf16[2,272,384]{2,1,0:T(8,128)(2,1)S(1)} %shard_map.72.refs_2_), channel_id=1, source_target_pairs={{0,128},{16,144},{32,160},{48,176},{64,192},{80,208},{96,224},{112... | collective-permute-start | bytes 1253384 | tf_op jit(solution)/shard_map/ppermute | solution.py:413
  22.9 0.7 shard_map.73
  23.6 2.0 %collective-permute-start.12 = (bf16[256,384]{1,0:T(8,128)(2,1)S(1)}, bf16[256,384]{1,0:T(8,128)(2,1)S(1)}, u32[]{:S(2)}, u32[]{:S(2)}) collective-permute-start(bf16[256,384]{1,0:T(8,128)(2,1)S(1)} %get-tuple-element.40), channel_id=1, source_target_pairs={{0,16},{16,32},{32,48},{48,64},{64,80},{80,96},{96,112},{112,0},{1... | collective-permute-start | bytes 589832 | tf_op jit(solution)/shard_map/ppermute | solution.py:407
  25.6 4.0 %collective-permute-start.11 = (bf16[256,384]{1,0:T(8,128)(2,1)S(1)}, bf16[256,384]{1,0:T(8,128)(2,1)S(1)}, u32[]{:S(2)}, u32[]{:S(2)}) collective-permute-start(bf16[256,384]{1,0:T(8,128)(2,1)S(1)} %get-tuple-element.37.refs_3_), channel_id=1, source_target_pairs={{0,112},{16,0},{32,16},{48,32},{64,48},{80,64},{96,80},{112,96},{1... | collective-permute-start | bytes 589832 | tf_op jit(solution)/shard_map/ppermute | solution.py:407
  30.6 1.3 %shard_map.75 = (f32[512,384]{1,0:T(8,128)S(1)}, f32[512,384]{1,0:T(8,128)S(1)}) custom-call(bf16[8,1024,384]{2,1,0:T(8,128)(2,1)S(1)} %shard_map.68.refs_10_.refs_0_, bf16[528,1024]{1,0:T(8,128)(2,1)S(1)} %collective-permute-done.7.refs_1_.refs_2_, bf16[272,384]{1,0:T(8,128)(2,1)S(1)} %shard_map.74.refs_2_), custom_call_target="tpu_custom_call" | custom-call | flops 1000000000 | bytes 1 | tf_op jit(solution)/shard_map/pallas_call | solution.py:27
  31.9 2.7 %collective-permute-done.12.refs_3_ = bf16[256,384]{1,0:T(8,128)(2,1)S(1)} collective-permute-done((bf16[256,384]{1,0:T(8,128)(2,1)S(1)}, bf16[256,384]{1,0:T(8,128)(2,1)S(1)}, u32[]{:S(2)}, u32[]{:S(2)}) %collective-permute-start.12) | collective-permute-done | bytes 196640 | tf_op jit(solution)/shard_map/ppermute | solution.py:407
  34.8 3.2 %collective-permute-start.17 = (bf16[512,384]{1,0:T(8,128)(2,1)S(1)}, bf16[512,384]{1,0:T(8,128)(2,1)S(1)}, u32[]{:S(2)}, u32[]{:S(2)}) collective-permute-start(bf16[512,384]{1,0:T(8,128)(2,1)S(1)} %get-tuple-element.41.refs_2_), channel_id=1, source_target_pairs={{0,112},{16,0},{32,16},{48,32},{64,48},{80,64},{96,80},{112,96},{1... | collective-permute-start | bytes 1179656 | tf_op jit(solution)/shard_map/ppermute | solution.py:407
  38.0 0.8 shard_map.77.refs_4_
  39.4 1.0 %collective-permute-done.10.refs_3_ = bf16[272,384]{1,0:T(8,128)(2,1)S(1)} collective-permute-done((bf16[272,384]{1,0:T(8,128)(2,1)S(1)}, bf16[272,384]{1,0:T(8,128)(2,1)S(1)}, u32[]{:S(2)}, u32[]{:S(2)}) %collective-permute-start.10) | collective-permute-done | bytes 208928 | tf_op jit(solution)/shard_map/ppermute | solution.py:407
  40.4 0.8 shard_map.78
  41.3 1.1 %shard_map.79.refs_2_ = bf16[3,272,384]{2,1,0:T(8,128)(2,1)S(1)} custom-call(bf16[8,1024,384]{2,1,0:T(8,128)(2,1)S(1)} %shard_map.68.refs_10_.refs_0_, bf16[528,1024]{1,0:T(8,128)(2,1)S(1)} %shard_map.70.refs_1_, bf16[272,384]{1,0:T(8,128)(2,1)S(1)} %get-tuple-element.42.refs_2_), custom_call_target="tpu_custom_call" | custom-call | flops 2000000000 | bytes 1 | tf_op jit(solution)/shard_map/pallas_call | solution.py:27
  42.3 3.3 %collective-permute-start.16 = (bf16[272,384]{1,0:T(8,128)(2,1)S(1)}, bf16[272,384]{1,0:T(8,128)(2,1)S(1)}, u32[]{:S(2)}, u32[]{:S(2)}) collective-permute-start(bf16[272,384]{1,0:T(8,128)(2,1)S(1)} %get-tuple-element.43), channel_id=1, source_target_pairs={{0,112},{16,0},{32,16},{48,32},{64,48},{80,64},{96,80},{112,96},{1... | collective-permute-start | bytes 626696 | tf_op jit(solution)/shard_map/ppermute | solution.py:407
  45.6 1.3 %shard_map.80 = (f32[512,384]{1,0:T(8,128)S(1)}, f32[512,384]{1,0:T(8,128)S(1)}) custom-call(bf16[8,1024,384]{2,1,0:T(8,128)(2,1)S(1)} %shard_map.68.refs_10_.refs_0_, bf16[528,1024]{1,0:T(8,128)(2,1)S(1)} %collective-permute-done.7.refs_1_.refs_2_, bf16[3,272,384]{2,1,0:T(8,128)(2,1)S(1)} %shard_map.79.refs_2_), custom_call_target="tpu_custom_call" | custom-call | flops 1000000000 | bytes 1 | tf_op jit(solution)/shard_map/pallas_call | solution.py:27
  46.9 1.9 %collective-permute-done.18.refs_3_ = bf16[512,384]{1,0:T(8,128)(2,1)S(1)} collective-permute-done((bf16[512,384]{1,0:T(8,128)(2,1)S(1)}, bf16[512,384]{1,0:T(8,128)(2,1)S(1)}, u32[]{:S(2)}, u32[]{:S(2)}) %collective-permute-start.18) | collective-permute-done | bytes 393248 | tf_op jit(solution)/shard_map/ppermute | solution.py:407
  49.0 1.7 %collective-permute-start.22 = (bf16[512,384]{1,0:T(8,128)(2,1)S(1)}, bf16[512,384]{1,0:T(8,128)(2,1)S(1)}, u32[]{:S(2)}, u32[]{:S(2)}) collective-permute-start(bf16[512,384]{1,0:T(8,128)(2,1)S(1)} %get-tuple-element.52), channel_id=1, source_target_pairs={{0,16},{16,32},{32,48},{48,64},{64,80},{80,96},{96,112},{112,0},{1... | collective-permute-start | bytes 1179656 | tf_op jit(solution)/shard_map/ppermute | solution.py:407
  50.7 1.6 %collective-permute-start.21 = (bf16[512,384]{1,0:T(8,128)(2,1)S(1)}, bf16[512,384]{1,0:T(8,128)(2,1)S(1)}, u32[]{:S(2)}, u32[]{:S(2)}) collective-permute-start(bf16[512,384]{1,0:T(8,128)(2,1)S(1)} %get-tuple-element.47.refs_5_), channel_id=1, source_target_pairs={{0,112},{16,0},{32,16},{48,32},{64,48},{80,64},{96,80},{112,96},{1... | collective-permute-start | bytes 1179656 | tf_op jit(solution)/shard_map/ppermute | solution.py:407
  53.3 0.8 shard_map.82
  54.1 2.1 %collective-permute-start.20 = (bf16[272,384]{1,0:T(8,128)(2,1)S(1)}, bf16[272,384]{1,0:T(8,128)(2,1)S(1)}, u32[]{:S(2)}, u32[]{:S(2)}) collective-permute-start(bf16[272,384]{1,0:T(8,128)(2,1)S(1)} %get-tuple-element.49), channel_id=1, source_target_pairs={{0,112},{16,0},{32,16},{48,32},{64,48},{80,64},{96,80},{112,96},{1... | collective-permute-start | bytes 626696 | tf_op jit(solution)/shard_map/ppermute | solution.py:407
  56.6 1.3 %shard_map.83 = (f32[512,384]{1,0:T(8,128)S(1)}, f32[512,384]{1,0:T(8,128)S(1)}) custom-call(bf16[8,1024,384]{2,1,0:T(8,128)(2,1)S(1)} %shard_map.68.refs_10_.refs_0_, bf16[528,1024]{1,0:T(8,128)(2,1)S(1)} %collective-permute-done.7.refs_1_.refs_2_, bf16[272,384]{1,0:T(8,128)(2,1)S(1)} %get-tuple-element.48.refs_2_), custom_call_target="tpu_custom_call" | custom-call | flops 1000000000 | bytes 1 | tf_op jit(solution)/shard_map/pallas_call | solution.py:27
  57.8 4.5 %collective-permute-done.22.refs_3_ = bf16[512,384]{1,0:T(8,128)(2,1)S(1)} collective-permute-done((bf16[512,384]{1,0:T(8,128)(2,1)S(1)}, bf16[512,384]{1,0:T(8,128)(2,1)S(1)}, u32[]{:S(2)}, u32[]{:S(2)}) %collective-permute-start.22) | collective-permute-done | bytes 393248 | tf_op jit(solution)/shard_map/ppermute | solution.py:407
  62.6 1.4 %collective-permute-start.24 = (bf16[512,384]{1,0:T(8,128)(2,1)S(1)}, bf16[512,384]{1,0:T(8,128)(2,1)S(1)}, u32[]{:S(2)}, u32[]{:S(2)}) collective-permute-start(bf16[512,384]{1,0:T(8,128)(2,1)S(1)} %get-tuple-element.57), channel_id=1, source_target_pairs={{0,16},{16,32},{32,48},{48,64},{64,80},{80,96},{96,112},{112,0},{1... | collective-permute-start | bytes 1179656 | tf_op jit(solution)/shard_map/ppermute | solution.py:407
  64.0 1.9 %collective-permute-start.23 = (bf16[512,384]{1,0:T(8,128)(2,1)S(1)}, bf16[512,384]{1,0:T(8,128)(2,1)S(1)}, u32[]{:S(2)}, u32[]{:S(2)}) collective-permute-start(bf16[512,384]{1,0:T(8,128)(2,1)S(1)} %get-tuple-element.53.refs_5_), channel_id=1, source_target_pairs={{0,112},{16,0},{32,16},{48,32},{64,48},{80,64},{96,80},{112,96},{1... | collective-permute-start | bytes 1179656 | tf_op jit(solution)/shard_map/ppermute | solution.py:407
  65.9 1.0 %collective-permute-done.19.refs_3_ = bf16[272,384]{1,0:T(8,128)(2,1)S(1)} collective-permute-done((bf16[272,384]{1,0:T(8,128)(2,1)S(1)}, bf16[272,384]{1,0:T(8,128)(2,1)S(1)}, u32[]{:S(2)}, u32[]{:S(2)}) %collective-permute-start.19) | collective-permute-done | bytes 208928 | tf_op jit(solution)/shard_map/ppermute | solution.py:407
  66.8 0.8 shard_map.85
  67.6 1.8 %collective-permute-start.26 = (bf16[272,384]{1,0:T(8,128)(2,1)S(1)}, bf16[272,384]{1,0:T(8,128)(2,1)S(1)}, u32[]{:S(2)}, u32[]{:S(2)}) collective-permute-start(bf16[272,384]{1,0:T(8,128)(2,1)S(1)} %get-tuple-element.59), channel_id=1, source_target_pairs={{0,112},{16,0},{32,16},{48,32},{64,48},{80,64},{96,80},{112,96},{1... | collective-permute-start | bytes 626696 | tf_op jit(solution)/shard_map/ppermute | solution.py:407
  69.7 1.0 %shard_map.86 = (f32[272,384]{1,0:T(8,128)S(1)}, f32[512,384]{1,0:T(8,128)S(1)}) custom-call(bf16[8,1024,384]{2,1,0:T(8,128)(2,1)S(1)} %shard_map.68.refs_10_.refs_0_, bf16[528,1024]{1,0:T(8,128)(2,1)S(1)} %shard_map.70.refs_1_, bf16[528,1024]{1,0:T(8,128)(2,1)S(1)} %collective-permute-done.7.refs_1_.refs_2_, ...), custom_call_target="tpu_custom_call" | custom-call | flops 1000000000 | bytes 1 | tf_op jit(solution)/shard_map/pallas_call | solution.py:27
  70.7 4.9 %collective-permute-done.24.refs_2_ = bf16[512,384]{1,0:T(8,128)(2,1)S(1)} collective-permute-done((bf16[512,384]{1,0:T(8,128)(2,1)S(1)}, bf16[512,384]{1,0:T(8,128)(2,1)S(1)}, u32[]{:S(2)}, u32[]{:S(2)}) %collective-permute-start.24) | collective-permute-done | bytes 393248 | tf_op jit(solution)/shard_map/ppermute | solution.py:407
  76.1 1.2 %collective-permute-start.27 = (bf16[192,256]{1,0:T(8,128)(2,1)S(1)}, bf16[192,256]{1,0:T(8,128)(2,1)S(1)}, u32[]{:S(2)}, u32[]{:S(2)}) collective-permute-start(bf16[192,256]{1,0:T(8,128)(2,1)S(1)} %get-tuple-element.63), channel_id=1, source_target_pairs={{0,129},{1,128},{16,145},{17,144},{32,161},{33,160},{48,177},{49,1... | collective-permute-start | bytes 294920 | tf_op jit(solution)/shard_map/ppermute | solution.py:438
  77.3 1.5 %collective-permute-start.28 = (bf16[192,256]{1,0:T(8,128)(2,1)S(1)}, bf16[192,256]{1,0:T(8,128)(2,1)S(1)}, u32[]{:S(2)}, u32[]{:S(2)}) collective-permute-start(bf16[192,256]{1,0:T(8,128)(2,1)S(1)} %get-tuple-element.64), channel_id=1, source_target_pairs={{0,1},{1,0},{2,3},{3,2},{4,5},{5,4},{6,7},{7,6},{8,9},{9,8},{10,11... | collective-permute-start | bytes 294920 | tf_op jit(solution)/shard_map/ppermute | solution.py:429
  79.1 2.1 %collective-permute-start.31 = (bf16[192,256]{1,0:T(8,128)(2,1)S(1)}, bf16[192,256]{1,0:T(8,128)(2,1)S(1)}, u32[]{:S(2)}, u32[]{:S(2)}) collective-permute-start(bf16[192,256]{1,0:T(8,128)(2,1)S(1)} %get-tuple-element.67), channel_id=1, source_target_pairs={{0,1},{1,0},{2,3},{3,2},{4,5},{5,4},{6,7},{7,6},{8,9},{9,8},{10,11... | collective-permute-start | bytes 294920 | tf_op jit(solution)/shard_map/ppermute | solution.py:429
  81.2 2.1 %collective-permute-start.30 = (bf16[208,256]{1,0:T(8,128)(2,1)S(1)}, bf16[208,256]{1,0:T(8,128)(2,1)S(1)}, u32[]{:S(2)}, u32[]{:S(2)}) collective-permute-start(bf16[208,256]{1,0:T(8,128)(2,1)S(1)} %get-tuple-element.66), channel_id=1, source_target_pairs={{0,129},{1,128},{16,145},{17,144},{32,161},{33,160},{48,177},{49,1... | collective-permute-start | bytes 319496 | tf_op jit(solution)/shard_map/ppermute | solution.py:438
  83.3 0.8 collective-permute-done.27.refs_0_
  84.4 1.7 %collective-permute-done.31.refs_6_ = bf16[192,256]{1,0:T(8,128)(2,1)S(1)} collective-permute-done((bf16[192,256]{1,0:T(8,128)(2,1)S(1)}, bf16[192,256]{1,0:T(8,128)(2,1)S(1)}, u32[]{:S(2)}, u32[]{:S(2)}) %collective-permute-start.31) | collective-permute-done | bytes 98336 | tf_op jit(solution)/shard_map/ppermute | solution.py:429
  86.1 1.1 %collective-permute-done.30.refs_5_ = bf16[208,256]{1,0:T(8,128)(2,1)S(1)} collective-permute-done((bf16[208,256]{1,0:T(8,128)(2,1)S(1)}, bf16[208,256]{1,0:T(8,128)(2,1)S(1)}, u32[]{:S(2)}, u32[]{:S(2)}) %collective-permute-start.30) | collective-permute-done | bytes 106528 | tf_op jit(solution)/shard_map/ppermute | solution.py:438
  87.2 1.7 %collective-permute-done.29.refs_4_ = bf16[192,512]{1,0:T(8,128)(2,1)S(1)} collective-permute-done((bf16[192,512]{1,0:T(8,128)(2,1)S(1)}, bf16[192,512]{1,0:T(8,128)(2,1)S(1)}, u32[]{:S(2)}, u32[]{:S(2)}) %collective-permute-start.29) | collective-permute-done | bytes 196640 | tf_op jit(solution)/shard_map/ppermute | solution.py:413
  89.0 1.2 %shard_map.90 = (f32[1,2,192,512]{3,2,1,0:T(8,128)}, f32[1,2,192]{2,1,0:T(2,128)}) custom-call(f32[192,128]{1,0:T(8,128)S(1)} %get-tuple-element.61.refs_2_.refs_0_, f32[192,256]{1,0:T(8,128)S(1)} %get-tuple-element.60.refs_4_.refs_1_, f32[8,192]{1,0:T(8,128)S(1)} %get-tuple-element.62.refs_2_, f32[192,256]{1,0:T(8,128)S(1)} %shard_map.89.refs_3_, ...), custom_call_target="tpu_custom_call" | custom-call | flops 4000000000 | bytes 1 | tf_op jit(solution)/shard_map/pallas_call | solution.py:27
  (49 shorter events, 6.9 us)
Async XLA Ops:
  0.6 17.0 %copy-start.4 = (f32[8]{0:T(128)S(1)}, f32[8]{0:T(128)}, u32[]{:S(2)}) copy-start(f32[8]{0:T(128)} %sigma_ref.1) | copy-start | bytes 100
  0.6 7.0 %collective-permute-start = (bf16[64,1024]{1,0:T(8,128)(2,1)}, bf16[64,1024]{1,0:T(8,128)(2,1)S(1)}, u32[]{:S(2)}, u32[]{:S(2)}) collective-permute-start(bf16[64,1024]{1,0:T(8,128)(2,1)} %bitcast.5), channel_id=1, source_target_pairs={{0,1},{1,0},{2,3},{3,2},{4,5},{5,4},{6,7},{7,6},{8,9},{9,8},{10,11... | collective-permute-start | bytes 393224 | tf_op jit(solution)/shard_map/ppermute | solution.py:429
  3.8 6.8 %collective-permute-start.5 = (bf16[64,1024]{1,0:T(8,128)(2,1)}, bf16[64,1024]{1,0:T(8,128)(2,1)S(1)}, u32[]{:S(2)}, u32[]{:S(2)}) collective-permute-start(bf16[64,1024]{1,0:T(8,128)(2,1)} %bitcast.6), channel_id=1, source_target_pairs={{0,4},{2,6},{4,8},{6,10},{8,12},{10,14},{12,0},{14,2},{1,5},{3,7},... | collective-permute-start | bytes 393224 | tf_op jit(solution)/shard_map/ppermute | solution.py:419
  5.0 13.2 %collective-permute-start.3 = (bf16[64,1024]{1,0:T(8,128)(2,1)}, bf16[64,1024]{1,0:T(8,128)(2,1)S(1)}, u32[]{:S(2)}, u32[]{:S(2)}) collective-permute-start(bf16[64,1024]{1,0:T(8,128)(2,1)} %bitcast.7), channel_id=1, source_target_pairs={{0,8},{2,10},{4,12},{6,14},{8,0},{10,2},{12,4},{14,6},{1,9},{3,11}... | collective-permute-start | bytes 393224 | tf_op jit(solution)/shard_map/ppermute | solution.py:419
  5.7 12.6 %collective-permute-start.1 = (bf16[64,1024]{1,0:T(8,128)(2,1)}, bf16[64,1024]{1,0:T(8,128)(2,1)S(1)}, u32[]{:S(2)}, u32[]{:S(2)}) collective-permute-start(bf16[64,1024]{1,0:T(8,128)(2,1)} %bitcast.8), channel_id=1, source_target_pairs={{0,12},{2,14},{4,0},{6,2},{8,4},{10,6},{12,8},{14,10},{1,13},{3,15... | collective-permute-start | bytes 393224 | tf_op jit(solution)/shard_map/ppermute | solution.py:419
  7.7 10.6 %collective-permute-start.6 = (bf16[64,1024]{1,0:T(8,128)(2,1)S(1)}, bf16[64,1024]{1,0:T(8,128)(2,1)S(1)}, u32[]{:S(2)}, u32[]{:S(2)}) collective-permute-start(bf16[64,1024]{1,0:T(8,128)(2,1)S(1)} %collective-permute-done.refs_3_), channel_id=1, source_target_pairs={{0,4},{2,6},{4,8},{6,10},{8,12},{10,14},{12,0},{14,2},{1,5},{3,7},... | collective-permute-start | bytes 393224 | tf_op jit(solution)/shard_map/ppermute | solution.py:419
  9.0 9.3 %collective-permute-start.4 = (bf16[64,1024]{1,0:T(8,128)(2,1)S(1)}, bf16[64,1024]{1,0:T(8,128)(2,1)S(1)}, u32[]{:S(2)}, u32[]{:S(2)}) collective-permute-start(bf16[64,1024]{1,0:T(8,128)(2,1)S(1)} %collective-permute-done.refs_3_), channel_id=1, source_target_pairs={{0,8},{2,10},{4,12},{6,14},{8,0},{10,2},{12,4},{14,6},{1,9},{3,11}... | collective-permute-start | bytes 393224 | tf_op jit(solution)/shard_map/ppermute | solution.py:419
  10.6 8.6 %collective-permute-start.2 = (bf16[64,1024]{1,0:T(8,128)(2,1)S(1)}, bf16[64,1024]{1,0:T(8,128)(2,1)S(1)}, u32[]{:S(2)}, u32[]{:S(2)}) collective-permute-start(bf16[64,1024]{1,0:T(8,128)(2,1)S(1)} %collective-permute-done.refs_3_), channel_id=1, source_target_pairs={{0,12},{2,14},{4,0},{6,2},{8,4},{10,6},{12,8},{14,10},{1,13},{3,15... | collective-permute-start | bytes 393224 | tf_op jit(solution)/shard_map/ppermute | solution.py:419
  12.6 2.8 %copy-start = (bf16[1024,3072]{1,0:T(8,128)(2,1)S(1)}, bf16[1024,3072]{1,0:T(8,128)(2,1)}, u32[]{:S(2)}) copy-start(bf16[1024,3072]{1,0:T(8,128)(2,1)} %second_ref.1) | copy-start | bytes 18874372
  15.3 2.3 %copy-start.2 = (f32[1024]{0:T(1024)S(1)}, f32[1024]{0:T(1024)}, u32[]{:S(2)}) copy-start(f32[1024]{0:T(1024)} %param.7) | copy-start | bytes 12292
  15.3 2.3 %copy-start.3 = (s32[1024]{0:T(1024)S(1)}, s32[1024]{0:T(1024)}, u32[]{:S(2)}) copy-start(s32[1024]{0:T(1024)} %param.8) | copy-start | bytes 12292
  15.3 3.8 %copy-start.1 = (bf16[1024,1,64]{0,2,1:T(8,128)(2,1)S(1)}, bf16[1024,1,64]{0,2,1:T(8,128)(2,1)}, u32[]{:S(2)}) copy-start(bf16[1024,1,64]{0,2,1:T(8,128)(2,1)} %param.6) | copy-start | bytes 393220
  19.4 3.5 %collective-permute-start.7 = (bf16[528,1024]{1,0:T(8,128)(2,1)S(1)}, bf16[528,1024]{1,0:T(8,128)(2,1)S(1)}, u32[]{:S(2)}, u32[]{:S(2)}) collective-permute-start(bf16[528,1024]{1,0:T(8,128)(2,1)S(1)} %shard_map.70.refs_1_), channel_id=1, source_target_pairs={{0,2},{2,0},{4,6},{6,4},{8,10},{10,8},{12,14},{14,12},{1,3},{3,1},... | collective-permute-start | bytes 3244040 | tf_op jit(solution)/shard_map/ppermute | solution.py:425
  19.9 9.7 %collective-permute-start.9 = (bf16[1,272,384]{2,1,0:T(8,128)(2,1)S(1)}, bf16[1,272,384]{2,1,0:T(8,128)(2,1)S(1)}, u32[]{:S(2)}, u32[]{:S(2)}) collective-permute-start(bf16[1,272,384]{2,1,0:T(8,128)(2,1)S(1)} %shard_map.71.refs_2_), channel_id=1, source_target_pairs={{0,128},{16,144},{32,160},{48,176},{64,192},{80,208},{96,224},{112... | collective-permute-start | bytes 626696 | tf_op jit(solution)/shard_map/ppermute | solution.py:413
  21.4 18.0 %collective-permute-start.8 = (bf16[2,272,384]{2,1,0:T(8,128)(2,1)S(1)}, bf16[2,272,384]{2,1,0:T(8,128)(2,1)S(1)}, u32[]{:S(2)}, u32[]{:S(2)}) collective-permute-start(bf16[2,272,384]{2,1,0:T(8,128)(2,1)S(1)} %shard_map.72.refs_2_), channel_id=1, source_target_pairs={{0,128},{16,144},{32,160},{48,176},{64,192},{80,208},{96,224},{112... | collective-permute-start | bytes 1253384 | tf_op jit(solution)/shard_map/ppermute | solution.py:413
  23.6 10.9 %collective-permute-start.12 = (bf16[256,384]{1,0:T(8,128)(2,1)S(1)}, bf16[256,384]{1,0:T(8,128)(2,1)S(1)}, u32[]{:S(2)}, u32[]{:S(2)}) collective-permute-start(bf16[256,384]{1,0:T(8,128)(2,1)S(1)} %get-tuple-element.40), channel_id=1, source_target_pairs={{0,16},{16,32},{32,48},{48,64},{64,80},{80,96},{96,112},{112,0},{1... | collective-permute-start | bytes 589832 | tf_op jit(solution)/shard_map/ppermute | solution.py:407
  25.6 8.9 %collective-permute-start.11 = (bf16[256,384]{1,0:T(8,128)(2,1)S(1)}, bf16[256,384]{1,0:T(8,128)(2,1)S(1)}, u32[]{:S(2)}, u32[]{:S(2)}) collective-permute-start(bf16[256,384]{1,0:T(8,128)(2,1)S(1)} %get-tuple-element.37.refs_3_), channel_id=1, source_target_pairs={{0,112},{16,0},{32,16},{48,32},{64,48},{80,64},{96,80},{112,96},{1... | collective-permute-start | bytes 589832 | tf_op jit(solution)/shard_map/ppermute | solution.py:407
  30.1 10.3 %collective-permute-start.10 = (bf16[272,384]{1,0:T(8,128)(2,1)S(1)}, bf16[272,384]{1,0:T(8,128)(2,1)S(1)}, u32[]{:S(2)}, u32[]{:S(2)}) collective-permute-start(bf16[272,384]{1,0:T(8,128)(2,1)S(1)} %shard_map.74.refs_2_), channel_id=1, source_target_pairs={{0,16},{16,32},{32,48},{48,64},{64,80},{80,96},{96,112},{112,0},{1... | collective-permute-start | bytes 626696 | tf_op jit(solution)/shard_map/ppermute | solution.py:407
  34.7 14.1 %collective-permute-start.18 = (bf16[512,384]{1,0:T(8,128)(2,1)S(1)}, bf16[512,384]{1,0:T(8,128)(2,1)S(1)}, u32[]{:S(2)}, u32[]{:S(2)}) collective-permute-start(bf16[512,384]{1,0:T(8,128)(2,1)S(1)} %get-tuple-element.46), channel_id=1, source_target_pairs={{0,16},{16,32},{32,48},{48,64},{64,80},{80,96},{96,112},{112,0},{1... | collective-permute-start | bytes 1179656 | tf_op jit(solution)/shard_map/ppermute | solution.py:407
  34.8 14.1 %collective-permute-start.17 = (bf16[512,384]{1,0:T(8,128)(2,1)S(1)}, bf16[512,384]{1,0:T(8,128)(2,1)S(1)}, u32[]{:S(2)}, u32[]{:S(2)}) collective-permute-start(bf16[512,384]{1,0:T(8,128)(2,1)S(1)} %get-tuple-element.41.refs_2_), channel_id=1, source_target_pairs={{0,112},{16,0},{32,16},{48,32},{64,48},{80,64},{96,80},{112,96},{1... | collective-permute-start | bytes 1179656 | tf_op jit(solution)/shard_map/ppermute | solution.py:407
  38.7 14.6 %collective-permute-start.14 = (bf16[2,272,384]{2,1,0:T(8,128)(2,1)S(1)}, bf16[2,272,384]{2,1,0:T(8,128)(2,1)S(1)}, u32[]{:S(2)}, u32[]{:S(2)}) collective-permute-start(bf16[2,272,384]{2,1,0:T(8,128)(2,1)S(1)} %shard_map.77.refs_4_), channel_id=1, source_target_pairs={{0,128},{16,144},{32,160},{48,176},{64,192},{80,208},{96,224},{112... | collective-permute-start | bytes 1253384 | tf_op jit(solution)/shard_map/ppermute | solution.py:413
  41.2 12.1 %collective-permute-start.15 = (bf16[272,384]{1,0:T(8,128)(2,1)S(1)}, bf16[272,384]{1,0:T(8,128)(2,1)S(1)}, u32[]{:S(2)}, u32[]{:S(2)}) collective-permute-start(bf16[272,384]{1,0:T(8,128)(2,1)S(1)} %get-tuple-element.42.refs_2_), channel_id=1, source_target_pairs={{0,16},{16,32},{32,48},{48,64},{64,80},{80,96},{96,112},{112,0},{1... | collective-permute-start | bytes 626696 | tf_op jit(solution)/shard_map/ppermute | solution.py:407
  42.3 10.0 %collective-permute-start.16 = (bf16[272,384]{1,0:T(8,128)(2,1)S(1)}, bf16[272,384]{1,0:T(8,128)(2,1)S(1)}, u32[]{:S(2)}, u32[]{:S(2)}) collective-permute-start(bf16[272,384]{1,0:T(8,128)(2,1)S(1)} %get-tuple-element.43), channel_id=1, source_target_pairs={{0,112},{16,0},{32,16},{48,32},{64,48},{80,64},{96,80},{112,96},{1... | collective-permute-start | bytes 626696 | tf_op jit(solution)/shard_map/ppermute | solution.py:407
  49.0 13.3 %collective-permute-start.22 = (bf16[512,384]{1,0:T(8,128)(2,1)S(1)}, bf16[512,384]{1,0:T(8,128)(2,1)S(1)}, u32[]{:S(2)}, u32[]{:S(2)}) collective-permute-start(bf16[512,384]{1,0:T(8,128)(2,1)S(1)} %get-tuple-element.52), channel_id=1, source_target_pairs={{0,16},{16,32},{32,48},{48,64},{64,80},{80,96},{96,112},{112,0},{1... | collective-permute-start | bytes 1179656 | tf_op jit(solution)/shard_map/ppermute | solution.py:407
  50.7 11.7 %collective-permute-start.21 = (bf16[512,384]{1,0:T(8,128)(2,1)S(1)}, bf16[512,384]{1,0:T(8,128)(2,1)S(1)}, u32[]{:S(2)}, u32[]{:S(2)}) collective-permute-start(bf16[512,384]{1,0:T(8,128)(2,1)S(1)} %get-tuple-element.47.refs_5_), channel_id=1, source_target_pairs={{0,112},{16,0},{32,16},{48,32},{64,48},{80,64},{96,80},{112,96},{1... | collective-permute-start | bytes 1179656 | tf_op jit(solution)/shard_map/ppermute | solution.py:407
  52.3 14.5 %collective-permute-start.13 = (bf16[3,272,384]{2,1,0:T(8,128)(2,1)S(1)}, bf16[3,272,384]{2,1,0:T(8,128)(2,1)S(1)}, u32[]{:S(2)}, u32[]{:S(2)}) collective-permute-start(bf16[3,272,384]{2,1,0:T(8,128)(2,1)S(1)} %shard_map.79.refs_2_), channel_id=1, source_target_pairs={{0,128},{16,144},{32,160},{48,176},{64,192},{80,208},{96,224},{112... | collective-permute-start | bytes 1880072 | tf_op jit(solution)/shard_map/ppermute | solution.py:413
  54.1 11.8 %collective-permute-start.20 = (bf16[272,384]{1,0:T(8,128)(2,1)S(1)}, bf16[272,384]{1,0:T(8,128)(2,1)S(1)}, u32[]{:S(2)}, u32[]{:S(2)}) collective-permute-start(bf16[272,384]{1,0:T(8,128)(2,1)S(1)} %get-tuple-element.49), channel_id=1, source_target_pairs={{0,112},{16,0},{32,16},{48,32},{64,48},{80,64},{96,80},{112,96},{1... | collective-permute-start | bytes 626696 | tf_op jit(solution)/shard_map/ppermute | solution.py:407
  56.2 10.7 %collective-permute-start.19 = (bf16[272,384]{1,0:T(8,128)(2,1)S(1)}, bf16[272,384]{1,0:T(8,128)(2,1)S(1)}, u32[]{:S(2)}, u32[]{:S(2)}) collective-permute-start(bf16[272,384]{1,0:T(8,128)(2,1)S(1)} %get-tuple-element.48.refs_2_), channel_id=1, source_target_pairs={{0,16},{16,32},{32,48},{48,64},{64,80},{80,96},{96,112},{112,0},{1... | collective-permute-start | bytes 626696 | tf_op jit(solution)/shard_map/ppermute | solution.py:407
  62.6 13.1 %collective-permute-start.24 = (bf16[512,384]{1,0:T(8,128)(2,1)S(1)}, bf16[512,384]{1,0:T(8,128)(2,1)S(1)}, u32[]{:S(2)}, u32[]{:S(2)}) collective-permute-start(bf16[512,384]{1,0:T(8,128)(2,1)S(1)} %get-tuple-element.57), channel_id=1, source_target_pairs={{0,16},{16,32},{32,48},{48,64},{64,80},{80,96},{96,112},{112,0},{1... | collective-permute-start | bytes 1179656 | tf_op jit(solution)/shard_map/ppermute | solution.py:407
  64.0 11.7 %collective-permute-start.23 = (bf16[512,384]{1,0:T(8,128)(2,1)S(1)}, bf16[512,384]{1,0:T(8,128)(2,1)S(1)}, u32[]{:S(2)}, u32[]{:S(2)}) collective-permute-start(bf16[512,384]{1,0:T(8,128)(2,1)S(1)} %get-tuple-element.53.refs_5_), channel_id=1, source_target_pairs={{0,112},{16,0},{32,16},{48,32},{64,48},{80,64},{96,80},{112,96},{1... | collective-permute-start | bytes 1179656 | tf_op jit(solution)/shard_map/ppermute | solution.py:407
  67.6 11.2 %collective-permute-start.26 = (bf16[272,384]{1,0:T(8,128)(2,1)S(1)}, bf16[272,384]{1,0:T(8,128)(2,1)S(1)}, u32[]{:S(2)}, u32[]{:S(2)}) collective-permute-start(bf16[272,384]{1,0:T(8,128)(2,1)S(1)} %get-tuple-element.59), channel_id=1, source_target_pairs={{0,112},{16,0},{32,16},{48,32},{64,48},{80,64},{96,80},{112,96},{1... | collective-permute-start | bytes 626696 | tf_op jit(solution)/shard_map/ppermute | solution.py:407
  69.5 9.4 %collective-permute-start.25 = (bf16[272,384]{1,0:T(8,128)(2,1)S(1)}, bf16[272,384]{1,0:T(8,128)(2,1)S(1)}, u32[]{:S(2)}, u32[]{:S(2)}) collective-permute-start(bf16[272,384]{1,0:T(8,128)(2,1)S(1)} %get-tuple-element.54.refs_4_), channel_id=1, source_target_pairs={{0,16},{16,32},{32,48},{48,64},{64,80},{80,96},{96,112},{112,0},{1... | collective-permute-start | bytes 626696 | tf_op jit(solution)/shard_map/ppermute | solution.py:407
  76.1 8.0 %collective-permute-start.27 = (bf16[192,256]{1,0:T(8,128)(2,1)S(1)}, bf16[192,256]{1,0:T(8,128)(2,1)S(1)}, u32[]{:S(2)}, u32[]{:S(2)}) collective-permute-start(bf16[192,256]{1,0:T(8,128)(2,1)S(1)} %get-tuple-element.63), channel_id=1, source_target_pairs={{0,129},{1,128},{16,145},{17,144},{32,161},{33,160},{48,177},{49,1... | collective-permute-start | bytes 294920 | tf_op jit(solution)/shard_map/ppermute | solution.py:438
  77.3 7.1 %collective-permute-start.28 = (bf16[192,256]{1,0:T(8,128)(2,1)S(1)}, bf16[192,256]{1,0:T(8,128)(2,1)S(1)}, u32[]{:S(2)}, u32[]{:S(2)}) collective-permute-start(bf16[192,256]{1,0:T(8,128)(2,1)S(1)} %get-tuple-element.64), channel_id=1, source_target_pairs={{0,1},{1,0},{2,3},{3,2},{4,5},{5,4},{6,7},{7,6},{8,9},{9,8},{10,11... | collective-permute-start | bytes 294920 | tf_op jit(solution)/shard_map/ppermute | solution.py:429
  79.1 7.0 %collective-permute-start.31 = (bf16[192,256]{1,0:T(8,128)(2,1)S(1)}, bf16[192,256]{1,0:T(8,128)(2,1)S(1)}, u32[]{:S(2)}, u32[]{:S(2)}) collective-permute-start(bf16[192,256]{1,0:T(8,128)(2,1)S(1)} %get-tuple-element.67), channel_id=1, source_target_pairs={{0,1},{1,0},{2,3},{3,2},{4,5},{5,4},{6,7},{7,6},{8,9},{9,8},{10,11... | collective-permute-start | bytes 294920 | tf_op jit(solution)/shard_map/ppermute | solution.py:429
  81.2 6.1 %collective-permute-start.30 = (bf16[208,256]{1,0:T(8,128)(2,1)S(1)}, bf16[208,256]{1,0:T(8,128)(2,1)S(1)}, u32[]{:S(2)}, u32[]{:S(2)}) collective-permute-start(bf16[208,256]{1,0:T(8,128)(2,1)S(1)} %get-tuple-element.66), channel_id=1, source_target_pairs={{0,129},{1,128},{16,145},{17,144},{32,161},{33,160},{48,177},{49,1... | collective-permute-start | bytes 319496 | tf_op jit(solution)/shard_map/ppermute | solution.py:438
  83.3 5.7 %collective-permute-start.29 = (bf16[192,512]{1,0:T(8,128)(2,1)S(1)}, bf16[192,512]{1,0:T(8,128)(2,1)S(1)}, u32[]{:S(2)}, u32[]{:S(2)}) collective-permute-start(bf16[192,512]{1,0:T(8,128)(2,1)S(1)} %get-tuple-element.65), channel_id=1, source_target_pairs={{0,128},{16,144},{32,160},{48,176},{64,192},{80,208},{96,224},{112... | collective-permute-start | bytes 589832 | tf_op jit(solution)/shard_map/ppermute | solution.py:413

commit v5 on v4

--- a/solution.py
+++ b/solution.py
@@ -486,16 +486,16 @@
         x_got = (z_shift(sent[0], 1),) + tuple(z_shift(v, -1) for v in sent[1:])
 
     piece(4)
+    z_next(4)
     piece(3, -3)
-    z_next(4)
     x_next(4)
     z_ahead(3)
     z_next(3)
+    x_next(3)
     piece(2, -2)
-    x_next(3)
-    piece(1, -1, 0)
     z_ahead(2)
     z_next(2)
+    piece(1, -1, 0)
     x_next(2)
     z_ahead(1)
     z_next(1)

time: 90.5 us -> 89.8 us (level)
    ppermute x15, waiting for transfers between devices: 16.3 us -> 11.8 us  [z_shift(): lax.ppermute(x, 'rep', [(a * NZ + z, a * NZ + (z + d) % NZ) for a in rang...]
    ppermute x5, waiting for transfers between devices: 1.74 us -> 3.73 us  [x_swap(): lax.ppermute(x, 'rep', [(a * NZ + z, (1 - a) * NZ + z) for a in range(2)...]
    ppermute x1, waiting for transfers between devices: 0.01 us -> 1.54 us  [core_swap(): return lax.ppermute(x, 'row', [(i, i ^ 1) for i in range(8)])]
  transfers between devices with their start and end apart: 32 -> 32, of which waited for: 14 -> 17; matrix products, arithmetic and copies ran while one was open for 0% -> 0% of each run, Pallas kernels for 17% -> 17%
where the time goes in v5:
time: 89.8 us; the launch traced here: 89.5 us
  starting transfers between devices  46 us (51%)
  waiting for transfers between devices  23.3 us (26%)
  Pallas kernels  16.6 us (18%)
  local copies, waits for them, and re-layouts  2.8 us (3%)
  between operations  0.91 us (1%)
    ppermute x15, starting transfers between devices, z_shift(): lax.ppermute(x, 'rep', [(a * NZ + z, a * NZ + (z + d) % NZ) for a in rang...  24.4 us
    pallas_call x21, Pallas kernels, call(): pl.pallas_call(body, out_shape=out_shape, in_specs=[IN_VMEM] * (n + extra...  13.8 us
    ppermute x15, waiting for transfers between devices, z_shift(): lax.ppermute(x, 'rep', [(a * NZ + z, a * NZ + (z + d) % NZ) for a in rang...  11.8 us
    ppermute x6, starting transfers between devices, y_shift(): lax.ppermute(x, 'row', [(y * 2 + c, (y + d) % 4 * 2 + c) for y in range(4...  7.84 us
    ppermute x3, starting transfers between devices, half_swap(): return lax.ppermute(x, 'col', [(0, 1), (1, 0)])  6.62 us
    ppermute x5, waiting for transfers between devices, x_swap(): lax.ppermute(x, 'rep', [(a * NZ + z, (1 - a) * NZ + z) for a in range(2)...  3.73 us
    ppermute x5, starting transfers between devices, x_swap(): lax.ppermute(x, 'rep', [(a * NZ + z, (1 - a) * NZ + z) for a in range(2)...  3.67 us
    ppermute x2, starting transfers between devices, cross_swap(): return lax.ppermute(x, ('rep', 'col'), pairs)  3.32 us
  transfers between devices with their start and end apart: 32, of which 17 were waited for; matrix products, arithmetic and copies ran while one was open for 0% of the time, Pallas kernels for 17%

profile of v5, /device:TPU:16, one launch (start us, length us, event | category | flops | bytes accessed | tf_op | source)
XLA Modules:
  0.0 89.5 jit_solution(442093141679565123)
XLA Ops:
  0.6 3.1 %collective-permute-start = (bf16[64,1024]{1,0:T(8,128)(2,1)}, bf16[64,1024]{1,0:T(8,128)(2,1)S(1)}, u32[]{:S(2)}, u32[]{:S(2)}) collective-permute-start(bf16[64,1024]{1,0:T(8,128)(2,1)} %bitcast.5), channel_id=1, source_target_pairs={{0,1},{1,0},{2,3},{3,2},{4,5},{5,4},{6,7},{7,6},{8,9},{9,8},{10,11... | collective-permute-start | bytes 393224 | tf_op jit(solution)/shard_map/ppermute | solution.py:429
  3.8 1.3 %collective-permute-start.5 = (bf16[64,1024]{1,0:T(8,128)(2,1)}, bf16[64,1024]{1,0:T(8,128)(2,1)S(1)}, u32[]{:S(2)}, u32[]{:S(2)}) collective-permute-start(bf16[64,1024]{1,0:T(8,128)(2,1)} %bitcast.6), channel_id=1, source_target_pairs={{0,4},{2,6},{4,8},{6,10},{8,12},{10,14},{12,0},{14,2},{1,5},{3,7},... | collective-permute-start | bytes 393224 | tf_op jit(solution)/shard_map/ppermute | solution.py:419
  5.7 1.1 %collective-permute-start.1 = (bf16[64,1024]{1,0:T(8,128)(2,1)}, bf16[64,1024]{1,0:T(8,128)(2,1)S(1)}, u32[]{:S(2)}, u32[]{:S(2)}) collective-permute-start(bf16[64,1024]{1,0:T(8,128)(2,1)} %bitcast.8), channel_id=1, source_target_pairs={{0,12},{2,14},{4,0},{6,2},{8,4},{10,6},{12,8},{14,10},{1,13},{3,15... | collective-permute-start | bytes 393224 | tf_op jit(solution)/shard_map/ppermute | solution.py:419
  6.7 1.0 %collective-permute-done.refs_3_ = bf16[64,1024]{1,0:T(8,128)(2,1)S(1)} collective-permute-done((bf16[64,1024]{1,0:T(8,128)(2,1)}, bf16[64,1024]{1,0:T(8,128)(2,1)S(1)}, u32[]{:S(2)}, u32[]{:S(2)}) %collective-permute-start) | collective-permute-done | bytes 131104 | tf_op jit(solution)/shard_map/ppermute | solution.py:429
  7.7 1.3 %collective-permute-start.6 = (bf16[64,1024]{1,0:T(8,128)(2,1)S(1)}, bf16[64,1024]{1,0:T(8,128)(2,1)S(1)}, u32[]{:S(2)}, u32[]{:S(2)}) collective-permute-start(bf16[64,1024]{1,0:T(8,128)(2,1)S(1)} %collective-permute-done.refs_3_), channel_id=1, source_target_pairs={{0,4},{2,6},{4,8},{6,10},{8,12},{10,14},{12,0},{14,2},{1,5},{3,7},... | collective-permute-start | bytes 393224 | tf_op jit(solution)/shard_map/ppermute | solution.py:419
  9.0 1.6 %collective-permute-start.4 = (bf16[64,1024]{1,0:T(8,128)(2,1)S(1)}, bf16[64,1024]{1,0:T(8,128)(2,1)S(1)}, u32[]{:S(2)}, u32[]{:S(2)}) collective-permute-start(bf16[64,1024]{1,0:T(8,128)(2,1)S(1)} %collective-permute-done.refs_3_), channel_id=1, source_target_pairs={{0,8},{2,10},{4,12},{6,14},{8,0},{10,2},{12,4},{14,6},{1,9},{3,11}... | collective-permute-start | bytes 393224 | tf_op jit(solution)/shard_map/ppermute | solution.py:419
  10.6 2.0 %collective-permute-start.2 = (bf16[64,1024]{1,0:T(8,128)(2,1)S(1)}, bf16[64,1024]{1,0:T(8,128)(2,1)S(1)}, u32[]{:S(2)}, u32[]{:S(2)}) collective-permute-start(bf16[64,1024]{1,0:T(8,128)(2,1)S(1)} %collective-permute-done.refs_3_), channel_id=1, source_target_pairs={{0,12},{2,14},{4,0},{6,2},{8,4},{10,6},{12,8},{14,10},{1,13},{3,15... | collective-permute-start | bytes 393224 | tf_op jit(solution)/shard_map/ppermute | solution.py:419
  12.6 2.8 %copy-done = bf16[1024,3072]{1,0:T(8,128)(2,1)S(1)} copy-done((bf16[1024,3072]{1,0:T(8,128)(2,1)S(1)}, bf16[1024,3072]{1,0:T(8,128)(2,1)}, u32[]{:S(2)}) %copy-start) | copy-done | bytes 6291480
  15.3 2.3 %shard_map.68.refs_10_.refs_0_ = bf16[8,1024,384]{2,1,0:T(8,128)(2,1)S(1)} custom-call(bf16[1024,3072]{1,0:T(8,128)(2,1)S(1)} %copy-done, bf16[1024,3072]{1,0:T(8,128)(2,1)S(1)} %copy-done), custom_call_target="tpu_custom_call" | custom-call | bytes 12582912 | tf_op jit(solution)/shard_map/pallas_call | solution.py:76
  18.3 0.9 %collective-permute-done.2.refs_5_ = bf16[64,1024]{1,0:T(8,128)(2,1)S(1)} collective-permute-done((bf16[64,1024]{1,0:T(8,128)(2,1)S(1)}, bf16[64,1024]{1,0:T(8,128)(2,1)S(1)}, u32[]{:S(2)}, u32[]{:S(2)}) %collective-permute-start.2) | collective-permute-done | bytes 131104 | tf_op jit(solution)/shard_map/ppermute | solution.py:419
  20.6 1.5 %collective-permute-done.7.refs_1_.refs_2_ = bf16[528,1024]{1,0:T(8,128)(2,1)S(1)} collective-permute-done((bf16[528,1024]{1,0:T(8,128)(2,1)S(1)}, bf16[528,1024]{1,0:T(8,128)(2,1)S(1)}, u32[]{:S(2)}, u32[]{:S(2)}) %collective-permute-start.7) | collective-permute-done | bytes 1081376 | tf_op jit(solution)/shard_map/ppermute | solution.py:425
  22.9 2.0 %collective-permute-start.12 = (bf16[256,384]{1,0:T(8,128)(2,1)S(1)}, bf16[256,384]{1,0:T(8,128)(2,1)S(1)}, u32[]{:S(2)}, u32[]{:S(2)}) collective-permute-start(bf16[256,384]{1,0:T(8,128)(2,1)S(1)} %get-tuple-element.40), channel_id=1, source_target_pairs={{0,16},{16,32},{32,48},{48,64},{64,80},{80,96},{96,112},{112,0},{1... | collective-permute-start | bytes 589832 | tf_op jit(solution)/shard_map/ppermute | solution.py:407
  24.9 4.0 %collective-permute-start.11 = (bf16[256,384]{1,0:T(8,128)(2,1)S(1)}, bf16[256,384]{1,0:T(8,128)(2,1)S(1)}, u32[]{:S(2)}, u32[]{:S(2)}) collective-permute-start(bf16[256,384]{1,0:T(8,128)(2,1)S(1)} %get-tuple-element.37.refs_2_), channel_id=1, source_target_pairs={{0,112},{16,0},{32,16},{48,32},{64,48},{80,64},{96,80},{112,96},{1... | collective-permute-start | bytes 589832 | tf_op jit(solution)/shard_map/ppermute | solution.py:407
  28.9 0.8 shard_map.73.refs_3_
  31.1 1.3 %shard_map.75 = (f32[512,384]{1,0:T(8,128)S(1)}, f32[512,384]{1,0:T(8,128)S(1)}) custom-call(bf16[8,1024,384]{2,1,0:T(8,128)(2,1)S(1)} %shard_map.68.refs_10_.refs_0_, bf16[528,1024]{1,0:T(8,128)(2,1)S(1)} %collective-permute-done.7.refs_1_.refs_2_, bf16[272,384]{1,0:T(8,128)(2,1)S(1)} %shard_map.74.refs_2_), custom_call_target="tpu_custom_call" | custom-call | flops 1000000000 | bytes 1 | tf_op jit(solution)/shard_map/pallas_call | solution.py:27
  32.4 1.7 %collective-permute-done.12.refs_3_ = bf16[256,384]{1,0:T(8,128)(2,1)S(1)} collective-permute-done((bf16[256,384]{1,0:T(8,128)(2,1)S(1)}, bf16[256,384]{1,0:T(8,128)(2,1)S(1)}, u32[]{:S(2)}, u32[]{:S(2)}) %collective-permute-start.12) | collective-permute-done | bytes 196640 | tf_op jit(solution)/shard_map/ppermute | solution.py:407
  34.2 3.2 %collective-permute-start.13 = (bf16[512,384]{1,0:T(8,128)(2,1)S(1)}, bf16[512,384]{1,0:T(8,128)(2,1)S(1)}, u32[]{:S(2)}, u32[]{:S(2)}) collective-permute-start(bf16[512,384]{1,0:T(8,128)(2,1)S(1)} %get-tuple-element.41.refs_4_), channel_id=1, source_target_pairs={{0,112},{16,0},{32,16},{48,32},{64,48},{80,64},{96,80},{112,96},{1... | collective-permute-start | bytes 1179656 | tf_op jit(solution)/shard_map/ppermute | solution.py:407
  37.4 2.9 %collective-permute-done.10.refs_3_ = bf16[272,384]{1,0:T(8,128)(2,1)S(1)} collective-permute-done((bf16[272,384]{1,0:T(8,128)(2,1)S(1)}, bf16[272,384]{1,0:T(8,128)(2,1)S(1)}, u32[]{:S(2)}, u32[]{:S(2)}) %collective-permute-start.10) | collective-permute-done | bytes 208928 | tf_op jit(solution)/shard_map/ppermute | solution.py:407
  40.3 0.8 collective-permute-done.8.refs_2_
  41.1 0.8 shard_map.77
  41.9 1.7 %collective-permute-start.18 = (bf16[272,384]{1,0:T(8,128)(2,1)S(1)}, bf16[272,384]{1,0:T(8,128)(2,1)S(1)}, u32[]{:S(2)}, u32[]{:S(2)}) collective-permute-start(bf16[272,384]{1,0:T(8,128)(2,1)S(1)} %get-tuple-element.47), channel_id=1, source_target_pairs={{0,112},{16,0},{32,16},{48,32},{64,48},{80,64},{96,80},{112,96},{1... | collective-permute-start | bytes 626696 | tf_op jit(solution)/shard_map/ppermute | solution.py:407
  44.8 0.8 collective-permute-start.16
  45.5 1.3 %shard_map.79 = (f32[512,384]{1,0:T(8,128)S(1)}, f32[512,384]{1,0:T(8,128)S(1)}) custom-call(bf16[8,1024,384]{2,1,0:T(8,128)(2,1)S(1)} %shard_map.68.refs_10_.refs_0_, bf16[528,1024]{1,0:T(8,128)(2,1)S(1)} %collective-permute-done.7.refs_1_.refs_2_, bf16[2,272,384]{2,1,0:T(8,128)(2,1)S(1)} %shard_map.78.refs_2_), custom_call_target="tpu_custom_call" | custom-call | flops 1000000000 | bytes 1 | tf_op jit(solution)/shard_map/pallas_call | solution.py:27
  46.8 2.0 %collective-permute-done.14.refs_3_ = bf16[512,384]{1,0:T(8,128)(2,1)S(1)} collective-permute-done((bf16[512,384]{1,0:T(8,128)(2,1)S(1)}, bf16[512,384]{1,0:T(8,128)(2,1)S(1)}, u32[]{:S(2)}, u32[]{:S(2)}) %collective-permute-start.14) | collective-permute-done | bytes 393248 | tf_op jit(solution)/shard_map/ppermute | solution.py:407
  48.9 1.2 %collective-permute-start.22 = (bf16[512,384]{1,0:T(8,128)(2,1)S(1)}, bf16[512,384]{1,0:T(8,128)(2,1)S(1)}, u32[]{:S(2)}, u32[]{:S(2)}) collective-permute-start(bf16[512,384]{1,0:T(8,128)(2,1)S(1)} %get-tuple-element.52), channel_id=1, source_target_pairs={{0,16},{16,32},{32,48},{48,64},{64,80},{80,96},{96,112},{112,0},{1... | collective-permute-start | bytes 1179656 | tf_op jit(solution)/shard_map/ppermute | solution.py:407
  50.1 2.1 %collective-permute-start.21 = (bf16[512,384]{1,0:T(8,128)(2,1)S(1)}, bf16[512,384]{1,0:T(8,128)(2,1)S(1)}, u32[]{:S(2)}, u32[]{:S(2)}) collective-permute-start(bf16[512,384]{1,0:T(8,128)(2,1)S(1)} %get-tuple-element.46.refs_2_), channel_id=1, source_target_pairs={{0,112},{16,0},{32,16},{48,32},{64,48},{80,64},{96,80},{112,96},{1... | collective-permute-start | bytes 1179656 | tf_op jit(solution)/shard_map/ppermute | solution.py:407
  52.2 1.0 %shard_map.81.refs_5_ = bf16[3,272,384]{2,1,0:T(8,128)(2,1)S(1)} custom-call(bf16[8,1024,384]{2,1,0:T(8,128)(2,1)S(1)} %shard_map.68.refs_10_.refs_0_, bf16[528,1024]{1,0:T(8,128)(2,1)S(1)} %shard_map.70.refs_1_, bf16[512,384]{1,0:T(8,128)(2,1)S(1)} %get-tuple-element.46.refs_2_), custom_call_target="tpu_custom_call" | custom-call | flops 2000000000 | bytes 1 | tf_op jit(solution)/shard_map/pallas_call | solution.py:27
  53.3 1.6 %collective-permute-start.15 = (bf16[3,272,384]{2,1,0:T(8,128)(2,1)S(1)}, bf16[3,272,384]{2,1,0:T(8,128)(2,1)S(1)}, u32[]{:S(2)}, u32[]{:S(2)}) collective-permute-start(bf16[3,272,384]{2,1,0:T(8,128)(2,1)S(1)} %shard_map.81.refs_5_), channel_id=1, source_target_pairs={{0,128},{16,144},{32,160},{48,176},{64,192},{80,208},{96,224},{112... | collective-permute-start | bytes 1880072 | tf_op jit(solution)/shard_map/ppermute | solution.py:413
  54.8 1.5 %collective-permute-done.16.refs_2_ = bf16[2,272,384]{2,1,0:T(8,128)(2,1)S(1)} collective-permute-done((bf16[2,272,384]{2,1,0:T(8,128)(2,1)S(1)}, bf16[2,272,384]{2,1,0:T(8,128)(2,1)S(1)}, u32[]{:S(2)}, u32[]{:S(2)}) %collective-permute-start.16) | collective-permute-done | bytes 417824 | tf_op jit(solution)/shard_map/ppermute | solution.py:413
  56.4 0.8 shard_map.82
  57.2 3.9 %collective-permute-start.20 = (bf16[272,384]{1,0:T(8,128)(2,1)S(1)}, bf16[272,384]{1,0:T(8,128)(2,1)S(1)}, u32[]{:S(2)}, u32[]{:S(2)}) collective-permute-start(bf16[272,384]{1,0:T(8,128)(2,1)S(1)} %get-tuple-element.49), channel_id=1, source_target_pairs={{0,112},{16,0},{32,16},{48,32},{64,48},{80,64},{96,80},{112,96},{1... | collective-permute-start | bytes 626696 | tf_op jit(solution)/shard_map/ppermute | solution.py:407
  61.1 1.3 %shard_map.83 = (f32[512,384]{1,0:T(8,128)S(1)}, f32[512,384]{1,0:T(8,128)S(1)}) custom-call(bf16[8,1024,384]{2,1,0:T(8,128)(2,1)S(1)} %shard_map.68.refs_10_.refs_0_, bf16[528,1024]{1,0:T(8,128)(2,1)S(1)} %collective-permute-done.7.refs_1_.refs_2_, bf16[272,384]{1,0:T(8,128)(2,1)S(1)} %get-tuple-element.48.refs_2_), custom_call_target="tpu_custom_call" | custom-call | flops 1000000000 | bytes 1 | tf_op jit(solution)/shard_map/pallas_call | solution.py:27
  62.5 1.5 %collective-permute-start.24 = (bf16[512,384]{1,0:T(8,128)(2,1)S(1)}, bf16[512,384]{1,0:T(8,128)(2,1)S(1)}, u32[]{:S(2)}, u32[]{:S(2)}) collective-permute-start(bf16[512,384]{1,0:T(8,128)(2,1)S(1)} %get-tuple-element.57), channel_id=1, source_target_pairs={{0,16},{16,32},{32,48},{48,64},{64,80},{80,96},{96,112},{112,0},{1... | collective-permute-start | bytes 1179656 | tf_op jit(solution)/shard_map/ppermute | solution.py:407
  64.1 1.9 %collective-permute-start.23 = (bf16[512,384]{1,0:T(8,128)(2,1)S(1)}, bf16[512,384]{1,0:T(8,128)(2,1)S(1)}, u32[]{:S(2)}, u32[]{:S(2)}) collective-permute-start(bf16[512,384]{1,0:T(8,128)(2,1)S(1)} %get-tuple-element.53.refs_5_), channel_id=1, source_target_pairs={{0,112},{16,0},{32,16},{48,32},{64,48},{80,64},{96,80},{112,96},{1... | collective-permute-start | bytes 1179656 | tf_op jit(solution)/shard_map/ppermute | solution.py:407
  66.5 2.9 %collective-permute-done.19.refs_3_ = bf16[272,384]{1,0:T(8,128)(2,1)S(1)} collective-permute-done((bf16[272,384]{1,0:T(8,128)(2,1)S(1)}, bf16[272,384]{1,0:T(8,128)(2,1)S(1)}, u32[]{:S(2)}, u32[]{:S(2)}) %collective-permute-start.19) | collective-permute-done | bytes 208928 | tf_op jit(solution)/shard_map/ppermute | solution.py:407
  69.4 0.8 shard_map.85
  70.2 1.5 %collective-permute-start.26 = (bf16[272,384]{1,0:T(8,128)(2,1)S(1)}, bf16[272,384]{1,0:T(8,128)(2,1)S(1)}, u32[]{:S(2)}, u32[]{:S(2)}) collective-permute-start(bf16[272,384]{1,0:T(8,128)(2,1)S(1)} %get-tuple-element.59), channel_id=1, source_target_pairs={{0,112},{16,0},{32,16},{48,32},{64,48},{80,64},{96,80},{112,96},{1... | collective-permute-start | bytes 626696 | tf_op jit(solution)/shard_map/ppermute | solution.py:407
  72.3 1.0 %shard_map.86 = (f32[272,384]{1,0:T(8,128)S(1)}, f32[512,384]{1,0:T(8,128)S(1)}) custom-call(bf16[8,1024,384]{2,1,0:T(8,128)(2,1)S(1)} %shard_map.68.refs_10_.refs_0_, bf16[528,1024]{1,0:T(8,128)(2,1)S(1)} %shard_map.70.refs_1_, bf16[528,1024]{1,0:T(8,128)(2,1)S(1)} %collective-permute-done.7.refs_1_.refs_2_, ...), custom_call_target="tpu_custom_call" | custom-call | flops 1000000000 | bytes 1 | tf_op jit(solution)/shard_map/pallas_call | solution.py:27
  73.3 1.4 %collective-permute-done.24.refs_2_ = bf16[512,384]{1,0:T(8,128)(2,1)S(1)} collective-permute-done((bf16[512,384]{1,0:T(8,128)(2,1)S(1)}, bf16[512,384]{1,0:T(8,128)(2,1)S(1)}, u32[]{:S(2)}, u32[]{:S(2)}) %collective-permute-start.24) | collective-permute-done | bytes 393248 | tf_op jit(solution)/shard_map/ppermute | solution.py:407
  75.4 1.2 %collective-permute-start.27 = (bf16[192,256]{1,0:T(8,128)(2,1)S(1)}, bf16[192,256]{1,0:T(8,128)(2,1)S(1)}, u32[]{:S(2)}, u32[]{:S(2)}) collective-permute-start(bf16[192,256]{1,0:T(8,128)(2,1)S(1)} %get-tuple-element.63), channel_id=1, source_target_pairs={{0,129},{1,128},{16,145},{17,144},{32,161},{33,160},{48,177},{49,1... | collective-permute-start | bytes 294920 | tf_op jit(solution)/shard_map/ppermute | solution.py:438
  76.7 1.9 %collective-permute-start.28 = (bf16[192,256]{1,0:T(8,128)(2,1)S(1)}, bf16[192,256]{1,0:T(8,128)(2,1)S(1)}, u32[]{:S(2)}, u32[]{:S(2)}) collective-permute-start(bf16[192,256]{1,0:T(8,128)(2,1)S(1)} %get-tuple-element.64), channel_id=1, source_target_pairs={{0,1},{1,0},{2,3},{3,2},{4,5},{5,4},{6,7},{7,6},{8,9},{9,8},{10,11... | collective-permute-start | bytes 294920 | tf_op jit(solution)/shard_map/ppermute | solution.py:429
  79.0 1.6 %collective-permute-start.31 = (bf16[192,256]{1,0:T(8,128)(2,1)S(1)}, bf16[192,256]{1,0:T(8,128)(2,1)S(1)}, u32[]{:S(2)}, u32[]{:S(2)}) collective-permute-start(bf16[192,256]{1,0:T(8,128)(2,1)S(1)} %get-tuple-element.67), channel_id=1, source_target_pairs={{0,1},{1,0},{2,3},{3,2},{4,5},{5,4},{6,7},{7,6},{8,9},{9,8},{10,11... | collective-permute-start | bytes 294920 | tf_op jit(solution)/shard_map/ppermute | solution.py:429
  80.6 2.1 %collective-permute-start.30 = (bf16[208,256]{1,0:T(8,128)(2,1)S(1)}, bf16[208,256]{1,0:T(8,128)(2,1)S(1)}, u32[]{:S(2)}, u32[]{:S(2)}) collective-permute-start(bf16[208,256]{1,0:T(8,128)(2,1)S(1)} %get-tuple-element.66), channel_id=1, source_target_pairs={{0,129},{1,128},{16,145},{17,144},{32,161},{33,160},{48,177},{49,1... | collective-permute-start | bytes 319496 | tf_op jit(solution)/shard_map/ppermute | solution.py:438
  82.7 1.7 %collective-permute-done.27.refs_0_ = bf16[192,256]{1,0:T(8,128)(2,1)S(1)} collective-permute-done((bf16[192,256]{1,0:T(8,128)(2,1)S(1)}, bf16[192,256]{1,0:T(8,128)(2,1)S(1)}, u32[]{:S(2)}, u32[]{:S(2)}) %collective-permute-start.27) | collective-permute-done | bytes 98336 | tf_op jit(solution)/shard_map/ppermute | solution.py:438
  84.4 1.6 %collective-permute-done.31.refs_6_ = bf16[192,256]{1,0:T(8,128)(2,1)S(1)} collective-permute-done((bf16[192,256]{1,0:T(8,128)(2,1)S(1)}, bf16[192,256]{1,0:T(8,128)(2,1)S(1)}, u32[]{:S(2)}, u32[]{:S(2)}) %collective-permute-start.31) | collective-permute-done | bytes 98336 | tf_op jit(solution)/shard_map/ppermute | solution.py:429
  86.0 1.0 %collective-permute-done.30.refs_5_ = bf16[208,256]{1,0:T(8,128)(2,1)S(1)} collective-permute-done((bf16[208,256]{1,0:T(8,128)(2,1)S(1)}, bf16[208,256]{1,0:T(8,128)(2,1)S(1)}, u32[]{:S(2)}, u32[]{:S(2)}) %collective-permute-start.30) | collective-permute-done | bytes 106528 | tf_op jit(solution)/shard_map/ppermute | solution.py:438
  87.0 1.4 %collective-permute-done.29.refs_4_ = bf16[192,512]{1,0:T(8,128)(2,1)S(1)} collective-permute-done((bf16[192,512]{1,0:T(8,128)(2,1)S(1)}, bf16[192,512]{1,0:T(8,128)(2,1)S(1)}, u32[]{:S(2)}, u32[]{:S(2)}) %collective-permute-start.29) | collective-permute-done | bytes 196640 | tf_op jit(solution)/shard_map/ppermute | solution.py:413
  88.4 1.2 %shard_map.90 = (f32[1,2,192,512]{3,2,1,0:T(8,128)}, f32[1,2,192]{2,1,0:T(2,128)}) custom-call(f32[192,128]{1,0:T(8,128)S(1)} %get-tuple-element.61.refs_2_.refs_0_, f32[192,256]{1,0:T(8,128)S(1)} %get-tuple-element.60.refs_4_.refs_1_, f32[8,192]{1,0:T(8,128)S(1)} %get-tuple-element.62.refs_2_, f32[192,256]{1,0:T(8,128)S(1)} %shard_map.89.refs_3_, ...), custom_call_target="tpu_custom_call" | custom-call | flops 4000000000 | bytes 1 | tf_op jit(solution)/shard_map/pallas_call | solution.py:27
  (49 shorter events, 8.8 us)
Async XLA Ops:
  0.6 17.0 %copy-start.4 = (f32[8]{0:T(128)S(1)}, f32[8]{0:T(128)}, u32[]{:S(2)}) copy-start(f32[8]{0:T(128)} %sigma_ref.1) | copy-start | bytes 100
  0.6 7.0 %collective-permute-start = (bf16[64,1024]{1,0:T(8,128)(2,1)}, bf16[64,1024]{1,0:T(8,128)(2,1)S(1)}, u32[]{:S(2)}, u32[]{:S(2)}) collective-permute-start(bf16[64,1024]{1,0:T(8,128)(2,1)} %bitcast.5), channel_id=1, source_target_pairs={{0,1},{1,0},{2,3},{3,2},{4,5},{5,4},{6,7},{7,6},{8,9},{9,8},{10,11... | collective-permute-start | bytes 393224 | tf_op jit(solution)/shard_map/ppermute | solution.py:429
  3.8 6.8 %collective-permute-start.5 = (bf16[64,1024]{1,0:T(8,128)(2,1)}, bf16[64,1024]{1,0:T(8,128)(2,1)S(1)}, u32[]{:S(2)}, u32[]{:S(2)}) collective-permute-start(bf16[64,1024]{1,0:T(8,128)(2,1)} %bitcast.6), channel_id=1, source_target_pairs={{0,4},{2,6},{4,8},{6,10},{8,12},{10,14},{12,0},{14,2},{1,5},{3,7},... | collective-permute-start | bytes 393224 | tf_op jit(solution)/shard_map/ppermute | solution.py:419
  5.0 13.2 %collective-permute-start.3 = (bf16[64,1024]{1,0:T(8,128)(2,1)}, bf16[64,1024]{1,0:T(8,128)(2,1)S(1)}, u32[]{:S(2)}, u32[]{:S(2)}) collective-permute-start(bf16[64,1024]{1,0:T(8,128)(2,1)} %bitcast.7), channel_id=1, source_target_pairs={{0,8},{2,10},{4,12},{6,14},{8,0},{10,2},{12,4},{14,6},{1,9},{3,11}... | collective-permute-start | bytes 393224 | tf_op jit(solution)/shard_map/ppermute | solution.py:419
  5.7 12.6 %collective-permute-start.1 = (bf16[64,1024]{1,0:T(8,128)(2,1)}, bf16[64,1024]{1,0:T(8,128)(2,1)S(1)}, u32[]{:S(2)}, u32[]{:S(2)}) collective-permute-start(bf16[64,1024]{1,0:T(8,128)(2,1)} %bitcast.8), channel_id=1, source_target_pairs={{0,12},{2,14},{4,0},{6,2},{8,4},{10,6},{12,8},{14,10},{1,13},{3,15... | collective-permute-start | bytes 393224 | tf_op jit(solution)/shard_map/ppermute | solution.py:419
  7.7 10.6 %collective-permute-start.6 = (bf16[64,1024]{1,0:T(8,128)(2,1)S(1)}, bf16[64,1024]{1,0:T(8,128)(2,1)S(1)}, u32[]{:S(2)}, u32[]{:S(2)}) collective-permute-start(bf16[64,1024]{1,0:T(8,128)(2,1)S(1)} %collective-permute-done.refs_3_), channel_id=1, source_target_pairs={{0,4},{2,6},{4,8},{6,10},{8,12},{10,14},{12,0},{14,2},{1,5},{3,7},... | collective-permute-start | bytes 393224 | tf_op jit(solution)/shard_map/ppermute | solution.py:419
  9.0 9.3 %collective-permute-start.4 = (bf16[64,1024]{1,0:T(8,128)(2,1)S(1)}, bf16[64,1024]{1,0:T(8,128)(2,1)S(1)}, u32[]{:S(2)}, u32[]{:S(2)}) collective-permute-start(bf16[64,1024]{1,0:T(8,128)(2,1)S(1)} %collective-permute-done.refs_3_), channel_id=1, source_target_pairs={{0,8},{2,10},{4,12},{6,14},{8,0},{10,2},{12,4},{14,6},{1,9},{3,11}... | collective-permute-start | bytes 393224 | tf_op jit(solution)/shard_map/ppermute | solution.py:419
  10.6 8.6 %collective-permute-start.2 = (bf16[64,1024]{1,0:T(8,128)(2,1)S(1)}, bf16[64,1024]{1,0:T(8,128)(2,1)S(1)}, u32[]{:S(2)}, u32[]{:S(2)}) collective-permute-start(bf16[64,1024]{1,0:T(8,128)(2,1)S(1)} %collective-permute-done.refs_3_), channel_id=1, source_target_pairs={{0,12},{2,14},{4,0},{6,2},{8,4},{10,6},{12,8},{14,10},{1,13},{3,15... | collective-permute-start | bytes 393224 | tf_op jit(solution)/shard_map/ppermute | solution.py:419
  12.6 2.8 %copy-start = (bf16[1024,3072]{1,0:T(8,128)(2,1)S(1)}, bf16[1024,3072]{1,0:T(8,128)(2,1)}, u32[]{:S(2)}) copy-start(bf16[1024,3072]{1,0:T(8,128)(2,1)} %second_ref.1) | copy-start | bytes 18874372
  15.3 2.3 %copy-start.2 = (f32[1024]{0:T(1024)S(1)}, f32[1024]{0:T(1024)}, u32[]{:S(2)}) copy-start(f32[1024]{0:T(1024)} %param.7) | copy-start | bytes 12292
  15.3 2.3 %copy-start.3 = (s32[1024]{0:T(1024)S(1)}, s32[1024]{0:T(1024)}, u32[]{:S(2)}) copy-start(s32[1024]{0:T(1024)} %param.8) | copy-start | bytes 12292
  15.3 3.8 %copy-start.1 = (bf16[1024,1,64]{0,2,1:T(8,128)(2,1)S(1)}, bf16[1024,1,64]{0,2,1:T(8,128)(2,1)}, u32[]{:S(2)}) copy-start(bf16[1024,1,64]{0,2,1:T(8,128)(2,1)} %param.6) | copy-start | bytes 393220
  19.4 2.8 %collective-permute-start.7 = (bf16[528,1024]{1,0:T(8,128)(2,1)S(1)}, bf16[528,1024]{1,0:T(8,128)(2,1)S(1)}, u32[]{:S(2)}, u32[]{:S(2)}) collective-permute-start(bf16[528,1024]{1,0:T(8,128)(2,1)S(1)} %shard_map.70.refs_1_), channel_id=1, source_target_pairs={{0,2},{2,0},{4,6},{6,4},{8,10},{10,8},{12,14},{14,12},{1,3},{3,1},... | collective-permute-start | bytes 3244040 | tf_op jit(solution)/shard_map/ppermute | solution.py:425
  19.9 10.4 %collective-permute-start.9 = (bf16[1,272,384]{2,1,0:T(8,128)(2,1)S(1)}, bf16[1,272,384]{2,1,0:T(8,128)(2,1)S(1)}, u32[]{:S(2)}, u32[]{:S(2)}) collective-permute-start(bf16[1,272,384]{2,1,0:T(8,128)(2,1)S(1)} %shard_map.71.refs_2_), channel_id=1, source_target_pairs={{0,128},{16,144},{32,160},{48,176},{64,192},{80,208},{96,224},{112... | collective-permute-start | bytes 626696 | tf_op jit(solution)/shard_map/ppermute | solution.py:413
  22.9 11.1 %collective-permute-start.12 = (bf16[256,384]{1,0:T(8,128)(2,1)S(1)}, bf16[256,384]{1,0:T(8,128)(2,1)S(1)}, u32[]{:S(2)}, u32[]{:S(2)}) collective-permute-start(bf16[256,384]{1,0:T(8,128)(2,1)S(1)} %get-tuple-element.40), channel_id=1, source_target_pairs={{0,16},{16,32},{32,48},{48,64},{64,80},{80,96},{96,112},{112,0},{1... | collective-permute-start | bytes 589832 | tf_op jit(solution)/shard_map/ppermute | solution.py:407
  24.9 9.1 %collective-permute-start.11 = (bf16[256,384]{1,0:T(8,128)(2,1)S(1)}, bf16[256,384]{1,0:T(8,128)(2,1)S(1)}, u32[]{:S(2)}, u32[]{:S(2)}) collective-permute-start(bf16[256,384]{1,0:T(8,128)(2,1)S(1)} %get-tuple-element.37.refs_2_), channel_id=1, source_target_pairs={{0,112},{16,0},{32,16},{48,32},{64,48},{80,64},{96,80},{112,96},{1... | collective-permute-start | bytes 589832 | tf_op jit(solution)/shard_map/ppermute | solution.py:407
  29.7 11.5 %collective-permute-start.8 = (bf16[2,272,384]{2,1,0:T(8,128)(2,1)S(1)}, bf16[2,272,384]{2,1,0:T(8,128)(2,1)S(1)}, u32[]{:S(2)}, u32[]{:S(2)}) collective-permute-start(bf16[2,272,384]{2,1,0:T(8,128)(2,1)S(1)} %shard_map.73.refs_3_), channel_id=1, source_target_pairs={{0,128},{16,144},{32,160},{48,176},{64,192},{80,208},{96,224},{112... | collective-permute-start | bytes 1253384 | tf_op jit(solution)/shard_map/ppermute | solution.py:413
  30.8 9.5 %collective-permute-start.10 = (bf16[272,384]{1,0:T(8,128)(2,1)S(1)}, bf16[272,384]{1,0:T(8,128)(2,1)S(1)}, u32[]{:S(2)}, u32[]{:S(2)}) collective-permute-start(bf16[272,384]{1,0:T(8,128)(2,1)S(1)} %shard_map.74.refs_2_), channel_id=1, source_target_pairs={{0,16},{16,32},{32,48},{48,64},{64,80},{80,96},{96,112},{112,0},{1... | collective-permute-start | bytes 626696 | tf_op jit(solution)/shard_map/ppermute | solution.py:407
  34.1 14.6 %collective-permute-start.14 = (bf16[512,384]{1,0:T(8,128)(2,1)S(1)}, bf16[512,384]{1,0:T(8,128)(2,1)S(1)}, u32[]{:S(2)}, u32[]{:S(2)}) collective-permute-start(bf16[512,384]{1,0:T(8,128)(2,1)S(1)} %get-tuple-element.45), channel_id=1, source_target_pairs={{0,16},{16,32},{32,48},{48,64},{64,80},{80,96},{96,112},{112,0},{1... | collective-permute-start | bytes 1179656 | tf_op jit(solution)/shard_map/ppermute | solution.py:407
  34.2 14.5 %collective-permute-start.13 = (bf16[512,384]{1,0:T(8,128)(2,1)S(1)}, bf16[512,384]{1,0:T(8,128)(2,1)S(1)}, u32[]{:S(2)}, u32[]{:S(2)}) collective-permute-start(bf16[512,384]{1,0:T(8,128)(2,1)S(1)} %get-tuple-element.41.refs_4_), channel_id=1, source_target_pairs={{0,112},{16,0},{32,16},{48,32},{64,48},{80,64},{96,80},{112,96},{1... | collective-permute-start | bytes 1179656 | tf_op jit(solution)/shard_map/ppermute | solution.py:407
  41.9 11.4 %collective-permute-start.18 = (bf16[272,384]{1,0:T(8,128)(2,1)S(1)}, bf16[272,384]{1,0:T(8,128)(2,1)S(1)}, u32[]{:S(2)}, u32[]{:S(2)}) collective-permute-start(bf16[272,384]{1,0:T(8,128)(2,1)S(1)} %get-tuple-element.47), channel_id=1, source_target_pairs={{0,112},{16,0},{32,16},{48,32},{64,48},{80,64},{96,80},{112,96},{1... | collective-permute-start | bytes 626696 | tf_op jit(solution)/shard_map/ppermute | solution.py:407
  43.7 11.2 %collective-permute-start.17 = (bf16[272,384]{1,0:T(8,128)(2,1)S(1)}, bf16[272,384]{1,0:T(8,128)(2,1)S(1)}, u32[]{:S(2)}, u32[]{:S(2)}) collective-permute-start(bf16[272,384]{1,0:T(8,128)(2,1)S(1)} %get-tuple-element.42.refs_2_), channel_id=1, source_target_pairs={{0,16},{16,32},{32,48},{48,64},{64,80},{80,96},{96,112},{112,0},{1... | collective-permute-start | bytes 626696 | tf_op jit(solution)/shard_map/ppermute | solution.py:407
  44.8 11.6 %collective-permute-start.16 = (bf16[2,272,384]{2,1,0:T(8,128)(2,1)S(1)}, bf16[2,272,384]{2,1,0:T(8,128)(2,1)S(1)}, u32[]{:S(2)}, u32[]{:S(2)}) collective-permute-start(bf16[2,272,384]{2,1,0:T(8,128)(2,1)S(1)} %shard_map.78.refs_2_), channel_id=1, source_target_pairs={{0,128},{16,144},{32,160},{48,176},{64,192},{80,208},{96,224},{112... | collective-permute-start | bytes 1253384 | tf_op jit(solution)/shard_map/ppermute | solution.py:413
  48.9 13.4 %collective-permute-start.22 = (bf16[512,384]{1,0:T(8,128)(2,1)S(1)}, bf16[512,384]{1,0:T(8,128)(2,1)S(1)}, u32[]{:S(2)}, u32[]{:S(2)}) collective-permute-start(bf16[512,384]{1,0:T(8,128)(2,1)S(1)} %get-tuple-element.52), channel_id=1, source_target_pairs={{0,16},{16,32},{32,48},{48,64},{64,80},{80,96},{96,112},{112,0},{1... | collective-permute-start | bytes 1179656 | tf_op jit(solution)/shard_map/ppermute | solution.py:407
  50.1 12.2 %collective-permute-start.21 = (bf16[512,384]{1,0:T(8,128)(2,1)S(1)}, bf16[512,384]{1,0:T(8,128)(2,1)S(1)}, u32[]{:S(2)}, u32[]{:S(2)}) collective-permute-start(bf16[512,384]{1,0:T(8,128)(2,1)S(1)} %get-tuple-element.46.refs_2_), channel_id=1, source_target_pairs={{0,112},{16,0},{32,16},{48,32},{64,48},{80,64},{96,80},{112,96},{1... | collective-permute-start | bytes 1179656 | tf_op jit(solution)/shard_map/ppermute | solution.py:407
  53.3 16.1 %collective-permute-start.15 = (bf16[3,272,384]{2,1,0:T(8,128)(2,1)S(1)}, bf16[3,272,384]{2,1,0:T(8,128)(2,1)S(1)}, u32[]{:S(2)}, u32[]{:S(2)}) collective-permute-start(bf16[3,272,384]{2,1,0:T(8,128)(2,1)S(1)} %shard_map.81.refs_5_), channel_id=1, source_target_pairs={{0,128},{16,144},{32,160},{48,176},{64,192},{80,208},{96,224},{112... | collective-permute-start | bytes 1880072 | tf_op jit(solution)/shard_map/ppermute | solution.py:413
  57.2 9.4 %collective-permute-start.20 = (bf16[272,384]{1,0:T(8,128)(2,1)S(1)}, bf16[272,384]{1,0:T(8,128)(2,1)S(1)}, u32[]{:S(2)}, u32[]{:S(2)}) collective-permute-start(bf16[272,384]{1,0:T(8,128)(2,1)S(1)} %get-tuple-element.49), channel_id=1, source_target_pairs={{0,112},{16,0},{32,16},{48,32},{64,48},{80,64},{96,80},{112,96},{1... | collective-permute-start | bytes 626696 | tf_op jit(solution)/shard_map/ppermute | solution.py:407
  61.1 8.4 %collective-permute-start.19 = (bf16[272,384]{1,0:T(8,128)(2,1)S(1)}, bf16[272,384]{1,0:T(8,128)(2,1)S(1)}, u32[]{:S(2)}, u32[]{:S(2)}) collective-permute-start(bf16[272,384]{1,0:T(8,128)(2,1)S(1)} %get-tuple-element.48.refs_2_), channel_id=1, source_target_pairs={{0,16},{16,32},{32,48},{48,64},{64,80},{80,96},{96,112},{112,0},{1... | collective-permute-start | bytes 626696 | tf_op jit(solution)/shard_map/ppermute | solution.py:407
  62.5 12.2 %collective-permute-start.24 = (bf16[512,384]{1,0:T(8,128)(2,1)S(1)}, bf16[512,384]{1,0:T(8,128)(2,1)S(1)}, u32[]{:S(2)}, u32[]{:S(2)}) collective-permute-start(bf16[512,384]{1,0:T(8,128)(2,1)S(1)} %get-tuple-element.57), channel_id=1, source_target_pairs={{0,16},{16,32},{32,48},{48,64},{64,80},{80,96},{96,112},{112,0},{1... | collective-permute-start | bytes 1179656 | tf_op jit(solution)/shard_map/ppermute | solution.py:407
  64.1 11.0 %collective-permute-start.23 = (bf16[512,384]{1,0:T(8,128)(2,1)S(1)}, bf16[512,384]{1,0:T(8,128)(2,1)S(1)}, u32[]{:S(2)}, u32[]{:S(2)}) collective-permute-start(bf16[512,384]{1,0:T(8,128)(2,1)S(1)} %get-tuple-element.53.refs_5_), channel_id=1, source_target_pairs={{0,112},{16,0},{32,16},{48,32},{64,48},{80,64},{96,80},{112,96},{1... | collective-permute-start | bytes 1179656 | tf_op jit(solution)/shard_map/ppermute | solution.py:407
  70.2 8.4 %collective-permute-start.26 = (bf16[272,384]{1,0:T(8,128)(2,1)S(1)}, bf16[272,384]{1,0:T(8,128)(2,1)S(1)}, u32[]{:S(2)}, u32[]{:S(2)}) collective-permute-start(bf16[272,384]{1,0:T(8,128)(2,1)S(1)} %get-tuple-element.59), channel_id=1, source_target_pairs={{0,112},{16,0},{32,16},{48,32},{64,48},{80,64},{96,80},{112,96},{1... | collective-permute-start | bytes 626696 | tf_op jit(solution)/shard_map/ppermute | solution.py:407
  71.7 7.0 %collective-permute-start.25 = (bf16[272,384]{1,0:T(8,128)(2,1)S(1)}, bf16[272,384]{1,0:T(8,128)(2,1)S(1)}, u32[]{:S(2)}, u32[]{:S(2)}) collective-permute-start(bf16[272,384]{1,0:T(8,128)(2,1)S(1)} %get-tuple-element.54.refs_4_), channel_id=1, source_target_pairs={{0,16},{16,32},{32,48},{48,64},{64,80},{80,96},{96,112},{112,0},{1... | collective-permute-start | bytes 626696 | tf_op jit(solution)/shard_map/ppermute | solution.py:407
  75.4 9.0 %collective-permute-start.27 = (bf16[192,256]{1,0:T(8,128)(2,1)S(1)}, bf16[192,256]{1,0:T(8,128)(2,1)S(1)}, u32[]{:S(2)}, u32[]{:S(2)}) collective-permute-start(bf16[192,256]{1,0:T(8,128)(2,1)S(1)} %get-tuple-element.63), channel_id=1, source_target_pairs={{0,129},{1,128},{16,145},{17,144},{32,161},{33,160},{48,177},{49,1... | collective-permute-start | bytes 294920 | tf_op jit(solution)/shard_map/ppermute | solution.py:438
  76.7 7.7 %collective-permute-start.28 = (bf16[192,256]{1,0:T(8,128)(2,1)S(1)}, bf16[192,256]{1,0:T(8,128)(2,1)S(1)}, u32[]{:S(2)}, u32[]{:S(2)}) collective-permute-start(bf16[192,256]{1,0:T(8,128)(2,1)S(1)} %get-tuple-element.64), channel_id=1, source_target_pairs={{0,1},{1,0},{2,3},{3,2},{4,5},{5,4},{6,7},{7,6},{8,9},{9,8},{10,11... | collective-permute-start | bytes 294920 | tf_op jit(solution)/shard_map/ppermute | solution.py:429
  79.0 7.0 %collective-permute-start.31 = (bf16[192,256]{1,0:T(8,128)(2,1)S(1)}, bf16[192,256]{1,0:T(8,128)(2,1)S(1)}, u32[]{:S(2)}, u32[]{:S(2)}) collective-permute-start(bf16[192,256]{1,0:T(8,128)(2,1)S(1)} %get-tuple-element.67), channel_id=1, source_target_pairs={{0,1},{1,0},{2,3},{3,2},{4,5},{5,4},{6,7},{7,6},{8,9},{9,8},{10,11... | collective-permute-start | bytes 294920 | tf_op jit(solution)/shard_map/ppermute | solution.py:429
  80.6 6.4 %collective-permute-start.30 = (bf16[208,256]{1,0:T(8,128)(2,1)S(1)}, bf16[208,256]{1,0:T(8,128)(2,1)S(1)}, u32[]{:S(2)}, u32[]{:S(2)}) collective-permute-start(bf16[208,256]{1,0:T(8,128)(2,1)S(1)} %get-tuple-element.66), channel_id=1, source_target_pairs={{0,129},{1,128},{16,145},{17,144},{32,161},{33,160},{48,177},{49,1... | collective-permute-start | bytes 319496 | tf_op jit(solution)/shard_map/ppermute | solution.py:438
  82.7 5.7 %collective-permute-start.29 = (bf16[192,512]{1,0:T(8,128)(2,1)S(1)}, bf16[192,512]{1,0:T(8,128)(2,1)S(1)}, u32[]{:S(2)}, u32[]{:S(2)}) collective-permute-start(bf16[192,512]{1,0:T(8,128)(2,1)S(1)} %get-tuple-element.65), channel_id=1, source_target_pairs={{0,128},{16,144},{32,160},{48,176},{64,192},{80,208},{96,224},{112... | collective-permute-start | bytes 589832 | tf_op jit(solution)/shard_map/ppermute | solution.py:413

commit v6 on v5

--- a/solution.py
+++ b/solution.py
@@ -199,7 +199,7 @@
         [jax.ShapeDtypeStruct((HALF, PAIR), BF16)] * 2,
         (*ready, *received),
         after,
-        cost=3000000000.0,
+        cost=2500000000.0,
     )
 
 
@@ -215,7 +215,7 @@
         [jax.ShapeDtypeStruct((len(steps), PART + TAIL, PAIR), BF16)],
         (rows, panel),
         after,
-        cost=2000000000.0,
+        cost=1500000000.0,
     )
 
 

time: 89.8 us -> 89.8 us (level)
  no operation moved by 1% of the time
where the time goes in v6:
time: 89.8 us; the launch traced here: 89.5 us
  starting transfers between devices  46 us (51%)
  waiting for transfers between devices  23.3 us (26%)
  Pallas kernels  16.6 us (18%)
  local copies, waits for them, and re-layouts  2.8 us (3%)
  between operations  0.91 us (1%)
    ppermute x15, starting transfers between devices, z_shift(): lax.ppermute(x, 'rep', [(a * NZ + z, a * NZ + (z + d) % NZ) for a in rang...  24.4 us
    pallas_call x21, Pallas kernels, call(): pl.pallas_call(body, out_shape=out_shape, in_specs=[IN_VMEM] * (n + extra...  13.8 us
    ppermute x15, waiting for transfers between devices, z_shift(): lax.ppermute(x, 'rep', [(a * NZ + z, a * NZ + (z + d) % NZ) for a in rang...  11.8 us
    ppermute x6, starting transfers between devices, y_shift(): lax.ppermute(x, 'row', [(y * 2 + c, (y + d) % 4 * 2 + c) for y in range(4...  7.84 us
    ppermute x3, starting transfers between devices, half_swap(): return lax.ppermute(x, 'col', [(0, 1), (1, 0)])  6.62 us
    ppermute x5, waiting for transfers between devices, x_swap(): lax.ppermute(x, 'rep', [(a * NZ + z, (1 - a) * NZ + z) for a in range(2)...  3.73 us
    ppermute x5, starting transfers between devices, x_swap(): lax.ppermute(x, 'rep', [(a * NZ + z, (1 - a) * NZ + z) for a in range(2)...  3.67 us
    ppermute x2, starting transfers between devices, cross_swap(): return lax.ppermute(x, ('rep', 'col'), pairs)  3.32 us
  transfers between devices with their start and end apart: 32, of which 17 were waited for; matrix products, arithmetic and copies ran while one was open for 0% of the time, Pallas kernels for 17%

profile of v6, /device:TPU:16, one launch (start us, length us, event | category | flops | bytes accessed | tf_op | source)
XLA Modules:
  0.0 89.5 jit_solution(442093141679565123)
XLA Ops:
  0.6 3.1 %collective-permute-start = (bf16[64,1024]{1,0:T(8,128)(2,1)}, bf16[64,1024]{1,0:T(8,128)(2,1)S(1)}, u32[]{:S(2)}, u32[]{:S(2)}) collective-permute-start(bf16[64,1024]{1,0:T(8,128)(2,1)} %bitcast.5), channel_id=1, source_target_pairs={{0,1},{1,0},{2,3},{3,2},{4,5},{5,4},{6,7},{7,6},{8,9},{9,8},{10,11... | collective-permute-start | bytes 393224 | tf_op jit(solution)/shard_map/ppermute | solution.py:429
  3.8 1.3 %collective-permute-start.5 = (bf16[64,1024]{1,0:T(8,128)(2,1)}, bf16[64,1024]{1,0:T(8,128)(2,1)S(1)}, u32[]{:S(2)}, u32[]{:S(2)}) collective-permute-start(bf16[64,1024]{1,0:T(8,128)(2,1)} %bitcast.6), channel_id=1, source_target_pairs={{0,4},{2,6},{4,8},{6,10},{8,12},{10,14},{12,0},{14,2},{1,5},{3,7},... | collective-permute-start | bytes 393224 | tf_op jit(solution)/shard_map/ppermute | solution.py:419
  5.7 1.1 %collective-permute-start.1 = (bf16[64,1024]{1,0:T(8,128)(2,1)}, bf16[64,1024]{1,0:T(8,128)(2,1)S(1)}, u32[]{:S(2)}, u32[]{:S(2)}) collective-permute-start(bf16[64,1024]{1,0:T(8,128)(2,1)} %bitcast.8), channel_id=1, source_target_pairs={{0,12},{2,14},{4,0},{6,2},{8,4},{10,6},{12,8},{14,10},{1,13},{3,15... | collective-permute-start | bytes 393224 | tf_op jit(solution)/shard_map/ppermute | solution.py:419
  6.7 1.0 %collective-permute-done.refs_3_ = bf16[64,1024]{1,0:T(8,128)(2,1)S(1)} collective-permute-done((bf16[64,1024]{1,0:T(8,128)(2,1)}, bf16[64,1024]{1,0:T(8,128)(2,1)S(1)}, u32[]{:S(2)}, u32[]{:S(2)}) %collective-permute-start) | collective-permute-done | bytes 131104 | tf_op jit(solution)/shard_map/ppermute | solution.py:429
  7.7 1.3 %collective-permute-start.6 = (bf16[64,1024]{1,0:T(8,128)(2,1)S(1)}, bf16[64,1024]{1,0:T(8,128)(2,1)S(1)}, u32[]{:S(2)}, u32[]{:S(2)}) collective-permute-start(bf16[64,1024]{1,0:T(8,128)(2,1)S(1)} %collective-permute-done.refs_3_), channel_id=1, source_target_pairs={{0,4},{2,6},{4,8},{6,10},{8,12},{10,14},{12,0},{14,2},{1,5},{3,7},... | collective-permute-start | bytes 393224 | tf_op jit(solution)/shard_map/ppermute | solution.py:419
  9.0 1.6 %collective-permute-start.4 = (bf16[64,1024]{1,0:T(8,128)(2,1)S(1)}, bf16[64,1024]{1,0:T(8,128)(2,1)S(1)}, u32[]{:S(2)}, u32[]{:S(2)}) collective-permute-start(bf16[64,1024]{1,0:T(8,128)(2,1)S(1)} %collective-permute-done.refs_3_), channel_id=1, source_target_pairs={{0,8},{2,10},{4,12},{6,14},{8,0},{10,2},{12,4},{14,6},{1,9},{3,11}... | collective-permute-start | bytes 393224 | tf_op jit(solution)/shard_map/ppermute | solution.py:419
  10.6 2.0 %collective-permute-start.2 = (bf16[64,1024]{1,0:T(8,128)(2,1)S(1)}, bf16[64,1024]{1,0:T(8,128)(2,1)S(1)}, u32[]{:S(2)}, u32[]{:S(2)}) collective-permute-start(bf16[64,1024]{1,0:T(8,128)(2,1)S(1)} %collective-permute-done.refs_3_), channel_id=1, source_target_pairs={{0,12},{2,14},{4,0},{6,2},{8,4},{10,6},{12,8},{14,10},{1,13},{3,15... | collective-permute-start | bytes 393224 | tf_op jit(solution)/shard_map/ppermute | solution.py:419
  12.6 2.8 %copy-done = bf16[1024,3072]{1,0:T(8,128)(2,1)S(1)} copy-done((bf16[1024,3072]{1,0:T(8,128)(2,1)S(1)}, bf16[1024,3072]{1,0:T(8,128)(2,1)}, u32[]{:S(2)}) %copy-start) | copy-done | bytes 6291480
  15.3 2.3 %shard_map.68.refs_10_.refs_0_ = bf16[8,1024,384]{2,1,0:T(8,128)(2,1)S(1)} custom-call(bf16[1024,3072]{1,0:T(8,128)(2,1)S(1)} %copy-done, bf16[1024,3072]{1,0:T(8,128)(2,1)S(1)} %copy-done), custom_call_target="tpu_custom_call" | custom-call | bytes 12582912 | tf_op jit(solution)/shard_map/pallas_call | solution.py:76
  18.3 0.9 %collective-permute-done.2.refs_5_ = bf16[64,1024]{1,0:T(8,128)(2,1)S(1)} collective-permute-done((bf16[64,1024]{1,0:T(8,128)(2,1)S(1)}, bf16[64,1024]{1,0:T(8,128)(2,1)S(1)}, u32[]{:S(2)}, u32[]{:S(2)}) %collective-permute-start.2) | collective-permute-done | bytes 131104 | tf_op jit(solution)/shard_map/ppermute | solution.py:419
  20.6 1.5 %collective-permute-done.7.refs_1_.refs_2_ = bf16[528,1024]{1,0:T(8,128)(2,1)S(1)} collective-permute-done((bf16[528,1024]{1,0:T(8,128)(2,1)S(1)}, bf16[528,1024]{1,0:T(8,128)(2,1)S(1)}, u32[]{:S(2)}, u32[]{:S(2)}) %collective-permute-start.7) | collective-permute-done | bytes 1081376 | tf_op jit(solution)/shard_map/ppermute | solution.py:425
  22.9 2.0 %collective-permute-start.12 = (bf16[256,384]{1,0:T(8,128)(2,1)S(1)}, bf16[256,384]{1,0:T(8,128)(2,1)S(1)}, u32[]{:S(2)}, u32[]{:S(2)}) collective-permute-start(bf16[256,384]{1,0:T(8,128)(2,1)S(1)} %get-tuple-element.40), channel_id=1, source_target_pairs={{0,16},{16,32},{32,48},{48,64},{64,80},{80,96},{96,112},{112,0},{1... | collective-permute-start | bytes 589832 | tf_op jit(solution)/shard_map/ppermute | solution.py:407
  24.9 4.0 %collective-permute-start.11 = (bf16[256,384]{1,0:T(8,128)(2,1)S(1)}, bf16[256,384]{1,0:T(8,128)(2,1)S(1)}, u32[]{:S(2)}, u32[]{:S(2)}) collective-permute-start(bf16[256,384]{1,0:T(8,128)(2,1)S(1)} %get-tuple-element.37.refs_2_), channel_id=1, source_target_pairs={{0,112},{16,0},{32,16},{48,32},{64,48},{80,64},{96,80},{112,96},{1... | collective-permute-start | bytes 589832 | tf_op jit(solution)/shard_map/ppermute | solution.py:407
  28.9 0.8 shard_map.73.refs_3_
  31.1 1.3 %shard_map.75 = (f32[512,384]{1,0:T(8,128)S(1)}, f32[512,384]{1,0:T(8,128)S(1)}) custom-call(bf16[8,1024,384]{2,1,0:T(8,128)(2,1)S(1)} %shard_map.68.refs_10_.refs_0_, bf16[528,1024]{1,0:T(8,128)(2,1)S(1)} %collective-permute-done.7.refs_1_.refs_2_, bf16[272,384]{1,0:T(8,128)(2,1)S(1)} %shard_map.74.refs_2_), custom_call_target="tpu_custom_call" | custom-call | flops 1000000000 | bytes 1 | tf_op jit(solution)/shard_map/pallas_call | solution.py:27
  32.4 1.7 %collective-permute-done.12.refs_3_ = bf16[256,384]{1,0:T(8,128)(2,1)S(1)} collective-permute-done((bf16[256,384]{1,0:T(8,128)(2,1)S(1)}, bf16[256,384]{1,0:T(8,128)(2,1)S(1)}, u32[]{:S(2)}, u32[]{:S(2)}) %collective-permute-start.12) | collective-permute-done | bytes 196640 | tf_op jit(solution)/shard_map/ppermute | solution.py:407
  34.2 3.2 %collective-permute-start.13 = (bf16[512,384]{1,0:T(8,128)(2,1)S(1)}, bf16[512,384]{1,0:T(8,128)(2,1)S(1)}, u32[]{:S(2)}, u32[]{:S(2)}) collective-permute-start(bf16[512,384]{1,0:T(8,128)(2,1)S(1)} %get-tuple-element.41.refs_4_), channel_id=1, source_target_pairs={{0,112},{16,0},{32,16},{48,32},{64,48},{80,64},{96,80},{112,96},{1... | collective-permute-start | bytes 1179656 | tf_op jit(solution)/shard_map/ppermute | solution.py:407
  37.4 2.9 %collective-permute-done.10.refs_3_ = bf16[272,384]{1,0:T(8,128)(2,1)S(1)} collective-permute-done((bf16[272,384]{1,0:T(8,128)(2,1)S(1)}, bf16[272,384]{1,0:T(8,128)(2,1)S(1)}, u32[]{:S(2)}, u32[]{:S(2)}) %collective-permute-start.10) | collective-permute-done | bytes 208928 | tf_op jit(solution)/shard_map/ppermute | solution.py:407
  40.3 0.8 collective-permute-done.8.refs_2_
  41.1 0.8 shard_map.77
  41.9 1.7 %collective-permute-start.18 = (bf16[272,384]{1,0:T(8,128)(2,1)S(1)}, bf16[272,384]{1,0:T(8,128)(2,1)S(1)}, u32[]{:S(2)}, u32[]{:S(2)}) collective-permute-start(bf16[272,384]{1,0:T(8,128)(2,1)S(1)} %get-tuple-element.47), channel_id=1, source_target_pairs={{0,112},{16,0},{32,16},{48,32},{64,48},{80,64},{96,80},{112,96},{1... | collective-permute-start | bytes 626696 | tf_op jit(solution)/shard_map/ppermute | solution.py:407
  44.8 0.8 collective-permute-start.16
  45.5 1.3 %shard_map.79 = (f32[512,384]{1,0:T(8,128)S(1)}, f32[512,384]{1,0:T(8,128)S(1)}) custom-call(bf16[8,1024,384]{2,1,0:T(8,128)(2,1)S(1)} %shard_map.68.refs_10_.refs_0_, bf16[528,1024]{1,0:T(8,128)(2,1)S(1)} %collective-permute-done.7.refs_1_.refs_2_, bf16[2,272,384]{2,1,0:T(8,128)(2,1)S(1)} %shard_map.78.refs_2_), custom_call_target="tpu_custom_call" | custom-call | flops 1000000000 | bytes 1 | tf_op jit(solution)/shard_map/pallas_call | solution.py:27
  46.8 2.0 %collective-permute-done.14.refs_3_ = bf16[512,384]{1,0:T(8,128)(2,1)S(1)} collective-permute-done((bf16[512,384]{1,0:T(8,128)(2,1)S(1)}, bf16[512,384]{1,0:T(8,128)(2,1)S(1)}, u32[]{:S(2)}, u32[]{:S(2)}) %collective-permute-start.14) | collective-permute-done | bytes 393248 | tf_op jit(solution)/shard_map/ppermute | solution.py:407
  48.9 1.2 %collective-permute-start.22 = (bf16[512,384]{1,0:T(8,128)(2,1)S(1)}, bf16[512,384]{1,0:T(8,128)(2,1)S(1)}, u32[]{:S(2)}, u32[]{:S(2)}) collective-permute-start(bf16[512,384]{1,0:T(8,128)(2,1)S(1)} %get-tuple-element.52), channel_id=1, source_target_pairs={{0,16},{16,32},{32,48},{48,64},{64,80},{80,96},{96,112},{112,0},{1... | collective-permute-start | bytes 1179656 | tf_op jit(solution)/shard_map/ppermute | solution.py:407
  50.1 2.1 %collective-permute-start.21 = (bf16[512,384]{1,0:T(8,128)(2,1)S(1)}, bf16[512,384]{1,0:T(8,128)(2,1)S(1)}, u32[]{:S(2)}, u32[]{:S(2)}) collective-permute-start(bf16[512,384]{1,0:T(8,128)(2,1)S(1)} %get-tuple-element.46.refs_2_), channel_id=1, source_target_pairs={{0,112},{16,0},{32,16},{48,32},{64,48},{80,64},{96,80},{112,96},{1... | collective-permute-start | bytes 1179656 | tf_op jit(solution)/shard_map/ppermute | solution.py:407
  52.2 1.0 %shard_map.81.refs_5_ = bf16[3,272,384]{2,1,0:T(8,128)(2,1)S(1)} custom-call(bf16[8,1024,384]{2,1,0:T(8,128)(2,1)S(1)} %shard_map.68.refs_10_.refs_0_, bf16[528,1024]{1,0:T(8,128)(2,1)S(1)} %shard_map.70.refs_1_, bf16[512,384]{1,0:T(8,128)(2,1)S(1)} %get-tuple-element.46.refs_2_), custom_call_target="tpu_custom_call" | custom-call | flops 1500000000 | bytes 1 | tf_op jit(solution)/shard_map/pallas_call | solution.py:27
  53.3 1.6 %collective-permute-start.15 = (bf16[3,272,384]{2,1,0:T(8,128)(2,1)S(1)}, bf16[3,272,384]{2,1,0:T(8,128)(2,1)S(1)}, u32[]{:S(2)}, u32[]{:S(2)}) collective-permute-start(bf16[3,272,384]{2,1,0:T(8,128)(2,1)S(1)} %shard_map.81.refs_5_), channel_id=1, source_target_pairs={{0,128},{16,144},{32,160},{48,176},{64,192},{80,208},{96,224},{112... | collective-permute-start | bytes 1880072 | tf_op jit(solution)/shard_map/ppermute | solution.py:413
  54.8 1.5 %collective-permute-done.16.refs_2_ = bf16[2,272,384]{2,1,0:T(8,128)(2,1)S(1)} collective-permute-done((bf16[2,272,384]{2,1,0:T(8,128)(2,1)S(1)}, bf16[2,272,384]{2,1,0:T(8,128)(2,1)S(1)}, u32[]{:S(2)}, u32[]{:S(2)}) %collective-permute-start.16) | collective-permute-done | bytes 417824 | tf_op jit(solution)/shard_map/ppermute | solution.py:413
  56.4 0.8 shard_map.82
  57.2 3.9 %collective-permute-start.20 = (bf16[272,384]{1,0:T(8,128)(2,1)S(1)}, bf16[272,384]{1,0:T(8,128)(2,1)S(1)}, u32[]{:S(2)}, u32[]{:S(2)}) collective-permute-start(bf16[272,384]{1,0:T(8,128)(2,1)S(1)} %get-tuple-element.49), channel_id=1, source_target_pairs={{0,112},{16,0},{32,16},{48,32},{64,48},{80,64},{96,80},{112,96},{1... | collective-permute-start | bytes 626696 | tf_op jit(solution)/shard_map/ppermute | solution.py:407
  61.1 1.3 %shard_map.83 = (f32[512,384]{1,0:T(8,128)S(1)}, f32[512,384]{1,0:T(8,128)S(1)}) custom-call(bf16[8,1024,384]{2,1,0:T(8,128)(2,1)S(1)} %shard_map.68.refs_10_.refs_0_, bf16[528,1024]{1,0:T(8,128)(2,1)S(1)} %collective-permute-done.7.refs_1_.refs_2_, bf16[272,384]{1,0:T(8,128)(2,1)S(1)} %get-tuple-element.48.refs_2_), custom_call_target="tpu_custom_call" | custom-call | flops 1000000000 | bytes 1 | tf_op jit(solution)/shard_map/pallas_call | solution.py:27
  62.5 1.5 %collective-permute-start.24 = (bf16[512,384]{1,0:T(8,128)(2,1)S(1)}, bf16[512,384]{1,0:T(8,128)(2,1)S(1)}, u32[]{:S(2)}, u32[]{:S(2)}) collective-permute-start(bf16[512,384]{1,0:T(8,128)(2,1)S(1)} %get-tuple-element.57), channel_id=1, source_target_pairs={{0,16},{16,32},{32,48},{48,64},{64,80},{80,96},{96,112},{112,0},{1... | collective-permute-start | bytes 1179656 | tf_op jit(solution)/shard_map/ppermute | solution.py:407
  64.1 1.9 %collective-permute-start.23 = (bf16[512,384]{1,0:T(8,128)(2,1)S(1)}, bf16[512,384]{1,0:T(8,128)(2,1)S(1)}, u32[]{:S(2)}, u32[]{:S(2)}) collective-permute-start(bf16[512,384]{1,0:T(8,128)(2,1)S(1)} %get-tuple-element.53.refs_5_), channel_id=1, source_target_pairs={{0,112},{16,0},{32,16},{48,32},{64,48},{80,64},{96,80},{112,96},{1... | collective-permute-start | bytes 1179656 | tf_op jit(solution)/shard_map/ppermute | solution.py:407
  66.5 2.9 %collective-permute-done.19.refs_3_ = bf16[272,384]{1,0:T(8,128)(2,1)S(1)} collective-permute-done((bf16[272,384]{1,0:T(8,128)(2,1)S(1)}, bf16[272,384]{1,0:T(8,128)(2,1)S(1)}, u32[]{:S(2)}, u32[]{:S(2)}) %collective-permute-start.19) | collective-permute-done | bytes 208928 | tf_op jit(solution)/shard_map/ppermute | solution.py:407
  69.4 0.8 shard_map.85
  70.2 1.5 %collective-permute-start.26 = (bf16[272,384]{1,0:T(8,128)(2,1)S(1)}, bf16[272,384]{1,0:T(8,128)(2,1)S(1)}, u32[]{:S(2)}, u32[]{:S(2)}) collective-permute-start(bf16[272,384]{1,0:T(8,128)(2,1)S(1)} %get-tuple-element.59), channel_id=1, source_target_pairs={{0,112},{16,0},{32,16},{48,32},{64,48},{80,64},{96,80},{112,96},{1... | collective-permute-start | bytes 626696 | tf_op jit(solution)/shard_map/ppermute | solution.py:407
  72.3 1.0 %shard_map.86 = (f32[272,384]{1,0:T(8,128)S(1)}, f32[512,384]{1,0:T(8,128)S(1)}) custom-call(bf16[8,1024,384]{2,1,0:T(8,128)(2,1)S(1)} %shard_map.68.refs_10_.refs_0_, bf16[528,1024]{1,0:T(8,128)(2,1)S(1)} %shard_map.70.refs_1_, bf16[528,1024]{1,0:T(8,128)(2,1)S(1)} %collective-permute-done.7.refs_1_.refs_2_, ...), custom_call_target="tpu_custom_call" | custom-call | flops 1000000000 | bytes 1 | tf_op jit(solution)/shard_map/pallas_call | solution.py:27
  73.3 1.4 %collective-permute-done.24.refs_2_ = bf16[512,384]{1,0:T(8,128)(2,1)S(1)} collective-permute-done((bf16[512,384]{1,0:T(8,128)(2,1)S(1)}, bf16[512,384]{1,0:T(8,128)(2,1)S(1)}, u32[]{:S(2)}, u32[]{:S(2)}) %collective-permute-start.24) | collective-permute-done | bytes 393248 | tf_op jit(solution)/shard_map/ppermute | solution.py:407
  75.4 1.2 %collective-permute-start.27 = (bf16[192,256]{1,0:T(8,128)(2,1)S(1)}, bf16[192,256]{1,0:T(8,128)(2,1)S(1)}, u32[]{:S(2)}, u32[]{:S(2)}) collective-permute-start(bf16[192,256]{1,0:T(8,128)(2,1)S(1)} %get-tuple-element.63), channel_id=1, source_target_pairs={{0,129},{1,128},{16,145},{17,144},{32,161},{33,160},{48,177},{49,1... | collective-permute-start | bytes 294920 | tf_op jit(solution)/shard_map/ppermute | solution.py:438
  76.7 1.9 %collective-permute-start.28 = (bf16[192,256]{1,0:T(8,128)(2,1)S(1)}, bf16[192,256]{1,0:T(8,128)(2,1)S(1)}, u32[]{:S(2)}, u32[]{:S(2)}) collective-permute-start(bf16[192,256]{1,0:T(8,128)(2,1)S(1)} %get-tuple-element.64), channel_id=1, source_target_pairs={{0,1},{1,0},{2,3},{3,2},{4,5},{5,4},{6,7},{7,6},{8,9},{9,8},{10,11... | collective-permute-start | bytes 294920 | tf_op jit(solution)/shard_map/ppermute | solution.py:429
  79.0 1.6 %collective-permute-start.31 = (bf16[192,256]{1,0:T(8,128)(2,1)S(1)}, bf16[192,256]{1,0:T(8,128)(2,1)S(1)}, u32[]{:S(2)}, u32[]{:S(2)}) collective-permute-start(bf16[192,256]{1,0:T(8,128)(2,1)S(1)} %get-tuple-element.67), channel_id=1, source_target_pairs={{0,1},{1,0},{2,3},{3,2},{4,5},{5,4},{6,7},{7,6},{8,9},{9,8},{10,11... | collective-permute-start | bytes 294920 | tf_op jit(solution)/shard_map/ppermute | solution.py:429
  80.6 2.1 %collective-permute-start.30 = (bf16[208,256]{1,0:T(8,128)(2,1)S(1)}, bf16[208,256]{1,0:T(8,128)(2,1)S(1)}, u32[]{:S(2)}, u32[]{:S(2)}) collective-permute-start(bf16[208,256]{1,0:T(8,128)(2,1)S(1)} %get-tuple-element.66), channel_id=1, source_target_pairs={{0,129},{1,128},{16,145},{17,144},{32,161},{33,160},{48,177},{49,1... | collective-permute-start | bytes 319496 | tf_op jit(solution)/shard_map/ppermute | solution.py:438
  82.7 1.7 %collective-permute-done.27.refs_0_ = bf16[192,256]{1,0:T(8,128)(2,1)S(1)} collective-permute-done((bf16[192,256]{1,0:T(8,128)(2,1)S(1)}, bf16[192,256]{1,0:T(8,128)(2,1)S(1)}, u32[]{:S(2)}, u32[]{:S(2)}) %collective-permute-start.27) | collective-permute-done | bytes 98336 | tf_op jit(solution)/shard_map/ppermute | solution.py:438
  84.4 1.6 %collective-permute-done.31.refs_6_ = bf16[192,256]{1,0:T(8,128)(2,1)S(1)} collective-permute-done((bf16[192,256]{1,0:T(8,128)(2,1)S(1)}, bf16[192,256]{1,0:T(8,128)(2,1)S(1)}, u32[]{:S(2)}, u32[]{:S(2)}) %collective-permute-start.31) | collective-permute-done | bytes 98336 | tf_op jit(solution)/shard_map/ppermute | solution.py:429
  86.0 1.0 %collective-permute-done.30.refs_5_ = bf16[208,256]{1,0:T(8,128)(2,1)S(1)} collective-permute-done((bf16[208,256]{1,0:T(8,128)(2,1)S(1)}, bf16[208,256]{1,0:T(8,128)(2,1)S(1)}, u32[]{:S(2)}, u32[]{:S(2)}) %collective-permute-start.30) | collective-permute-done | bytes 106528 | tf_op jit(solution)/shard_map/ppermute | solution.py:438
  87.0 1.4 %collective-permute-done.29.refs_4_ = bf16[192,512]{1,0:T(8,128)(2,1)S(1)} collective-permute-done((bf16[192,512]{1,0:T(8,128)(2,1)S(1)}, bf16[192,512]{1,0:T(8,128)(2,1)S(1)}, u32[]{:S(2)}, u32[]{:S(2)}) %collective-permute-start.29) | collective-permute-done | bytes 196640 | tf_op jit(solution)/shard_map/ppermute | solution.py:413
  88.4 1.2 %shard_map.90 = (f32[1,2,192,512]{3,2,1,0:T(8,128)}, f32[1,2,192]{2,1,0:T(2,128)}) custom-call(f32[192,128]{1,0:T(8,128)S(1)} %get-tuple-element.61.refs_2_.refs_0_, f32[192,256]{1,0:T(8,128)S(1)} %get-tuple-element.60.refs_4_.refs_1_, f32[8,192]{1,0:T(8,128)S(1)} %get-tuple-element.62.refs_2_, f32[192,256]{1,0:T(8,128)S(1)} %shard_map.89.refs_3_, ...), custom_call_target="tpu_custom_call" | custom-call | flops 4000000000 | bytes 1 | tf_op jit(solution)/shard_map/pallas_call | solution.py:27
  (49 shorter events, 8.8 us)
Async XLA Ops:
  0.6 17.0 %copy-start.4 = (f32[8]{0:T(128)S(1)}, f32[8]{0:T(128)}, u32[]{:S(2)}) copy-start(f32[8]{0:T(128)} %sigma_ref.1) | copy-start | bytes 100
  0.6 7.0 %collective-permute-start = (bf16[64,1024]{1,0:T(8,128)(2,1)}, bf16[64,1024]{1,0:T(8,128)(2,1)S(1)}, u32[]{:S(2)}, u32[]{:S(2)}) collective-permute-start(bf16[64,1024]{1,0:T(8,128)(2,1)} %bitcast.5), channel_id=1, source_target_pairs={{0,1},{1,0},{2,3},{3,2},{4,5},{5,4},{6,7},{7,6},{8,9},{9,8},{10,11... | collective-permute-start | bytes 393224 | tf_op jit(solution)/shard_map/ppermute | solution.py:429
  3.8 6.8 %collective-permute-start.5 = (bf16[64,1024]{1,0:T(8,128)(2,1)}, bf16[64,1024]{1,0:T(8,128)(2,1)S(1)}, u32[]{:S(2)}, u32[]{:S(2)}) collective-permute-start(bf16[64,1024]{1,0:T(8,128)(2,1)} %bitcast.6), channel_id=1, source_target_pairs={{0,4},{2,6},{4,8},{6,10},{8,12},{10,14},{12,0},{14,2},{1,5},{3,7},... | collective-permute-start | bytes 393224 | tf_op jit(solution)/shard_map/ppermute | solution.py:419
  5.0 13.2 %collective-permute-start.3 = (bf16[64,1024]{1,0:T(8,128)(2,1)}, bf16[64,1024]{1,0:T(8,128)(2,1)S(1)}, u32[]{:S(2)}, u32[]{:S(2)}) collective-permute-start(bf16[64,1024]{1,0:T(8,128)(2,1)} %bitcast.7), channel_id=1, source_target_pairs={{0,8},{2,10},{4,12},{6,14},{8,0},{10,2},{12,4},{14,6},{1,9},{3,11}... | collective-permute-start | bytes 393224 | tf_op jit(solution)/shard_map/ppermute | solution.py:419
  5.7 12.6 %collective-permute-start.1 = (bf16[64,1024]{1,0:T(8,128)(2,1)}, bf16[64,1024]{1,0:T(8,128)(2,1)S(1)}, u32[]{:S(2)}, u32[]{:S(2)}) collective-permute-start(bf16[64,1024]{1,0:T(8,128)(2,1)} %bitcast.8), channel_id=1, source_target_pairs={{0,12},{2,14},{4,0},{6,2},{8,4},{10,6},{12,8},{14,10},{1,13},{3,15... | collective-permute-start | bytes 393224 | tf_op jit(solution)/shard_map/ppermute | solution.py:419
  7.7 10.6 %collective-permute-start.6 = (bf16[64,1024]{1,0:T(8,128)(2,1)S(1)}, bf16[64,1024]{1,0:T(8,128)(2,1)S(1)}, u32[]{:S(2)}, u32[]{:S(2)}) collective-permute-start(bf16[64,1024]{1,0:T(8,128)(2,1)S(1)} %collective-permute-done.refs_3_), channel_id=1, source_target_pairs={{0,4},{2,6},{4,8},{6,10},{8,12},{10,14},{12,0},{14,2},{1,5},{3,7},... | collective-permute-start | bytes 393224 | tf_op jit(solution)/shard_map/ppermute | solution.py:419
  9.0 9.3 %collective-permute-start.4 = (bf16[64,1024]{1,0:T(8,128)(2,1)S(1)}, bf16[64,1024]{1,0:T(8,128)(2,1)S(1)}, u32[]{:S(2)}, u32[]{:S(2)}) collective-permute-start(bf16[64,1024]{1,0:T(8,128)(2,1)S(1)} %collective-permute-done.refs_3_), channel_id=1, source_target_pairs={{0,8},{2,10},{4,12},{6,14},{8,0},{10,2},{12,4},{14,6},{1,9},{3,11}... | collective-permute-start | bytes 393224 | tf_op jit(solution)/shard_map/ppermute | solution.py:419
  10.6 8.6 %collective-permute-start.2 = (bf16[64,1024]{1,0:T(8,128)(2,1)S(1)}, bf16[64,1024]{1,0:T(8,128)(2,1)S(1)}, u32[]{:S(2)}, u32[]{:S(2)}) collective-permute-start(bf16[64,1024]{1,0:T(8,128)(2,1)S(1)} %collective-permute-done.refs_3_), channel_id=1, source_target_pairs={{0,12},{2,14},{4,0},{6,2},{8,4},{10,6},{12,8},{14,10},{1,13},{3,15... | collective-permute-start | bytes 393224 | tf_op jit(solution)/shard_map/ppermute | solution.py:419
  12.6 2.8 %copy-start = (bf16[1024,3072]{1,0:T(8,128)(2,1)S(1)}, bf16[1024,3072]{1,0:T(8,128)(2,1)}, u32[]{:S(2)}) copy-start(bf16[1024,3072]{1,0:T(8,128)(2,1)} %second_ref.1) | copy-start | bytes 18874372
  15.3 2.3 %copy-start.2 = (f32[1024]{0:T(1024)S(1)}, f32[1024]{0:T(1024)}, u32[]{:S(2)}) copy-start(f32[1024]{0:T(1024)} %param.7) | copy-start | bytes 12292
  15.3 2.3 %copy-start.3 = (s32[1024]{0:T(1024)S(1)}, s32[1024]{0:T(1024)}, u32[]{:S(2)}) copy-start(s32[1024]{0:T(1024)} %param.8) | copy-start | bytes 12292
  15.3 3.8 %copy-start.1 = (bf16[1024,1,64]{0,2,1:T(8,128)(2,1)S(1)}, bf16[1024,1,64]{0,2,1:T(8,128)(2,1)}, u32[]{:S(2)}) copy-start(bf16[1024,1,64]{0,2,1:T(8,128)(2,1)} %param.6) | copy-start | bytes 393220
  19.4 2.8 %collective-permute-start.7 = (bf16[528,1024]{1,0:T(8,128)(2,1)S(1)}, bf16[528,1024]{1,0:T(8,128)(2,1)S(1)}, u32[]{:S(2)}, u32[]{:S(2)}) collective-permute-start(bf16[528,1024]{1,0:T(8,128)(2,1)S(1)} %shard_map.70.refs_1_), channel_id=1, source_target_pairs={{0,2},{2,0},{4,6},{6,4},{8,10},{10,8},{12,14},{14,12},{1,3},{3,1},... | collective-permute-start | bytes 3244040 | tf_op jit(solution)/shard_map/ppermute | solution.py:425
  19.9 10.4 %collective-permute-start.9 = (bf16[1,272,384]{2,1,0:T(8,128)(2,1)S(1)}, bf16[1,272,384]{2,1,0:T(8,128)(2,1)S(1)}, u32[]{:S(2)}, u32[]{:S(2)}) collective-permute-start(bf16[1,272,384]{2,1,0:T(8,128)(2,1)S(1)} %shard_map.71.refs_2_), channel_id=1, source_target_pairs={{0,128},{16,144},{32,160},{48,176},{64,192},{80,208},{96,224},{112... | collective-permute-start | bytes 626696 | tf_op jit(solution)/shard_map/ppermute | solution.py:413
  22.9 11.1 %collective-permute-start.12 = (bf16[256,384]{1,0:T(8,128)(2,1)S(1)}, bf16[256,384]{1,0:T(8,128)(2,1)S(1)}, u32[]{:S(2)}, u32[]{:S(2)}) collective-permute-start(bf16[256,384]{1,0:T(8,128)(2,1)S(1)} %get-tuple-element.40), channel_id=1, source_target_pairs={{0,16},{16,32},{32,48},{48,64},{64,80},{80,96},{96,112},{112,0},{1... | collective-permute-start | bytes 589832 | tf_op jit(solution)/shard_map/ppermute | solution.py:407
  24.9 9.1 %collective-permute-start.11 = (bf16[256,384]{1,0:T(8,128)(2,1)S(1)}, bf16[256,384]{1,0:T(8,128)(2,1)S(1)}, u32[]{:S(2)}, u32[]{:S(2)}) collective-permute-start(bf16[256,384]{1,0:T(8,128)(2,1)S(1)} %get-tuple-element.37.refs_2_), channel_id=1, source_target_pairs={{0,112},{16,0},{32,16},{48,32},{64,48},{80,64},{96,80},{112,96},{1... | collective-permute-start | bytes 589832 | tf_op jit(solution)/shard_map/ppermute | solution.py:407
  29.7 11.5 %collective-permute-start.8 = (bf16[2,272,384]{2,1,0:T(8,128)(2,1)S(1)}, bf16[2,272,384]{2,1,0:T(8,128)(2,1)S(1)}, u32[]{:S(2)}, u32[]{:S(2)}) collective-permute-start(bf16[2,272,384]{2,1,0:T(8,128)(2,1)S(1)} %shard_map.73.refs_3_), channel_id=1, source_target_pairs={{0,128},{16,144},{32,160},{48,176},{64,192},{80,208},{96,224},{112... | collective-permute-start | bytes 1253384 | tf_op jit(solution)/shard_map/ppermute | solution.py:413
  30.8 9.5 %collective-permute-start.10 = (bf16[272,384]{1,0:T(8,128)(2,1)S(1)}, bf16[272,384]{1,0:T(8,128)(2,1)S(1)}, u32[]{:S(2)}, u32[]{:S(2)}) collective-permute-start(bf16[272,384]{1,0:T(8,128)(2,1)S(1)} %shard_map.74.refs_2_), channel_id=1, source_target_pairs={{0,16},{16,32},{32,48},{48,64},{64,80},{80,96},{96,112},{112,0},{1... | collective-permute-start | bytes 626696 | tf_op jit(solution)/shard_map/ppermute | solution.py:407
  34.1 14.6 %collective-permute-start.14 = (bf16[512,384]{1,0:T(8,128)(2,1)S(1)}, bf16[512,384]{1,0:T(8,128)(2,1)S(1)}, u32[]{:S(2)}, u32[]{:S(2)}) collective-permute-start(bf16[512,384]{1,0:T(8,128)(2,1)S(1)} %get-tuple-element.45), channel_id=1, source_target_pairs={{0,16},{16,32},{32,48},{48,64},{64,80},{80,96},{96,112},{112,0},{1... | collective-permute-start | bytes 1179656 | tf_op jit(solution)/shard_map/ppermute | solution.py:407
  34.2 14.5 %collective-permute-start.13 = (bf16[512,384]{1,0:T(8,128)(2,1)S(1)}, bf16[512,384]{1,0:T(8,128)(2,1)S(1)}, u32[]{:S(2)}, u32[]{:S(2)}) collective-permute-start(bf16[512,384]{1,0:T(8,128)(2,1)S(1)} %get-tuple-element.41.refs_4_), channel_id=1, source_target_pairs={{0,112},{16,0},{32,16},{48,32},{64,48},{80,64},{96,80},{112,96},{1... | collective-permute-start | bytes 1179656 | tf_op jit(solution)/shard_map/ppermute | solution.py:407
  41.9 11.4 %collective-permute-start.18 = (bf16[272,384]{1,0:T(8,128)(2,1)S(1)}, bf16[272,384]{1,0:T(8,128)(2,1)S(1)}, u32[]{:S(2)}, u32[]{:S(2)}) collective-permute-start(bf16[272,384]{1,0:T(8,128)(2,1)S(1)} %get-tuple-element.47), channel_id=1, source_target_pairs={{0,112},{16,0},{32,16},{48,32},{64,48},{80,64},{96,80},{112,96},{1... | collective-permute-start | bytes 626696 | tf_op jit(solution)/shard_map/ppermute | solution.py:407
  43.7 11.2 %collective-permute-start.17 = (bf16[272,384]{1,0:T(8,128)(2,1)S(1)}, bf16[272,384]{1,0:T(8,128)(2,1)S(1)}, u32[]{:S(2)}, u32[]{:S(2)}) collective-permute-start(bf16[272,384]{1,0:T(8,128)(2,1)S(1)} %get-tuple-element.42.refs_2_), channel_id=1, source_target_pairs={{0,16},{16,32},{32,48},{48,64},{64,80},{80,96},{96,112},{112,0},{1... | collective-permute-start | bytes 626696 | tf_op jit(solution)/shard_map/ppermute | solution.py:407
  44.8 11.6 %collective-permute-start.16 = (bf16[2,272,384]{2,1,0:T(8,128)(2,1)S(1)}, bf16[2,272,384]{2,1,0:T(8,128)(2,1)S(1)}, u32[]{:S(2)}, u32[]{:S(2)}) collective-permute-start(bf16[2,272,384]{2,1,0:T(8,128)(2,1)S(1)} %shard_map.78.refs_2_), channel_id=1, source_target_pairs={{0,128},{16,144},{32,160},{48,176},{64,192},{80,208},{96,224},{112... | collective-permute-start | bytes 1253384 | tf_op jit(solution)/shard_map/ppermute | solution.py:413
  48.9 13.4 %collective-permute-start.22 = (bf16[512,384]{1,0:T(8,128)(2,1)S(1)}, bf16[512,384]{1,0:T(8,128)(2,1)S(1)}, u32[]{:S(2)}, u32[]{:S(2)}) collective-permute-start(bf16[512,384]{1,0:T(8,128)(2,1)S(1)} %get-tuple-element.52), channel_id=1, source_target_pairs={{0,16},{16,32},{32,48},{48,64},{64,80},{80,96},{96,112},{112,0},{1... | collective-permute-start | bytes 1179656 | tf_op jit(solution)/shard_map/ppermute | solution.py:407
  50.1 12.2 %collective-permute-start.21 = (bf16[512,384]{1,0:T(8,128)(2,1)S(1)}, bf16[512,384]{1,0:T(8,128)(2,1)S(1)}, u32[]{:S(2)}, u32[]{:S(2)}) collective-permute-start(bf16[512,384]{1,0:T(8,128)(2,1)S(1)} %get-tuple-element.46.refs_2_), channel_id=1, source_target_pairs={{0,112},{16,0},{32,16},{48,32},{64,48},{80,64},{96,80},{112,96},{1... | collective-permute-start | bytes 1179656 | tf_op jit(solution)/shard_map/ppermute | solution.py:407
  53.3 16.1 %collective-permute-start.15 = (bf16[3,272,384]{2,1,0:T(8,128)(2,1)S(1)}, bf16[3,272,384]{2,1,0:T(8,128)(2,1)S(1)}, u32[]{:S(2)}, u32[]{:S(2)}) collective-permute-start(bf16[3,272,384]{2,1,0:T(8,128)(2,1)S(1)} %shard_map.81.refs_5_), channel_id=1, source_target_pairs={{0,128},{16,144},{32,160},{48,176},{64,192},{80,208},{96,224},{112... | collective-permute-start | bytes 1880072 | tf_op jit(solution)/shard_map/ppermute | solution.py:413
  57.2 9.4 %collective-permute-start.20 = (bf16[272,384]{1,0:T(8,128)(2,1)S(1)}, bf16[272,384]{1,0:T(8,128)(2,1)S(1)}, u32[]{:S(2)}, u32[]{:S(2)}) collective-permute-start(bf16[272,384]{1,0:T(8,128)(2,1)S(1)} %get-tuple-element.49), channel_id=1, source_target_pairs={{0,112},{16,0},{32,16},{48,32},{64,48},{80,64},{96,80},{112,96},{1... | collective-permute-start | bytes 626696 | tf_op jit(solution)/shard_map/ppermute | solution.py:407
  61.1 8.4 %collective-permute-start.19 = (bf16[272,384]{1,0:T(8,128)(2,1)S(1)}, bf16[272,384]{1,0:T(8,128)(2,1)S(1)}, u32[]{:S(2)}, u32[]{:S(2)}) collective-permute-start(bf16[272,384]{1,0:T(8,128)(2,1)S(1)} %get-tuple-element.48.refs_2_), channel_id=1, source_target_pairs={{0,16},{16,32},{32,48},{48,64},{64,80},{80,96},{96,112},{112,0},{1... | collective-permute-start | bytes 626696 | tf_op jit(solution)/shard_map/ppermute | solution.py:407
  62.5 12.2 %collective-permute-start.24 = (bf16[512,384]{1,0:T(8,128)(2,1)S(1)}, bf16[512,384]{1,0:T(8,128)(2,1)S(1)}, u32[]{:S(2)}, u32[]{:S(2)}) collective-permute-start(bf16[512,384]{1,0:T(8,128)(2,1)S(1)} %get-tuple-element.57), channel_id=1, source_target_pairs={{0,16},{16,32},{32,48},{48,64},{64,80},{80,96},{96,112},{112,0},{1... | collective-permute-start | bytes 1179656 | tf_op jit(solution)/shard_map/ppermute | solution.py:407
  64.1 11.0 %collective-permute-start.23 = (bf16[512,384]{1,0:T(8,128)(2,1)S(1)}, bf16[512,384]{1,0:T(8,128)(2,1)S(1)}, u32[]{:S(2)}, u32[]{:S(2)}) collective-permute-start(bf16[512,384]{1,0:T(8,128)(2,1)S(1)} %get-tuple-element.53.refs_5_), channel_id=1, source_target_pairs={{0,112},{16,0},{32,16},{48,32},{64,48},{80,64},{96,80},{112,96},{1... | collective-permute-start | bytes 1179656 | tf_op jit(solution)/shard_map/ppermute | solution.py:407
  70.2 8.4 %collective-permute-start.26 = (bf16[272,384]{1,0:T(8,128)(2,1)S(1)}, bf16[272,384]{1,0:T(8,128)(2,1)S(1)}, u32[]{:S(2)}, u32[]{:S(2)}) collective-permute-start(bf16[272,384]{1,0:T(8,128)(2,1)S(1)} %get-tuple-element.59), channel_id=1, source_target_pairs={{0,112},{16,0},{32,16},{48,32},{64,48},{80,64},{96,80},{112,96},{1... | collective-permute-start | bytes 626696 | tf_op jit(solution)/shard_map/ppermute | solution.py:407
  71.7 7.0 %collective-permute-start.25 = (bf16[272,384]{1,0:T(8,128)(2,1)S(1)}, bf16[272,384]{1,0:T(8,128)(2,1)S(1)}, u32[]{:S(2)}, u32[]{:S(2)}) collective-permute-start(bf16[272,384]{1,0:T(8,128)(2,1)S(1)} %get-tuple-element.54.refs_4_), channel_id=1, source_target_pairs={{0,16},{16,32},{32,48},{48,64},{64,80},{80,96},{96,112},{112,0},{1... | collective-permute-start | bytes 626696 | tf_op jit(solution)/shard_map/ppermute | solution.py:407
  75.4 9.0 %collective-permute-start.27 = (bf16[192,256]{1,0:T(8,128)(2,1)S(1)}, bf16[192,256]{1,0:T(8,128)(2,1)S(1)}, u32[]{:S(2)}, u32[]{:S(2)}) collective-permute-start(bf16[192,256]{1,0:T(8,128)(2,1)S(1)} %get-tuple-element.63), channel_id=1, source_target_pairs={{0,129},{1,128},{16,145},{17,144},{32,161},{33,160},{48,177},{49,1... | collective-permute-start | bytes 294920 | tf_op jit(solution)/shard_map/ppermute | solution.py:438
  76.7 7.7 %collective-permute-start.28 = (bf16[192,256]{1,0:T(8,128)(2,1)S(1)}, bf16[192,256]{1,0:T(8,128)(2,1)S(1)}, u32[]{:S(2)}, u32[]{:S(2)}) collective-permute-start(bf16[192,256]{1,0:T(8,128)(2,1)S(1)} %get-tuple-element.64), channel_id=1, source_target_pairs={{0,1},{1,0},{2,3},{3,2},{4,5},{5,4},{6,7},{7,6},{8,9},{9,8},{10,11... | collective-permute-start | bytes 294920 | tf_op jit(solution)/shard_map/ppermute | solution.py:429
  79.0 7.0 %collective-permute-start.31 = (bf16[192,256]{1,0:T(8,128)(2,1)S(1)}, bf16[192,256]{1,0:T(8,128)(2,1)S(1)}, u32[]{:S(2)}, u32[]{:S(2)}) collective-permute-start(bf16[192,256]{1,0:T(8,128)(2,1)S(1)} %get-tuple-element.67), channel_id=1, source_target_pairs={{0,1},{1,0},{2,3},{3,2},{4,5},{5,4},{6,7},{7,6},{8,9},{9,8},{10,11... | collective-permute-start | bytes 294920 | tf_op jit(solution)/shard_map/ppermute | solution.py:429
  80.6 6.4 %collective-permute-start.30 = (bf16[208,256]{1,0:T(8,128)(2,1)S(1)}, bf16[208,256]{1,0:T(8,128)(2,1)S(1)}, u32[]{:S(2)}, u32[]{:S(2)}) collective-permute-start(bf16[208,256]{1,0:T(8,128)(2,1)S(1)} %get-tuple-element.66), channel_id=1, source_target_pairs={{0,129},{1,128},{16,145},{17,144},{32,161},{33,160},{48,177},{49,1... | collective-permute-start | bytes 319496 | tf_op jit(solution)/shard_map/ppermute | solution.py:438
  82.7 5.7 %collective-permute-start.29 = (bf16[192,512]{1,0:T(8,128)(2,1)S(1)}, bf16[192,512]{1,0:T(8,128)(2,1)S(1)}, u32[]{:S(2)}, u32[]{:S(2)}) collective-permute-start(bf16[192,512]{1,0:T(8,128)(2,1)S(1)} %get-tuple-element.65), channel_id=1, source_target_pairs={{0,128},{16,144},{32,160},{48,176},{64,192},{80,208},{96,224},{112... | collective-permute-start | bytes 589832 | tf_op jit(solution)/shard_map/ppermute | solution.py:413
